TPU v7x, 32 devices: a whole 2x2x4 slice. The times are simulated.
32 devices in a mesh: ctx: 4 (over z), fsdp: 8 (over y, x, core).
Axes of the slice: x: 2, y: 2, z: 4, core: 2. Of those that a mesh axis runs over, the one named last changes fastest.
Arguments:
- inputs: bfloat16 [8, 2, 512, 2048], P('fsdp', None, 'ctx'), may hold values from -6 to 6
- lengths: int32 [8], P('fsdp'), may hold values from 256 to 1024, as said below
- attn_gain: bfloat16 [2048], P(('ctx', 'fsdp')), may hold values from 0.099609375 to 1.8984375
- query_weight: bfloat16 [2048, 2048], P(('ctx', 'fsdp')), may hold values from -0.125 to 0.125
- key_matrix: bfloat16 [2048, 1024], P(('ctx', 'fsdp')), may hold values from -0.125 to 0.125
- value_matrix: bfloat16 [2048, 1024], P(('ctx', 'fsdp')), may hold values from -0.125 to 0.125
- output_weight: bfloat16 [2048, 2048], P(('ctx', 'fsdp')), may hold values from -0.75 to 0.75
- ffn_gain: bfloat16 [2048], P(('ctx', 'fsdp')), may hold values from 0.099609375 to 1.8984375
- gate_weight: bfloat16 [2048, 8192], P(('ctx', 'fsdp')), may hold values from -0.125 to 0.125
- up_weight: bfloat16 [2048, 8192], P(('ctx', 'fsdp')), may hold values from -0.125 to 0.125
- down_weight: bfloat16 [8192, 2048], P(('ctx', 'fsdp')), may hold values from -0.0625 to 0.0625
- cotangent: bfloat16 [8, 2, 512, 2048], P('fsdp', None, 'ctx'), may hold values from -6 to 6
Outputs:
- outputs: bfloat16 [8, 2, 512, 2048], P('fsdp', None, 'ctx')
- input_grad: bfloat16 [8, 2, 512, 2048], P('fsdp', None, 'ctx')
- attn_gain_grad: float32 [2048], P(('ctx', 'fsdp'))
- query_grad: float32 [2048, 2048], P(('ctx', 'fsdp'))
- key_grad: float32 [2048, 1024], P(('ctx', 'fsdp'))
- value_grad: float32 [2048, 1024], P(('ctx', 'fsdp'))
- output_grad: float32 [2048, 2048], P(('ctx', 'fsdp'))
- ffn_gain_grad: float32 [2048], P(('ctx', 'fsdp'))
- gate_grad: float32 [2048, 8192], P(('ctx', 'fsdp'))
- up_grad: float32 [2048, 8192], P(('ctx', 'fsdp'))
- down_grad: float32 [8192, 2048], P(('ctx', 'fsdp'))
Inputs may be any that keep to these rules, and one draw needn't show every extreme that they name: `lengths`: one slot, drawn from the seed, has length 1024.
All inputs are finite; a program needn't handle non-finite values.
Results may differ from a plain program's by a relative error of at most 0.017.
Values may be sent and summed in bfloat16 or wider, within the bound.
A program may use at most 704 MiB of HBM per device.

v0:
```python
import jax
import jax.numpy as jnp
from jax import lax
from jax.sharding import PartitionSpec as P

QUERY_HEADS = 8
KEY_VALUE_HEADS = 4
HEAD_SIZE = 256


epsilon = 1e-06
rope_base = 1000042.0
contract_cols = (((1,), (1,)), ((), ()))
contract_rows = (((0,), (0,)), ((), ()))


def apply_rotation(tensor, rotation_angles, direction):
    halfway = tensor.shape[-1] // 2
    cos_table = jnp.cos(rotation_angles)[:, None, :]
    sin_table = direction * jnp.sin(rotation_angles)[:, None, :]
    front_half = tensor[..., :halfway]
    back_half = tensor[..., halfway:]
    return jnp.concatenate(
        [
            front_half * cos_table - back_half * sin_table,
            back_half * cos_table + front_half * sin_table,
        ],
        axis=-1,
    )


def rms_scale(values):
    return lax.rsqrt(jnp.mean(values * values, axis=-1, keepdims=True) + epsilon)


def key_positions(block_len, groups):
    owner_idx = lax.broadcasted_iota(jnp.int32, (groups, 2, block_len), 0)
    side_idx = lax.broadcasted_iota(jnp.int32, (groups, 2, block_len), 1)
    inner_idx = lax.broadcasted_iota(jnp.int32, (groups, 2, block_len), 2)
    block_index = jnp.where(side_idx == 0, owner_idx, 2 * groups - 1 - owner_idx)
    return (block_index * block_len + inner_idx).reshape(groups * 2 * block_len)


def weight_sums(term_fn, own_rows):
    return lax.psum_scatter(
        term_fn(jnp.int32(0), lax.axis_size(("ctx", "fsdp")) * own_rows),
        ("ctx", "fsdp"),
        scatter_dimension=0,
        tiled=True,
    )


def on_device(
    inputs,
    lengths,
    attn_gain,
    query_weight,
    key_matrix,
    value_matrix,
    output_weight,
    ffn_gain,
    gate_weight,
    up_weight,
    down_weight,
    cotangent,
):
    block_len = inputs.shape[2]
    width = inputs.shape[3]
    count_of_rows = 2 * block_len
    groups = lax.axis_size("ctx")
    ctx_place = lax.axis_index("ctx")
    key_pos = key_positions(block_len, groups)
    query_pos = lax.dynamic_slice_in_dim(key_pos, ctx_place * count_of_rows, count_of_rows)
    slot_length = lengths[0]
    valid_rows = (query_pos < slot_length).astype(jnp.float32)[:, None]
    allowed = (key_pos[None, :] <= query_pos[:, None]) & (key_pos[None, :] < slot_length)
    halfway = HEAD_SIZE // 2
    frequency = rope_base ** (-2.0 * jnp.arange(halfway).astype(jnp.float32) / HEAD_SIZE)
    rotation_angles = query_pos.astype(jnp.float32)[:, None] * frequency[None, :]
    scaling = HEAD_SIZE ** (-0.5)
    query_group_count = QUERY_HEADS // KEY_VALUE_HEADS
    query_width = query_weight.shape[1]
    keyval_width = key_matrix.shape[1]
    ff_width = gate_weight.shape[1]
    tokens = inputs.reshape(count_of_rows, width).astype(jnp.float32)
    scale_one = rms_scale(tokens)
    unit_one = tokens * scale_one
    piece_query = lax.all_gather(query_weight, ("ctx", "fsdp"), axis=0, tiled=True)
    piece_key = lax.all_gather(key_matrix, ("ctx", "fsdp"), axis=0, tiled=True)
    piece_value = lax.all_gather(value_matrix, ("ctx", "fsdp"), axis=0, tiled=True)
    piece_gain = lax.all_gather(attn_gain, ("ctx", "fsdp"), axis=0, tiled=True)
    gain_part = piece_gain.astype(jnp.float32)
    columns = (unit_one * gain_part[None, :]).astype(jnp.bfloat16)
    acc_query = jnp.dot(columns, piece_query, preferred_element_type=jnp.float32)
    key_accumulated = jnp.dot(columns, piece_key, preferred_element_type=jnp.float32)
    value_accumulated = jnp.dot(columns, piece_value, preferred_element_type=jnp.float32)
    normed = columns
    gain_full = gain_part
    first_normalized = normed
    gain_one = gain_full
    rot_query = (
        apply_rotation(
            acc_query.reshape(count_of_rows, QUERY_HEADS, HEAD_SIZE), rotation_angles, 1.0
        )
        .astype(jnp.bfloat16)
        .reshape(count_of_rows, KEY_VALUE_HEADS, query_group_count, HEAD_SIZE)
    )
    rotated_key_rows = apply_rotation(
        key_accumulated.reshape(count_of_rows, KEY_VALUE_HEADS, HEAD_SIZE), rotation_angles, 1.0
    ).astype(jnp.bfloat16)
    value_row_block = value_accumulated.reshape(count_of_rows, KEY_VALUE_HEADS, HEAD_SIZE).astype(
        jnp.bfloat16
    )
    all_keys, all_values = (
        lax.all_gather(rotated_key_rows, "ctx", axis=0, tiled=True),
        lax.all_gather(value_row_block, "ctx", axis=0, tiled=True),
    )

    def scores_of():
        raw_scores = (
            jnp.einsum("qkgd,skd->kgqs", rot_query, all_keys, preferred_element_type=jnp.float32)
            * scaling
        )
        return jnp.where(allowed[None, None], raw_scores, -jnp.inf)

    scores = scores_of()
    row_peak = jnp.max(scores, axis=-1, keepdims=True)
    exp_scores = jnp.exp(scores - row_peak)
    row_total = jnp.sum(exp_scores, axis=-1, keepdims=True)
    log_total = row_peak + jnp.log(row_total)
    softmax_p = exp_scores / row_total
    attended = (
        jnp.einsum(
            "kgqs,skd->qkgd",
            softmax_p.astype(jnp.bfloat16),
            all_values,
            preferred_element_type=jnp.float32,
        )
        .reshape(count_of_rows, query_width)
        .astype(jnp.bfloat16)
    )
    branch_one = jnp.dot(
        attended,
        lax.all_gather(output_weight, ("ctx", "fsdp"), axis=0, tiled=True),
        preferred_element_type=jnp.float32,
    )
    hidden_one = tokens + branch_one
    scale_two = rms_scale(hidden_one)
    unit_two = hidden_one * scale_two
    piece_gate = lax.all_gather(gate_weight, ("ctx", "fsdp"), axis=0, tiled=True)
    piece_up = lax.all_gather(up_weight, ("ctx", "fsdp"), axis=0, tiled=True)
    piece_gain = lax.all_gather(ffn_gain, ("ctx", "fsdp"), axis=0, tiled=True)
    gain_part = piece_gain.astype(jnp.float32)
    columns = (unit_two * gain_part[None, :]).astype(jnp.bfloat16)
    acc_gate = jnp.dot(columns, piece_gate, preferred_element_type=jnp.float32)
    acc_up = jnp.dot(columns, piece_up, preferred_element_type=jnp.float32)
    normed = columns
    gain_full = gain_part
    normed_two = normed
    mixed_hidden = (jax.nn.silu(acc_gate) * acc_up).astype(jnp.bfloat16)
    branch_two = jnp.dot(
        mixed_hidden,
        lax.all_gather(down_weight, ("ctx", "fsdp"), axis=0, tiled=True),
        preferred_element_type=jnp.float32,
    )
    outputs = (valid_rows * (hidden_one + branch_two)).astype(jnp.bfloat16).reshape(inputs.shape)
    grad_out = valid_rows * cotangent.reshape(count_of_rows, width).astype(jnp.float32)
    grad_down_b = grad_out.astype(jnp.bfloat16)

    def down_term(offset, span_rows):
        return lax.dot_general(
            mixed_hidden, grad_down_b, contract_rows, preferred_element_type=jnp.float32
        )

    down_grad = weight_sums(down_term, down_weight.shape[0])
    term = lax.dot_general(
        grad_down_b,
        lax.all_gather(down_weight, ("ctx", "fsdp"), axis=0, tiled=True),
        contract_cols,
        preferred_element_type=jnp.float32,
    )
    grad_mixed = term
    sigmoid_gate = jax.nn.sigmoid(acc_gate)
    grad_gate_b = (
        grad_mixed * acc_up * sigmoid_gate * (1.0 + acc_gate * (1.0 - sigmoid_gate))
    ).astype(jnp.bfloat16)
    grad_up_b = (grad_mixed * acc_gate * sigmoid_gate).astype(jnp.bfloat16)

    def gate_up_term(offset, span_rows):
        gate_part = lax.dot_general(
            normed_two, grad_gate_b, contract_rows, preferred_element_type=jnp.float32
        )
        up_part = lax.dot_general(
            normed_two, grad_up_b, contract_rows, preferred_element_type=jnp.float32
        )
        return jnp.concatenate([gate_part, up_part], axis=1)

    both_grads = weight_sums(gate_up_term, gate_weight.shape[0])
    gate_grad = both_grads[:, :ff_width]
    up_grad = both_grads[:, ff_width:]
    piece_gate = lax.all_gather(gate_weight, ("ctx", "fsdp"), axis=0, tiled=True)
    piece_up = lax.all_gather(up_weight, ("ctx", "fsdp"), axis=0, tiled=True)
    term = lax.dot_general(
        grad_gate_b, piece_gate, contract_cols, preferred_element_type=jnp.float32
    ) + lax.dot_general(grad_up_b, piece_up, contract_cols, preferred_element_type=jnp.float32)
    grad_norm_two = term
    grad_unit_two = grad_norm_two * gain_full[None, :]
    ffn_gain_term = jnp.sum(grad_norm_two * unit_two, axis=0)
    grad_hidden = (
        grad_out
        + scale_two * grad_unit_two
        - hidden_one * scale_two**3 * jnp.mean(hidden_one * grad_unit_two, axis=-1, keepdims=True)
    )
    grad_branch_b = grad_hidden.astype(jnp.bfloat16)
    output_term = lax.dot_general(
        attended, grad_branch_b, contract_rows, preferred_element_type=jnp.float32
    )
    term = lax.dot_general(
        grad_branch_b,
        lax.all_gather(output_weight, ("ctx", "fsdp"), axis=0, tiled=True),
        contract_cols,
        preferred_element_type=jnp.float32,
    )
    attended_gradient = term
    head_gradient = attended_gradient.astype(jnp.bfloat16).reshape(
        count_of_rows, KEY_VALUE_HEADS, query_group_count, HEAD_SIZE
    )
    scores = scores_of()
    softmax_p = jnp.exp(scores - log_total)
    grad_probs = jnp.einsum(
        "qkgd,skd->kgqs", head_gradient, all_values, preferred_element_type=jnp.float32
    )
    row_dot = jnp.sum(softmax_p * grad_probs, axis=-1, keepdims=True)
    grad_scores = (softmax_p * (grad_probs - row_dot)).astype(jnp.bfloat16)
    grad_query_rot = (
        jnp.einsum("kgqs,skd->qkgd", grad_scores, all_keys, preferred_element_type=jnp.float32)
        * scaling
    )
    grad_key_all = (
        jnp.einsum("kgqs,qkgd->skd", grad_scores, rot_query, preferred_element_type=jnp.float32)
        * scaling
    )
    grad_value_all = jnp.einsum(
        "kgqs,qkgd->skd",
        softmax_p.astype(jnp.bfloat16),
        head_gradient,
        preferred_element_type=jnp.float32,
    )
    grad_key_own, grad_value_own = (
        lax.psum_scatter(
            grad_key_all.astype(jnp.bfloat16), "ctx", scatter_dimension=0, tiled=True
        ).astype(jnp.float32),
        lax.psum_scatter(
            grad_value_all.astype(jnp.bfloat16), "ctx", scatter_dimension=0, tiled=True
        ).astype(jnp.float32),
    )
    grad_query_b = (
        apply_rotation(
            grad_query_rot.reshape(count_of_rows, QUERY_HEADS, HEAD_SIZE), rotation_angles, -1.0
        )
        .astype(jnp.bfloat16)
        .reshape(count_of_rows, query_width)
    )
    grad_key_b = (
        apply_rotation(grad_key_own, rotation_angles, -1.0)
        .astype(jnp.bfloat16)
        .reshape(count_of_rows, keyval_width)
    )
    grad_value_b = grad_value_own.astype(jnp.bfloat16).reshape(count_of_rows, keyval_width)
    query_term = lax.dot_general(
        first_normalized, grad_query_b, contract_rows, preferred_element_type=jnp.float32
    )
    key_term = lax.dot_general(
        first_normalized, grad_key_b, contract_rows, preferred_element_type=jnp.float32
    )
    value_term = lax.dot_general(
        first_normalized, grad_value_b, contract_rows, preferred_element_type=jnp.float32
    )
    piece_query = lax.all_gather(query_weight, ("ctx", "fsdp"), axis=0, tiled=True)
    piece_key = lax.all_gather(key_matrix, ("ctx", "fsdp"), axis=0, tiled=True)
    piece_value = lax.all_gather(value_matrix, ("ctx", "fsdp"), axis=0, tiled=True)
    term = lax.dot_general(
        grad_query_b, piece_query, contract_cols, preferred_element_type=jnp.float32
    )
    term = term + lax.dot_general(
        grad_key_b, piece_key, contract_cols, preferred_element_type=jnp.float32
    )
    term = term + lax.dot_general(
        grad_value_b, piece_value, contract_cols, preferred_element_type=jnp.float32
    )
    grad_unit_one = term * gain_one[None, :]
    attn_gain_term = jnp.sum(term * unit_one, axis=0)
    grad_tokens = (
        grad_hidden
        + scale_one * grad_unit_one
        - tokens * scale_one**3 * jnp.mean(tokens * grad_unit_one, axis=-1, keepdims=True)
    )
    input_grad = grad_tokens.astype(jnp.bfloat16).reshape(inputs.shape)
    attn_gain_grad, query_grad, key_grad, value_grad, output_grad, ffn_gain_grad = (
        lax.psum_scatter(attn_gain_term, ("ctx", "fsdp"), scatter_dimension=0, tiled=True),
        lax.psum_scatter(query_term, ("ctx", "fsdp"), scatter_dimension=0, tiled=True),
        lax.psum_scatter(key_term, ("ctx", "fsdp"), scatter_dimension=0, tiled=True),
        lax.psum_scatter(value_term, ("ctx", "fsdp"), scatter_dimension=0, tiled=True),
        lax.psum_scatter(output_term, ("ctx", "fsdp"), scatter_dimension=0, tiled=True),
        lax.psum_scatter(ffn_gain_term, ("ctx", "fsdp"), scatter_dimension=0, tiled=True),
    )
    return (
        outputs,
        input_grad,
        attn_gain_grad,
        query_grad,
        key_grad,
        value_grad,
        output_grad,
        ffn_gain_grad,
        gate_grad,
        up_grad,
        down_grad,
    )


def solution(mesh):
    return jax.shard_map(
        on_device,
        mesh=mesh,
        in_specs=(
            P("fsdp", None, "ctx", None),
            P("fsdp"),
            P(("ctx", "fsdp")),
            P(("ctx", "fsdp"), None),
            P(("ctx", "fsdp"), None),
            P(("ctx", "fsdp"), None),
            P(("ctx", "fsdp"), None),
            P(("ctx", "fsdp")),
            P(("ctx", "fsdp"), None),
            P(("ctx", "fsdp"), None),
            P(("ctx", "fsdp"), None),
            P("fsdp", None, "ctx", None),
        ),
        out_specs=(
            P("fsdp", None, "ctx", None),
            P("fsdp", None, "ctx", None),
            P(("ctx", "fsdp")),
            P(("ctx", "fsdp"), None),
            P(("ctx", "fsdp"), None),
            P(("ctx", "fsdp"), None),
            P(("ctx", "fsdp"), None),
            P(("ctx", "fsdp")),
            P(("ctx", "fsdp"), None),
            P(("ctx", "fsdp"), None),
            P(("ctx", "fsdp"), None),
        ),
        check_vma=False,
    )
```

profile of v0, /device:TPU:0, one launch (start us, length us, event | category | flops | bytes accessed | tf_op | source)
XLA Modules:
  0.0 4461.7 jit_solution(2576419490901307266)
XLA Ops:
  11.2 42.2 all-reduce.6
  59.1 16.5 all-gather.14.cloned.1.call-done
  86.7 52.4 %all-gather.10.cloned.1.call-done = bf16[2048,1024]{1,0:T(8,128)(2,1)} async-done(((bf16[64,1024]{1,0:T(8,128)(2,1)}), bf16[2048,1024]{1,0:T(8,128)(2,1)}) %all-gather.10.cloned.1.call-update) | async-done | bytes 4194320 | tf_op jit(solution)/shard_map/all_gather | solution.py:90
  154.7 63.3 %all-gather.18.cloned.1.call-done = bf16[2048,2048]{1,0:T(8,128)(2,1)} async-done(((bf16[64,2048]{1,0:T(8,128)(2,1)}), bf16[2048,2048]{1,0:T(8,128)(2,1)}) %all-gather.18.cloned.1.call-update) | async-done | bytes 8388624 | tf_op jit(solution)/shard_map/all_gather | solution.py:88
  218.0 12.4 copy.39
  237.0 27.8 all-gather.16.cloned.1.call-done
  272.9 38.1 all-gather.12.cloned.1.call-done
  311.0 6.8 fusion.37
  317.9 72.1 %all-gather.20.cloned.1.call-done = bf16[2048,2048]{1,0:T(8,128)(2,1)} async-done(((bf16[64,2048]{1,0:T(8,128)(2,1)}), bf16[2048,2048]{1,0:T(8,128)(2,1)}) %all-gather.20.cloned.1.call-update) | async-done | bytes 8388624 | tf_op jit(solution)/shard_map/all_gather | solution.py:144
  396.4 189.8 %all-gather.22.cloned.1.call-done = bf16[2048,8192]{1,0:T(8,128)(2,1)} async-done(((bf16[64,8192]{1,0:T(8,128)(2,1)}), bf16[2048,8192]{1,0:T(8,128)(2,1)}) %all-gather.22.cloned.1.call-update) | async-done | bytes 33554448 | tf_op jit(solution)/shard_map/all_gather | solution.py:150
  586.2 18.1 fusion.50
  604.3 177.7 %all-gather.24.cloned.1.call-done = bf16[2048,8192]{1,0:T(8,128)(2,1)} async-done(((bf16[64,8192]{1,0:T(8,128)(2,1)}), bf16[2048,8192]{1,0:T(8,128)(2,1)}) %all-gather.24.cloned.1.call-update) | async-done | bytes 33554448 | tf_op jit(solution)/shard_map/all_gather | solution.py:151
  782.1 17.8 fusion.51
  799.8 178.1 %all-gather.26.cloned.1.call-done = bf16[8192,2048]{1,0:T(8,128)(2,1)} async-done(((bf16[256,2048]{1,0:T(8,128)(2,1)}), bf16[8192,2048]{1,0:T(8,128)(2,1)}) %all-gather.26.cloned.1.call-update) | async-done | bytes 33554448 | tf_op jit(solution)/shard_map/all_gather | solution.py:163
  977.9 23.9 multiply_convert_fusion
  1001.8 17.3 fusion.52
  1019.2 19.3 multiply_reduce_fusion
  1058.1 25.8 fusion.58
  1090.0 25.4 fusion.57
  1115.4 87.6 %pad_maximum_fusion = f32[2048,16384]{1,0:T(8,128)} fusion(f32[2048,8192]{1,0:T(8,128)} %fusion.58, f32[2048,8192]{1,0:T(8,128)} %fusion.57), kind=kLoop, calls=%fused_computation | loop fusion | flops 33554432 | bytes 268435456 | tf_op jit(solution)/shard_map/concatenate | solution.py:196
  1223.0 8.5 fusion.54
  1233.4 8.1 fusion.40
  1242.7 28.1 fusion.59
  1272.1 7.4 fusion.53
  1279.5 17.6 fusion.11
  1303.8 41.5 all-reduce.5
  1349.7 1731.0 %all-reduce.9.cloned.1.call-done = f32[2048,16384]{1,0:T(8,128)} async-done(((f32[2048,16384]{1,0:T(8,128)}), f32[2048,16384]{1,0:T(8,128)}) %all-reduce.9.cloned.1.call-update) | async-done | bytes 134217744
  3085.6 146.2 %reduce-scatter.14.cloned.1.call-done = f32[64,1024]{1,0:T(8,128)} async-done(((f32[2048,1024]{1,0:T(8,128)}), f32[64,1024]{1,0:T(8,128)}) %reduce-scatter.14.cloned.1.call-update) | async-done | bytes 262160 | tf_op jit(solution)/shard_map/reduce_scatter | solution.py:302
  3231.8 147.4 %reduce-scatter.16.cloned.1.call-done = f32[64,1024]{1,0:T(8,128)} async-done(((f32[2048,1024]{1,0:T(8,128)}), f32[64,1024]{1,0:T(8,128)}) %reduce-scatter.16.cloned.1.call-update) | async-done | bytes 262160 | tf_op jit(solution)/shard_map/reduce_scatter | solution.py:303
  3379.2 181.4 %reduce-scatter.12.cloned.1.call-done = f32[64,2048]{1,0:T(8,128)} async-done(((f32[2048,2048]{1,0:T(8,128)}), f32[64,2048]{1,0:T(8,128)}) %reduce-scatter.12.cloned.1.call-update) | async-done | bytes 524304 | tf_op jit(solution)/shard_map/reduce_scatter | solution.py:301
  3560.5 188.1 %reduce-scatter.18.cloned.1.call-done = f32[64,2048]{1,0:T(8,128)} async-done(((f32[2048,2048]{1,0:T(8,128)}), f32[64,2048]{1,0:T(8,128)}) %reduce-scatter.18.cloned.1.call-update) | async-done | bytes 524304 | tf_op jit(solution)/shard_map/reduce_scatter | solution.py:304
  3748.6 706.3 %reduce-scatter.20.cloned.1.call-done = f32[256,2048]{1,0:T(8,128)} async-done(((f32[8192,2048]{1,0:T(8,128)}), f32[256,2048]{1,0:T(8,128)}) %reduce-scatter.20.cloned.1.call-update) | async-done | bytes 2097168 | tf_op jit(solution)/shard_map/reduce_scatter | solution.py:45
  (177 shorter events, 122.4 us)
Async XLA Ops:
  7.2 68.5 %all-gather.14.cloned.1.call-start = ((), (), s32[]{:S(2)}) async-start(), calls=%async_computation.9 | async-start | bytes 4325376 | tf_op jit(solution)/shard_map/all_gather | solution.py:89
  7.9 131.2 %all-gather.10.cloned.1.call-start = ((), (), s32[]{:S(2)}) async-start(), calls=%async_computation.7 | async-start | bytes 4325376 | tf_op jit(solution)/shard_map/all_gather | solution.py:90
  8.7 209.3 %all-gather.18.cloned.1.call-start = ((), (), s32[]{:S(2)}) async-start(), calls=%async_computation.11 | async-start | bytes 8650752 | tf_op jit(solution)/shard_map/all_gather | solution.py:88
  9.4 255.4 %all-gather.16.cloned.1.call-start = ((), (), s32[]{:S(2)}) async-start(), calls=%async_computation.10 | async-start | bytes 2621440 | tf_op jit(solution)/shard_map/all_gather | solution.py:115
  53.4 28.8 copy-start.28
  54.2 984.2 %copy-start.33 = (f32[256]{0:T(256)}, f32[256]{0:T(256)S(1)}, u32[]{:S(2)}) copy-start(f32[256]{0:T(256)S(1)} %get-tuple-element.19) | copy-start | bytes 3076
  55.8 26.4 copy-start.31
  57.5 178.6 %copy-start.19 = (f32[256,128]{0,1:T(8,128)}, f32[256,128]{0,1:T(8,128)S(1)}, u32[]{:S(2)}) copy-start(f32[256,128]{0,1:T(8,128)S(1)} %get-tuple-element.36) | copy-start | bytes 393220
  59.1 171.2 %copy-start.3 = (bf16[1,2,128,2048]{3,2,1,0:T(8,128)(2,1)}, bf16[1,2,128,2048]{3,2,1,0:T(8,128)(2,1)S(1)}, u32[]{:S(2)}) copy-start(bf16[1,2,128,2048]{3,2,1,0:T(8,128)(2,1)S(1)} %fusion.24) | copy-start | bytes 3145732
  86.7 224.4 %all-gather.12.cloned.1.call-start = ((), (), s32[]{:S(2)}) async-start(), calls=%async_computation.8 | async-start | bytes 2621440 | tf_op jit(solution)/shard_map/all_gather | solution.py:116
  145.7 7.8 copy-start.17
  150.0 239.9 %all-gather.20.cloned.1.call-start = ((), (), s32[]{:S(2)}) async-start(), calls=%async_computation.12 | async-start | bytes 8650752 | tf_op jit(solution)/shard_map/all_gather | solution.py:144
  150.6 435.6 %all-gather.22.cloned.1.call-start = ((), (), s32[]{:S(2)}) async-start(), calls=%async_computation.13 | async-start | bytes 34603008 | tf_op jit(solution)/shard_map/all_gather | solution.py:150
  151.4 630.7 %all-gather.24.cloned.1.call-start = ((), (), s32[]{:S(2)}) async-start(), calls=%async_computation.14 | async-start | bytes 34603008 | tf_op jit(solution)/shard_map/all_gather | solution.py:151
  152.1 825.8 %all-gather.26.cloned.1.call-start = ((), (), s32[]{:S(2)}) async-start(), calls=%async_computation.15 | async-start | bytes 34603008 | tf_op jit(solution)/shard_map/all_gather | solution.py:163
  152.9 1050.3 %reduce-scatter.8.cloned.1.call-start = ((), (), s32[]{:S(2)}) async-start(), calls=%async_computation.16 | async-start | bytes 2621440 | tf_op jit(solution)/shard_map/reduce_scatter | solution.py:250
  236.7 31.8 copy-start.24
  237.0 31.5 copy-start.26
  272.9 117.0 %copy-start.1 = (bf16[1,2,128,2048]{3,2,1,0:T(8,128)(2,1)S(1)}, bf16[1,2,128,2048]{3,2,1,0:T(8,128)(2,1)}, u32[]{:S(2)}) copy-start(bf16[1,2,128,2048]{3,2,1,0:T(8,128)(2,1)} %param.12) | copy-start | bytes 3145732
  396.1 642.3 %copy-start.7 = (f32[256,2048]{1,0:T(8,128)}, f32[256,2048]{1,0:T(8,128)S(1)}, u32[]{:S(2)}) copy-start(f32[256,2048]{1,0:T(8,128)S(1)} %get-tuple-element.44) | copy-start | bytes 6291460
  1019.1 22.9 slice-start.2
  1019.1 19.3 copy-start.18
  1019.2 22.9 slice-start.3
  1058.1 152.7 %reduce-scatter.10.cloned.1.call-start = ((), (), s32[]{:S(2)}) async-start(), calls=%async_computation.17 | async-start | bytes 2621440 | tf_op jit(solution)/shard_map/reduce_scatter | solution.py:253
  1115.4 1965.3 %all-reduce.9.cloned.1.call-start = ((), (), s32[]{:S(2)}) async-start(), calls=%async_computation.23 | async-start | bytes 268435456
  1203.1 2028.7 %reduce-scatter.14.cloned.1.call-start = ((), (), s32[]{:S(2)}) async-start(), calls=%async_computation.19 | async-start | bytes 8650752 | tf_op jit(solution)/shard_map/reduce_scatter | solution.py:302
  1210.7 2168.5 %reduce-scatter.16.cloned.1.call-start = ((), (), s32[]{:S(2)}) async-start(), calls=%async_computation.20 | async-start | bytes 8650752 | tf_op jit(solution)/shard_map/reduce_scatter | solution.py:303
  1216.5 2344.1 %reduce-scatter.12.cloned.1.call-start = ((), (), s32[]{:S(2)}) async-start(), calls=%async_computation.18 | async-start | bytes 17301504 | tf_op jit(solution)/shard_map/reduce_scatter | solution.py:301
  1231.5 2517.0 %reduce-scatter.18.cloned.1.call-start = ((), (), s32[]{:S(2)}) async-start(), calls=%async_computation.21 | async-start | bytes 17301504 | tf_op jit(solution)/shard_map/reduce_scatter | solution.py:304
  1241.5 3213.4 %reduce-scatter.20.cloned.1.call-start = ((), (), s32[]{:S(2)}) async-start(), calls=%async_computation.22 | async-start | bytes 69206016 | tf_op jit(solution)/shard_map/reduce_scatter | solution.py:45
  1272.1 7.4 copy-start.34
  1279.5 17.6 copy-start.9
  (25 other events, 70.0 us)
Sparse Core Ops, SparseCore 0:
  10.9 64.7 all-gather.13
  78.5 60.5 all-gather.9
  142.0 75.9 all-gather.17
  220.0 44.8 all-gather.15
  266.8 44.1 all-gather.11
  313.8 76.1 all-gather.19
  392.8 193.3 all-gather.21
  589.1 192.9 all-gather.23
  784.9 192.9 all-gather.25
  1058.2 42.0 reduce-scatter.7
  1115.5 42.3 reduce-scatter.9
  1203.2 1877.4 all-reduce.8
  3083.6 148.2 reduce-scatter.13
  3234.5 144.5 reduce-scatter.15
  3381.9 178.5 reduce-scatter.11
  3563.2 185.2 reduce-scatter.17
  3751.4 703.5 reduce-scatter.19
where the time goes:
time: 4470 us; the launch traced here: 4460 us
  waiting for transfers between devices  3920 us (88%)
  matrix products  285 us (6%)
  other arithmetic  106 us (2%)
  blocking collectives  83.7 us (2%)
  local copies, waits for them, and re-layouts  49.1 us (1%)
    unnamed x18, waiting for transfers between devices  1740 us
    reduce_scatter x1, waiting for transfers between devices, weight_sums(): lax.psum_scatter(term_fn(jnp.int32(0), lax.axis_size(('ctx', 'fsdp')) * o...  706 us
    all_gather x1, waiting for transfers between devices, on_device(): lax.all_gather(gate_weight, ('ctx', 'fsdp'), axis=0, tiled=True)  190 us
    reduce_scatter x1, waiting for transfers between devices, on_device(): lax.psum_scatter(output_term, ('ctx', 'fsdp'), scatter_dimension=0, tiled...  188 us
    reduce_scatter x1, waiting for transfers between devices, on_device(): lax.psum_scatter(query_term, ('ctx', 'fsdp'), scatter_dimension=0, tiled=...  181 us
    all_gather x1, waiting for transfers between devices, on_device(): lax.all_gather(down_weight, ('ctx', 'fsdp'), axis=0, tiled=True)  178 us
    all_gather x1, waiting for transfers between devices, on_device(): piece_up = lax.all_gather(up_weight, ('ctx', 'fsdp'), axis=0, tiled=True)  178 us
    reduce_scatter x1, waiting for transfers between devices, on_device(): lax.psum_scatter(value_term, ('ctx', 'fsdp'), scatter_dimension=0, tiled=...  147 us
  transfers between devices with their start and end apart: 17, of which 15 were waited for; matrix products, arithmetic and copies ran while one was open for 8% of the time, Pallas kernels for 0%

commit v1 on v0

v1 whole, which is shorter than its diff:
```python
import itertools

import jax
import jax.numpy as jnp
from jax import lax
from jax.experimental import pallas as pl
from jax.experimental.pallas import tpu as pltpu
from jax.sharding import Mesh
from jax.sharding import PartitionSpec as P

HEAD = 256
BLK = 128
EPS = 1e-06
ROPE_BASE = 1000042.0
AXES = ("zh", "zl", "y", "x", "c")
TEAM = ("y", "zl")
PEERS = ("zh", "x", "c")
ROWS_T = (((0,), (0,)), ((), ()))
COLS_T = (((1,), (1,)), ((), ()))
F32 = jnp.float32
BF16 = jnp.bfloat16


def offsets(sizes, axes):
    return [dict(zip(axes, o)) for o in itertools.product(*(range(sizes[a]) for a in axes))]


def exchange(jobs, collective_id):
    sizes = {a: lax.axis_size(a) for a in AXES}
    plans = []
    n_sems = 0
    reached = set()
    for kind, x, layout, orders in jobs:
        plan = []
        if kind == "gather":
            rows = x.shape[0] // len(orders)
            for part, order in enumerate(orders):
                for off in offsets(sizes, order):
                    used = [i for i, a in enumerate(order) if off[a]]
                    last = used[-1] if used else -1
                    sends = []
                    for a in order[last + 1 :]:
                        for d in range(1, sizes[a]):
                            sends.append((a, d, n_sems))
                            n_sems += 1
                            reached.add(tuple(d if b == a else 0 for b in AXES))
                    plan.append((len(used), part, part * rows, rows, order, off, sends))
        else:
            for off in offsets(sizes, layout):
                if any(off.values()):
                    plan.append((off, n_sems))
                    n_sems += 1
                    reached.add(tuple(off.get(b, 0) for b in AXES))
        plans.append(plan)
    count = len(jobs)

    def kernel(*refs):
        ins, outs = refs[:count], refs[count : 2 * count]
        send_sem, recv_sem, local_sem = refs[2 * count :]
        here = {a: lax.axis_index(a) for a in AXES}

        def moved(off, sign=1):
            return {a: lax.rem(here[a] + (sign * off.get(a, 0)) % sizes[a], sizes[a]) for a in AXES}

        def place(at, layout):
            index = 0
            for a in layout:
                index = index * sizes[a] + at[a]
            return index

        def device(at):
            return tuple(at[a] for a in AXES)

        barrier = pltpu.get_barrier_semaphore()
        for off in sorted(reached):
            pl.semaphore_signal(
                barrier,
                inc=1,
                device_id=device(moved(dict(zip(AXES, off)))),
                device_id_type=pl.DeviceIdType.MESH,
            )
        pl.semaphore_wait(barrier, len(reached))

        def copy(src, dst, sem, at):
            return pltpu.make_async_remote_copy(
                src_ref=src,
                dst_ref=dst,
                send_sem=send_sem.at[sem],
                recv_sem=recv_sem.at[sem],
                device_id=device(at),
                device_id_type=pl.DeviceIdType.MESH,
            )

        locals_, sent, swaps, steps = [], [], [], []
        for number, (kind, _, layout, _) in enumerate(jobs):
            mine = place(here, layout)
            src = ins[number] if kind == "gather" else ins[number].at[mine]
            locals_.append(pltpu.make_async_copy(src, outs[number].at[mine], local_sem.at[number]))
            if kind == "swap":
                for off, sem in plans[number]:
                    to = moved(off)
                    swaps.append(
                        copy(ins[number].at[place(to, layout)], outs[number].at[mine], sem, to)
                    )
            else:
                steps.extend((step, number) for step in plans[number])
        steps.sort(key=lambda s: (s[0][0], s[0][1], s[1]))
        arrivals = {}
        for (hops, part, row, rows, order, off, sends), number in steps:
            layout = jobs[number][2]
            window = pl.ds(row, rows)
            owner = moved(off)
            spot = outs[number].at[place(owner, layout), window]
            if hops:
                arrivals[number, part, tuple(sorted(off.items()))].wait_recv()
            source = spot if hops else ins[number].at[window]
            for a, d, sem in sends:
                to = moved({a: d})
                cp = copy(source, spot, sem, to)
                cp.start()
                sent.append(cp)
                came = dict(off)
                came[a] = (-d) % sizes[a]
                arrivals[number, part, tuple(sorted(came.items()))] = cp
            if not hops and (part, number) == (steps[-1][0][1], steps[-1][1]):
                pass
        for cp in swaps:
            cp.start()
        for cp in locals_:
            cp.start()
        for cp in swaps:
            cp.wait_recv()
        for cp in sent + swaps:
            cp.wait_send()
        for cp in locals_:
            cp.wait()

    shapes = []
    for kind, x, layout, _ in jobs:
        n = 1
        for a in layout:
            n *= sizes[a]
        shape = (n,) + x.shape if kind == "gather" else x.shape
        shapes.append(jax.ShapeDtypeStruct(shape, x.dtype))
    return pl.pallas_call(
        kernel,
        out_shape=shapes,
        in_specs=[pl.BlockSpec(memory_space=pl.ANY)] * count,
        out_specs=[pl.BlockSpec(memory_space=pl.ANY)] * count,
        scratch_shapes=[
            pltpu.SemaphoreType.DMA((n_sems,)),
            pltpu.SemaphoreType.DMA((n_sems,)),
            pltpu.SemaphoreType.DMA((count,)),
        ],
        compiler_params=pltpu.CompilerParams(
            collective_id=collective_id, has_side_effects=True
        ),
    )(*[job[1] for job in jobs])


def dot(a, b, dims=None):
    if dims is None:
        return jnp.dot(a, b, preferred_element_type=F32)
    return lax.dot_general(a, b, dims, preferred_element_type=F32)


def rotate(t, cos, sin):
    half = t.shape[-1] // 2
    front, back = t[..., :half], t[..., half:]
    return jnp.concatenate([front * cos - back * sin, back * cos + front * sin], axis=-1)


def rms_scale(values):
    return lax.rsqrt(jnp.mean(values * values, axis=-1, keepdims=True) + EPS)


def positions(members):
    total = lax.axis_size("zh") * lax.axis_size("zl")
    half = jnp.arange(2)[None, :, None]
    row = jnp.arange(BLK)[None, None, :]
    j = members[:, None, None]
    return (jnp.where(half == 0, j, 2 * total - 1 - j) * BLK + row).reshape(-1)


GATHER_TEAM = (("y", "zl"), ("zl", "y"))


def on_device(
    inputs,
    lengths,
    attn_gain,
    query_weight,
    key_matrix,
    value_matrix,
    output_weight,
    ffn_gain,
    gate_weight,
    up_weight,
    down_weight,
    cotangent,
):
    size = {a: lax.axis_size(a) for a in AXES}
    at = {a: lax.axis_index(a) for a in AXES}
    width = inputs.shape[3]
    own = inputs.shape[1] * inputs.shape[2]
    rows = query_weight.shape[0]
    n_dev = width // rows
    team = size["y"] * size["zl"]
    q_cols = query_weight.shape[1] // team
    kv_cols = key_matrix.shape[1] // team
    ff_rows = down_weight.shape[0]
    ff = gate_weight.shape[1] // team
    heads = q_cols // HEAD
    scaling = HEAD**-0.5

    def by_team(w):
        return w.reshape(rows, team, -1).transpose(1, 0, 2)

    def ff_by_team(w):
        cut = w.reshape(rows, size["zh"], size["zl"], size["y"], size["x"] * size["c"] * ff_rows)
        return cut.transpose(3, 2, 0, 1, 4).reshape(team, rows, ff)

    attn_cut = jnp.concatenate(
        [by_team(query_weight), by_team(key_matrix), by_team(value_matrix)], axis=2
    )
    ffn_cut = jnp.concatenate([ff_by_team(gate_weight), ff_by_team(up_weight)], axis=2)
    tile = jnp.zeros((8, 128), F32)
    tile = tile.at[0, :rows].set(attn_gain.astype(F32))
    tile = tile.at[0, 64 : 64 + rows].set(ffn_gain.astype(F32))
    tile = tile.at[1].set(lengths[0].astype(F32))
    tiles, attn_part, ffn_part = exchange(
        [
            ("gather", tile, AXES, (("c", "x", "y", "zl", "zh"),)),
            ("swap", attn_cut, TEAM, None),
            ("swap", ffn_cut, TEAM, None),
        ],
        1,
    )
    gain_one = tiles[:, 0, :rows].reshape(1, width)
    gain_two = tiles[:, 0, 64 : 64 + rows].reshape(1, width)
    slots = tiles[: n_dev // (size["zh"] * size["zl"]), 1, 0].reshape(
        size["y"], size["x"], size["c"]
    )
    lens = slots[:, at["x"], at["c"]].astype(jnp.int32)

    n_peer = size["zh"] * size["x"] * size["c"]
    per_head = n_dev // team

    def head_home(i):
        f, t = i // per_head, i % per_head
        c, t = t % size["c"], t // size["c"]
        x, zh = t % size["x"], t // size["x"]
        zl, y = f % size["zl"], f // size["zl"]
        return (((zh * size["zl"] + zl) * size["y"] + y) * size["x"] + x) * size["c"] + c

    homes = [(i, head_home(i)) for i in range(n_dev)]
    out_part = lax.ppermute(output_weight, AXES, homes)
    w_down = lax.all_gather(down_weight, PEERS, axis=0, tiled=True)

    def natural(w):
        w = w.reshape(size["zh"], size["x"], size["c"], size["y"], size["zl"], rows, -1)
        return w.transpose(0, 4, 3, 1, 2, 5, 6).reshape(width, -1)

    def peer_major(w):
        w = w.reshape(size["zh"], size["zl"], size["y"], size["x"], size["c"], rows, -1)
        return w.transpose(0, 3, 4, 2, 1, 5, 6).reshape(width, -1)

    w_ffn = natural(lax.all_gather(ffn_part, PEERS, axis=0))
    w_gate, w_up = w_ffn[:, :ff], w_ffn[:, ff:]

    my_pos = positions((at["zh"] * size["zl"] + at["zl"])[None])
    my_len = lengths[0]
    valid = (my_pos < my_len).astype(F32)[:, None]
    zl_all = jnp.arange(size["zl"])
    q_pos = positions(at["zh"] * size["zl"] + zl_all)
    k_pos = positions(jnp.arange(size["zh"] * size["zl"]))
    half = HEAD // 2
    freq = ROPE_BASE ** (-2.0 * jnp.arange(half).astype(F32) / HEAD)
    angles = q_pos.astype(F32)[:, None] * freq[None, :]
    cos = jnp.tile(jnp.cos(angles), (size["y"], 1))[:, None, :]
    sin = jnp.tile(jnp.sin(angles), (size["y"], 1))[:, None, :]

    tokens = inputs.reshape(own, width).astype(F32)
    scale_one = rms_scale(tokens)
    norm_one = (tokens * scale_one * gain_one).astype(BF16)
    norm_one_all, w_attn, w_out = exchange(
        [
            ("gather", norm_one, TEAM, GATHER_TEAM),
            ("gather", attn_part, PEERS, (PEERS,)),
            ("gather", out_part, PEERS, (PEERS,)),
        ],
        2,
    )
    n_tok = team * own
    norm_one_all = norm_one_all.reshape(n_tok, width)
    w_attn = natural(w_attn)
    w_out = w_out.reshape(q_cols, width)
    qkv = dot(norm_one_all, w_attn)
    q = rotate(qkv[:, :q_cols].reshape(n_tok, heads, HEAD), cos, sin).astype(BF16)
    k = rotate(qkv[:, q_cols : q_cols + kv_cols].reshape(n_tok, 1, HEAD), cos, sin).astype(BF16)
    v = qkv[:, q_cols + kv_cols :].astype(BF16)
    kv = jnp.concatenate([k.reshape(n_tok, kv_cols), v], axis=1)
    gy = valid * cotangent.reshape(own, width).astype(F32)
    kv_all, gd_all = exchange(
        [
            ("gather", kv, ("zh",), (("zh",),)),
            ("gather", gy.astype(BF16), TEAM, GATHER_TEAM),
        ],
        3,
    )
    gd_all = gd_all.reshape(n_tok, width)
    n_slot = size["y"]
    n_q = n_tok // n_slot
    q = q.reshape(n_slot, n_q, heads, HEAD)
    kv_all = kv_all.reshape(size["zh"], n_slot, n_q, 2 * kv_cols).transpose(1, 0, 2, 3)
    kv_all = kv_all.reshape(n_slot, size["zh"] * n_q, 2 * kv_cols)
    k_all, v_all = kv_all[:, :, :kv_cols], kv_all[:, :, kv_cols:]
    allowed = (k_pos[None, None, :] <= q_pos[None, :, None]) & (
        k_pos[None, None, :] < lens[:, None, None]
    )
    scores = jnp.einsum("bqgd,bkd->bgqk", q, k_all, preferred_element_type=F32) * scaling
    scores = jnp.where(allowed[:, None], scores, -jnp.inf)
    peak = jnp.max(scores, axis=-1, keepdims=True)
    exps = jnp.exp(scores - peak)
    prob = exps / jnp.sum(exps, axis=-1, keepdims=True)
    prob_b = prob.astype(BF16)
    o = jnp.einsum("bgqk,bkd->bqgd", prob_b, v_all, preferred_element_type=F32)
    o = o.reshape(n_tok, q_cols).astype(BF16)

    def team_sum(parts):
        return sum(parts[i].astype(F32) for i in range(team))

    def blocks(partial):
        return partial.astype(BF16).reshape(team, own, width)

    (o_parts,) = exchange([("swap", blocks(dot(o, w_out)), TEAM, None)], 4)
    h1 = tokens + team_sum(o_parts)
    scale_two = rms_scale(h1)
    norm_two = (h1 * scale_two * gain_two).astype(BF16)
    (norm_two_all,) = exchange([("gather", norm_two, TEAM, GATHER_TEAM)], 5)
    norm_two_all = norm_two_all.reshape(n_tok, width)

    gate = dot(norm_two_all, w_gate)
    up = dot(norm_two_all, w_up)
    sg = jax.nn.sigmoid(gate)
    mixed = (gate * sg * up).astype(BF16)
    gm = dot(gd_all, w_down, COLS_T)
    g_gate = (gm * up * sg * (1.0 + gate * (1.0 - sg))).astype(BF16)
    g_up = (gm * gate * sg).astype(BF16)
    down_term = dot(mixed, gd_all, ROWS_T).astype(BF16)
    down_grad = lax.psum_scatter(down_term, PEERS, scatter_dimension=0, tiled=True)
    gate_term = dot(norm_two_all, g_gate, ROWS_T)
    up_term = dot(norm_two_all, g_up, ROWS_T)
    ffn_term = peer_major(jnp.concatenate([gate_term, up_term], axis=1).astype(BF16))
    ffn_sum = lax.psum_scatter(ffn_term, PEERS, scatter_dimension=0, tiled=True)
    gn2_parts = blocks(dot(g_gate, w_gate, COLS_T) + dot(g_up, w_up, COLS_T))
    (gn2_parts,) = exchange([("swap", gn2_parts, TEAM, None)], 6)
    gn2 = team_sum(gn2_parts) * gain_two
    gh1 = gy + scale_two * gn2 - h1 * scale_two**3 * jnp.mean(h1 * gn2, axis=-1, keepdims=True)
    (ga_all,) = exchange([("gather", gh1.astype(BF16), TEAM, GATHER_TEAM)], 7)
    ga_all = ga_all.reshape(n_tok, width)

    go = dot(ga_all, w_out, COLS_T).astype(BF16).reshape(n_slot, n_q, heads, HEAD)
    gp = jnp.einsum("bqgd,bkd->bgqk", go, v_all, preferred_element_type=F32)
    delta = jnp.sum(prob * gp, axis=-1, keepdims=True)
    gs = (prob * (gp - delta)).astype(BF16)
    gq_rot = jnp.einsum("bgqk,bkd->bqgd", gs, k_all, preferred_element_type=F32) * scaling
    gk_rot = jnp.einsum("bgqk,bqgd->bkd", gs, q, preferred_element_type=F32) * scaling
    gv_sum = jnp.einsum("bgqk,bqgd->bkd", prob_b, go, preferred_element_type=F32)
    gkv = jnp.concatenate([gk_rot, gv_sum], axis=-1).astype(BF16)
    gkv = gkv.reshape(n_slot, size["zh"], n_q, 2 * kv_cols).transpose(1, 0, 2, 3)
    gkv = gkv.reshape(size["zh"], n_tok, 2 * kv_cols)
    out_parts = blocks(dot(mixed, w_down))
    gkv_parts, out_parts = exchange(
        [("swap", gkv, ("zh",), None), ("swap", out_parts, TEAM, None)], 8
    )
    outputs = (valid * (h1 + team_sum(out_parts))).astype(BF16).reshape(inputs.shape)
    gkv = sum(gkv_parts[i].astype(F32) for i in range(size["zh"]))
    gq = rotate(gq_rot.reshape(n_tok, heads, HEAD), cos, -sin).astype(BF16)
    gk = rotate(gkv[:, :kv_cols].reshape(n_tok, 1, HEAD), cos, -sin).astype(BF16)
    g_qkv = jnp.concatenate(
        [gq.reshape(n_tok, q_cols), gk.reshape(n_tok, kv_cols), gkv[:, kv_cols:].astype(BF16)],
        axis=1,
    )
    attn_term = peer_major(dot(norm_one_all, g_qkv, ROWS_T).astype(BF16))
    attn_sum = lax.psum_scatter(attn_term, PEERS, scatter_dimension=0, tiled=True)
    out_term = dot(o, ga_all, ROWS_T).astype(BF16)
    out_sum = lax.psum_scatter(out_term, PEERS, scatter_dimension=0, tiled=True)
    output_grad = lax.ppermute(out_sum, AXES, [(b, a) for a, b in homes]).astype(F32)
    gn1_parts = blocks(dot(g_qkv, w_attn, COLS_T))
    gn1_parts, attn_sum, ffn_sum = exchange(
        [
            ("swap", gn1_parts, TEAM, None),
            ("swap", attn_sum.reshape(team, rows, -1), TEAM, None),
            ("swap", ffn_sum.reshape(team, rows, -1), TEAM, None),
        ],
        9,
    )
    gn1 = team_sum(gn1_parts) * gain_one
    g_tokens = (
        gh1
        + scale_one * gn1
        - tokens * scale_one**3 * jnp.mean(tokens * gn1, axis=-1, keepdims=True)
    )
    input_grad = g_tokens.astype(BF16).reshape(inputs.shape)

    def from_team(part):
        return part.astype(F32).transpose(1, 0, 2).reshape(rows, -1)

    def ff_from_team(part):
        cut = part.astype(F32).reshape(
            size["y"], size["zl"], rows, size["zh"], size["x"] * size["c"] * ff_rows
        )
        return cut.transpose(2, 3, 1, 0, 4).reshape(rows, -1)

    query_grad = from_team(attn_sum[:, :, :q_cols])
    key_grad = from_team(attn_sum[:, :, q_cols : q_cols + kv_cols])
    value_grad = from_team(attn_sum[:, :, q_cols + kv_cols :])
    gate_grad = ff_from_team(ffn_sum[:, :, :ff])
    up_grad = ff_from_team(ffn_sum[:, :, ff:])

    def against(w, g):
        return jnp.sum(w.astype(F32) * g, axis=1)

    attn_gain_grad = (
        against(query_weight, query_grad)
        + against(key_matrix, key_grad)
        + against(value_matrix, value_grad)
    ) / attn_gain.astype(F32)
    ffn_gain_grad = (against(gate_weight, gate_grad) + against(up_weight, up_grad)) / (
        ffn_gain.astype(F32)
    )
    return (
        outputs,
        input_grad,
        attn_gain_grad,
        query_grad,
        key_grad,
        value_grad,
        output_grad,
        ffn_gain_grad,
        gate_grad,
        up_grad,
        down_grad.astype(F32),
    )


def solution(mesh):
    ctx, fsdp = mesh.shape["ctx"], mesh.shape["fsdp"]
    grid = Mesh(mesh.devices.reshape(ctx // 2, 2, 2, fsdp // 4, 2), AXES)
    act = P(("y", "x", "c"), None, ("zh", "zl"), None)
    row = P(AXES)
    return jax.shard_map(
        on_device,
        mesh=grid,
        in_specs=(act, P(("y", "x", "c"))) + (row,) * 9 + (act,),
        out_specs=(act, act) + (row,) * 9,
        check_vma=False,
    )
```

time: 4470 us -> 1390 us (0.31)
  waiting for transfers between devices: 3920 us -> 224 us
  Pallas kernels: 0 us -> 766 us
  matrix products: 285 us -> 183 us
  blocking collectives: 83.7 us -> 0 us
  local copies, waits for them, and re-layouts: 49.1 us -> 110 us
    unnamed x18 -> x6, waiting for transfers between devices: 1740 us -> 0.76 us
    reduce_scatter x7 -> x4, waiting for transfers between devices: 1370 us -> 223 us  [the longest x1 187 us: on_device(): ffn_sum = lax.psum_scatter(ffn_term, PEERS, scatter_dimension=0, tiled=True)]
    all_gather x9 -> x2, waiting for transfers between devices: 816 us -> 0.02 us  [the longest x1 0.02 us: on_device(): w_down = lax.all_gather(down_weight, PEERS, axis=0, tiled=True)]
    pallas_call x0 -> x9, Pallas kernels: none -> 766 us  [exchange(): pl.pallas_call(kernel, out_shape=shapes, in_specs=[pl.BlockSpec(memory_sp...]
    dot_general x27 -> x21, matrix products: 285 us -> 183 us  [the longest x10 104 us: dot(): return lax.dot_general(a, b, dims, preferred_element_type=F32)]
    concatenate x2 -> x5, other arithmetic: 88.4 us -> 3.68 us  [the longest x1 1.45 us: on_device(): jnp.concatenate([ff_by_team(gate_weight), ff_by_team(up_weight)], axis=2)]
    unnamed x2 -> x0, blocking collectives: 83.7 us -> none
  transfers between devices with their start and end apart: 17 -> 8, of which waited for: 15 -> 2; matrix products, arithmetic and copies ran while one was open for 8% -> 16% of each run, Pallas kernels for 0% -> 42%
where the time goes in v1:
time: 1390 us; the launch traced here: 1380 us
  Pallas kernels  766 us (55%)
  waiting for transfers between devices  224 us (16%)
  matrix products  183 us (13%)
  local copies, waits for them, and re-layouts  110 us (8%)
  other arithmetic  81.1 us (6%)
  between operations  16.2 us (1%)
    pallas_call x9, Pallas kernels, exchange(): pl.pallas_call(kernel, out_shape=shapes, in_specs=[pl.BlockSpec(memory_sp...  766 us
    reduce_scatter x1, waiting for transfers between devices, on_device(): ffn_sum = lax.psum_scatter(ffn_term, PEERS, scatter_dimension=0, tiled=True)  187 us
    dot_general x10, matrix products, dot(): return lax.dot_general(a, b, dims, preferred_element_type=F32)  104 us
    dot_general x5, matrix products, dot(): return jnp.dot(a, b, preferred_element_type=F32)  52.7 us
    reduce_scatter x1, waiting for transfers between devices, on_device(): lax.psum_scatter(attn_term, PEERS, scatter_dimension=0, tiled=True)  36.1 us
  transfers between devices with their start and end apart: 8, of which 2 were waited for; matrix products, arithmetic and copies ran while one was open for 16% of the time, Pallas kernels for 42%

profile of v1, /device:TPU:0, one launch (start us, length us, event | category | flops | bytes accessed | tf_op | source)
XLA Modules:
  0.0 1382.7 jit_solution(283228222849643518)
XLA Ops:
  22.8 78.8 %shard_map.203 = (f32[32,8,128]{2,1,0:T(8,128)}, bf16[4,64,1024]{2,1,0:T(8,128)(2,1)}, bf16[4,64,4096]{2,1,0:T(8,128)(2,1)}) custom-call(f32[8,128]{1,0:T(8,128)} %copy-done.49, bf16[4,64,1024]{2,1,0:T(8,128)(2,1)} %pad_maximum_fusion.6.refs_1_, bf16[4,64,4096]{2,1,0:T(8,128)(2,1)} %pad_maximum_fusion.refs_2_), custom_call_target="tpu_custom_call" | custom-call | tf_op jit(solution)/shard_map/pallas_call | solution.py:145
  113.5 146.1 %shard_map.204 = (bf16[4,256,2048]{2,1,0:T(8,128)(2,1)}, bf16[8,4,64,1024]{3,2,1,0:T(8,128)(2,1)}, bf16[8,64,2048]{2,1,0:T(8,128)(2,1)}) custom-call(bf16[256,2048]{1,0:T(8,128)(2,1)} %fusion.31.refs_0_, bf16[4,64,1024]{2,1,0:T(8,128)(2,1)} %get-tuple-element.61.refs_1_, bf16[64,2048]{1,0:T(8,128)(2,1)} %copy-done.43), custom_call_target="tpu_custom_call" | custom-call | tf_op jit(solution)/shard_map/pallas_call | solution.py:145
  272.9 146.9 %shard_map.205 = (bf16[2,1024,512]{2,1,0:T(8,128)(2,1)}, bf16[4,256,2048]{2,1,0:T(8,128)(2,1)}) custom-call(bf16[1024,512]{1,0:T(8,128)(2,1)} %pad_maximum_fusion.3.refs_0_, bf16[256,2048]{1,0:T(8,128)(2,1)} %fusion.36.refs_1_), custom_call_target="tpu_custom_call" | custom-call | tf_op jit(solution)/shard_map/pallas_call | solution.py:145
  437.0 13.3 fusion.70
  450.3 5.7 fusion.42
  464.8 48.3 %shard_map.206 = bf16[4,256,2048]{2,1,0:T(8,128)(2,1)} custom-call(bf16[4,256,2048]{2,1,0:T(8,128)(2,1)} %bitcast.319), custom_call_target="tpu_custom_call" | custom-call | tf_op jit(solution)/shard_map/pallas_call | solution.py:145
  519.2 68.3 %shard_map.207 = bf16[4,256,2048]{2,1,0:T(8,128)(2,1)} custom-call(bf16[256,2048]{1,0:T(8,128)(2,1)} %multiply_convert_fusion.4.refs_0_), custom_call_target="tpu_custom_call" | custom-call | tf_op jit(solution)/shard_map/pallas_call | solution.py:145
  587.5 14.7 %fusion.72 = f32[1024,2048]{1,0:T(8,128)} fusion(bf16[1024,2048]{1,0:T(8,128)(2,1)} %bitcast.362, bf16[2048,2048]{1,0:T(8,128)(2,1)} %all-gather.4.cloned.1.call-done), kind=kOutput, calls=%fused_computation.178 | convolution fusion | flops 8589934592 | bytes 20971520 | tf_op jit(solution)/shard_map/dot_general | solution.py:164
  602.2 8.9 copy.165
  611.1 5.8 copy-done.6
  616.8 11.5 fusion.6
  628.4 21.8 %multiply_convert_fusion = (bf16[1024,2048]{1,0:T(8,128)(2,1)}, bf16[1024,2048]{1,0:T(8,128)(2,1)}, bf16[1024,2048]{1,0:T(8,128)(2,1)}) fusion(f32[1024,2048]{1,0:T(8,128)} %fusion.6, f32[1024,2048]{1,0:T(8,128)} %fusion.72, bf16[1024,2048]{1,0:T(8,128)(2,1)} %bitcast.286, bf16[2048,4096]{1,0:T(8,128)(2,1)} %bitcast.291), kind=kOutput, calls=%fused_computation.8 | convolution fusion | flops 8623489024 | bytes 41943040 | tf_op jit(solution)/shard_map/dot_general | solution.py:163
  650.2 12.7 fusion.4
  662.9 13.1 add_convert_fusion
  676.0 46.5 %shard_map.208 = bf16[4,256,2048]{2,1,0:T(8,128)(2,1)} custom-call(bf16[4,256,2048]{2,1,0:T(8,128)(2,1)} %bitcast.317), custom_call_target="tpu_custom_call" | custom-call | tf_op jit(solution)/shard_map/pallas_call | solution.py:145
  731.5 67.5 %shard_map.209 = bf16[4,256,2048]{2,1,0:T(8,128)(2,1)} custom-call(bf16[256,2048]{1,0:T(8,128)(2,1)} %fusion.24.refs_0_), custom_call_target="tpu_custom_call" | custom-call | tf_op jit(solution)/shard_map/pallas_call | solution.py:145
  799.0 5.9 convolution_convert_fusion.7
  804.9 14.1 %convolution_convert_fusion = bf16[2048,2048]{1,0:T(8,128)(2,1)} fusion(bf16[1024,2048]{1,0:T(8,128)(2,1)} %get-tuple-element.75, bf16[1024,2048]{1,0:T(8,128)(2,1)} %bitcast.363), kind=kOutput, calls=%fused_computation.14 | convolution fusion | flops 8594128896 | bytes 16777216 | tf_op jit(solution)/shard_map/dot_general | solution.py:164
  820.8 5.5 convolution_convert_fusion.8
  848.6 10.4 convolution_convert_fusion.3
  859.1 86.9 %shard_map.210 = (bf16[2,1024,512]{2,1,0:T(8,128)(2,1)}, bf16[4,256,2048]{2,1,0:T(8,128)(2,1)}) custom-call(bf16[2,1024,512]{2,1,0:T(8,128)(2,1)} %bitcast.300, bf16[4,256,2048]{2,1,0:T(8,128)(2,1)} %bitcast.311), custom_call_target="tpu_custom_call" | custom-call | tf_op jit(solution)/shard_map/pallas_call | solution.py:145
  952.7 5.5 multiply_bitcast_fusion
  961.7 8.5 convolution_convert_fusion.5
  972.8 6.6 copy.178
  979.4 12.2 convolution_convert_fusion.1
  991.5 9.4 convolution_convert_fusion.2
  1002.9 7.0 copy.179
  1010.6 8.4 convolution_convert_fusion.6
  1027.0 36.1 %reduce-scatter.5.cloned.1.call-done = bf16[256,1024]{1,0:T(8,128)(2,1)} async-done(((bf16[2048,1024]{1,0:T(8,128)(2,1)}), bf16[256,1024]{1,0:T(8,128)(2,1)}) %reduce-scatter.5.cloned.1.call-update) | async-done | bytes 524304 | tf_op jit(solution)/shard_map/reduce_scatter | solution.py:386
  1063.2 186.9 %reduce-scatter.7.cloned.1.call-done = bf16[256,4096]{1,0:T(8,128)(2,1)} async-done(((bf16[2048,4096]{1,0:T(8,128)(2,1)}), bf16[256,4096]{1,0:T(8,128)(2,1)}) %reduce-scatter.7.cloned.1.call-update) | async-done | bytes 2097168 | tf_op jit(solution)/shard_map/reduce_scatter | solution.py:355
  1250.1 76.9 %shard_map.211 = (bf16[4,256,2048]{2,1,0:T(8,128)(2,1)}, bf16[4,64,1024]{2,1,0:T(8,128)(2,1)}, bf16[4,64,4096]{2,1,0:T(8,128)(2,1)}) custom-call(bf16[4,256,2048]{2,1,0:T(8,128)(2,1)} %bitcast.324, bf16[4,64,1024]{2,1,0:T(8,128)(2,1)} %bitcast.352, bf16[4,64,4096]{2,1,0:T(8,128)(2,1)} %bitcast.325), custom_call_target="tpu_custom_call" | custom-call | tf_op jit(solution)/shard_map/pallas_call | solution.py:145
  1367.9 7.7 fusion.28
  (291 shorter events, 168.7 us)
Async XLA Ops:
  7.2 580.3 %all-gather.4.cloned.1.call-start = ((), (), s32[]{:S(2)}) async-start(), calls=%async_computation.4 | async-start | bytes 9437184 | tf_op jit(solution)/shard_map/all_gather | solution.py:258
  7.9 594.3 %all-gather.6.cloned.1.call-start = ((), (), s32[]{:S(2)}) async-start(), calls=%async_computation.9 | async-start | bytes 18874368 | tf_op jit(solution)/shard_map/all_gather | solution.py:268
  12.9 6.6 copy-start.40
  22.8 78.9 %copy-start.68 = (bf16[64,2048]{1,0:T(8,128)(2,1)S(1)}, bf16[64,2048]{1,0:T(8,128)(2,1)}, u32[]{:S(2)}) copy-start(bf16[64,2048]{1,0:T(8,128)(2,1)} %param.24) | copy-start | bytes 786436
  22.8 82.2 %copy-start.3 = (bf16[1,2,128,2048]{3,2,1,0:T(8,128)(2,1)S(1)}, bf16[1,2,128,2048]{3,2,1,0:T(8,128)(2,1)}, u32[]{:S(2)}) copy-start(bf16[1,2,128,2048]{3,2,1,0:T(8,128)(2,1)} %param.18) | copy-start | bytes 3145732
  101.6 6.6 copy-start.8
  101.6 917.3 %reduce-scatter.9.cloned.1.call-start = ((), (), s32[]{:S(2)}) async-start(), calls=%async_computation.7 | async-start | bytes 2359296 | tf_op jit(solution)/shard_map/reduce_scatter | solution.py:388
  101.7 11.0 collective-permute-start
  103.7 5.7 copy-start.47
  110.8 615.8 %copy-start.45 = (f32[2048]{0:T(1024)}, f32[2048]{0:T(1024)S(1)}, u32[]{:S(2)}) copy-start(f32[2048]{0:T(1024)S(1)} %mul.426) | copy-start | bytes 24580
  112.7 316.0 %copy-start.14 = (f32[512,128]{1,0:T(8,128)}, f32[512,128]{1,0:T(8,128)S(1)}, u32[]{:S(2)}) copy-start(f32[512,128]{1,0:T(8,128)S(1)} %get-tuple-element.95) | copy-start | bytes 786436
  262.6 5.0 copy-start.19
  421.6 28.7 %copy-start.11 = (bf16[2,2,512,512]{3,2,1,0:T(8,128)(2,1)}, bf16[2,2,512,512]{3,2,1,0:T(8,128)(2,1)S(1)}, u32[]{:S(2)}) copy-start(bf16[2,2,512,512]{3,2,1,0:T(8,128)(2,1)S(1)} %copy.157) | copy-start | bytes 6291460
  432.5 4.6 copy-start.33
  450.3 5.7 copy-start.52
  458.7 6.0 copy-start.34
  602.2 14.7 %copy-start.5 = (bf16[4,256,2048]{2,1,0:T(8,128)(2,1)S(1)}, bf16[4,256,2048]{2,1,0:T(8,128)(2,1)}, u32[]{:S(2)}) copy-start(bf16[4,256,2048]{2,1,0:T(8,128)(2,1)} %shard_map.207) | copy-start | bytes 12582916
  611.0 5.8 copy-start.6
  650.2 12.7 copy-start.70
  731.5 67.5 %copy-start.35 = (bf16[128,8,2,256]{3,1,2,0:T(8,128)(2,1)S(1)}, bf16[128,8,2,256]{3,1,2,0:T(8,128)(2,1)}, u32[]{:S(2)}) copy-start(bf16[128,8,2,256]{3,1,2,0:T(8,128)(2,1)} %copy-done.34) | copy-start | bytes 3145732
  804.9 219.4 %reduce-scatter.11.cloned.1.call-start = ((), (), s32[]{:S(2)}) async-start(), calls=%async_computation.8 | async-start | bytes 9437184 | tf_op jit(solution)/shard_map/reduce_scatter | solution.py:351
  819.0 244.2 %reduce-scatter.5.cloned.1.call-start = ((), (), s32[]{:S(2)}) async-start(), calls=%async_computation.5 | async-start | bytes 4718592 | tf_op jit(solution)/shard_map/reduce_scatter | solution.py:386
  820.8 7.5 copy-start.53
  832.6 6.8 copy-start.29
  832.6 6.8 copy-start.31
  839.4 7.7 slice-start
  840.7 6.5 slice-start.1
  972.7 277.4 %reduce-scatter.7.cloned.1.call-start = ((), (), s32[]{:S(2)}) async-start(), calls=%async_computation.6 | async-start | bytes 18874368 | tf_op jit(solution)/shard_map/reduce_scatter | solution.py:355
  979.4 12.2 copy-start.20
  979.4 12.2 copy-start.71
  1019.0 4.5 collective-permute-start.1
  1332.5 4.5 copy-start.36
  (51 other events, 113.6 us)
Sparse Core Ops, SparseCore 0:
  9.9 94.7 all-gather.3
  106.6 231.1 all-gather.5
  805.0 49.4 reduce-scatter.8
  858.2 122.5 reduce-scatter.10
  984.0 79.1 reduce-scatter.4
  1067.0 183.0 reduce-scatter.6

commit v2 on v1

v2 whole, which is shorter than its diff:
```python
import itertools
import math

import jax
import jax.numpy as jnp
from jax import lax
from jax.experimental import pallas as pl
from jax.experimental.pallas import tpu as pltpu
from jax.sharding import Mesh
from jax.sharding import PartitionSpec as P

HEAD = 256
VMEM_LIMIT = 48 << 20
BLK = 128
EPS = 1e-06
ROPE_BASE = 1000042.0
AXES = ("zh", "zl", "y", "x", "c")
TEAM = ("zl", "y")
SLOTS = ("y", "zl")
SHARES = ("c", "x", "zh")
OWNERS = ("zl", "y", "c")
ROWS_T = (((0,), (0,)), ((), ()))
PAIR_ROWS_T = (((0, 1), (0, 1)), ((), ()))
COLS_T = (((1,), (1,)), ((), ()))
F32 = jnp.float32
BF16 = jnp.bfloat16


def offsets(sizes, axes):
    return [dict(zip(axes, o)) for o in itertools.product(*(range(sizes[a]) for a in axes))]


def place(at, layout, sizes):
    index = 0
    for a in layout:
        index = index * sizes[a] + at[a]
    return index


class Gather:
    def __init__(self, x, layout, order, chunks=1, dim=0, rank=1):
        self.rank = rank
        self.x, self.layout, self.chunks, self.dim = x, layout, chunks, dim
        self.orders = [order] * chunks if isinstance(order[0], str) else order
        self.chunks = len(self.orders)

    def out_shape(self, sizes):
        return (math.prod(sizes[a] for a in self.layout),) + self.x.shape

    def own_shape(self, sizes):
        return self.x.shape

    def cut(self, ref, part):
        rows = self.x.shape[self.dim] // self.chunks
        return ref.at[(slice(None),) * self.dim + (pl.ds(part * rows, rows),)]

    def spot(self, out, owner, off, sizes):
        return out.at[place(owner, self.layout, sizes)]


class PairGather(Gather):
    def out_shape(self, sizes):
        return (2, math.prod(sizes[a] for a in self.layout)) + self.x.shape

    def spot(self, out, owner, off, sizes):
        return out.at[off["c"], place(owner, self.layout, sizes)]


class RowGather(Gather):
    def out_shape(self, sizes):
        zl, y, rows, columns = self.x.shape
        return (sizes["x"], sizes["zh"], zl, y, sizes["c"], rows, columns)

    def spot(self, out, owner, off, sizes):
        return out.at[owner["x"], owner["zh"], :, :, owner["c"]]


class Swap:
    def __init__(self, x, layout):
        self.x, self.layout = x, layout

    def out_shape(self, sizes):
        return self.x.shape

    def own_shape(self, sizes):
        return self.x.shape[1:]

    def offsets(self, sizes):
        return offsets(sizes, self.layout)

    def pair(self, x, out, here, to, off, sizes):
        return x.at[place(to, self.layout, sizes)], out.at[place(here, self.layout, sizes)]


class Halves:
    def __init__(self, x):
        self.x = x

    def out_shape(self, sizes):
        rows, columns = self.x.shape
        return (2, rows, columns // 2)

    def own_shape(self, sizes):
        rows, columns = self.x.shape
        return (rows, columns // 2)

    def offsets(self, sizes):
        return offsets(sizes, ("c",))

    def pair(self, x, out, here, to, off, sizes):
        width = self.x.shape[1] // 2
        start = pl.multiple_of(to["c"] * width, 128)
        return x.at[:, pl.ds(start, width)], out.at[off["c"]]


def exchange(jobs, collective_id, micros=50):
    sizes = {a: lax.axis_size(a) for a in AXES}
    n_sems = 0
    reached = set()
    steps, swaps = [], []
    for number, job in enumerate(jobs):
        if isinstance(job, Gather):
            for part, order in enumerate(job.orders):
                for off in offsets(sizes, order):
                    used = [i for i, a in enumerate(order) if off[a]]
                    sends = []
                    for a in order[used[-1] + 1 if used else 0 :]:
                        for d in range(1, sizes[a]):
                            sends.append((a, d, n_sems))
                            n_sems += 1
                            reached.add(tuple(d if b == a else 0 for b in AXES))
                    steps.append((job.rank, part + 2 * len(used), len(used), number, part, off, sends))
        else:
            for off in job.offsets(sizes):
                if any(off.values()):
                    swaps.append((number, off, n_sems))
                    n_sems += 1
                    reached.add(tuple(off.get(b, 0) for b in AXES))
    steps.sort(key=lambda s: s[:4])
    count = len(jobs)

    def kernel(*refs):
        ins, outs = refs[:count], refs[count : 2 * count]
        stages = refs[2 * count : 3 * count]
        send_sem, recv_sem, local_sem = refs[3 * count :]
        here = {a: lax.axis_index(a) for a in AXES}

        def moved(off):
            return {
                a: lax.rem(here[a] + off[a], sizes[a]) if off.get(a, 0) else here[a] for a in AXES
            }

        def device(at):
            return tuple(at[a] for a in AXES)

        barrier = pltpu.get_barrier_semaphore()
        for off in sorted(reached):
            pl.semaphore_signal(
                barrier,
                inc=1,
                device_id=device(moved(dict(zip(AXES, off)))),
                device_id_type=pl.DeviceIdType.MESH,
            )
        pl.semaphore_wait(barrier, len(reached))

        def copy(src, dst, sem, at):
            return pltpu.make_async_remote_copy(
                src_ref=src,
                dst_ref=dst,
                send_sem=send_sem.at[sem],
                recv_sem=recv_sem.at[sem],
                device_id=device(at),
                device_id_type=pl.DeviceIdType.MESH,
            )

        local, sent, received = [], [], []
        arrivals = {}

        def pass_on(step):
            _, _, hops, number, part, off, sends = step
            job = jobs[number]
            spot = job.cut(job.spot(outs[number], moved(off), off, sizes), part)
            if hops:
                arrivals[number, part, tuple(sorted(off.items()))].wait_recv()
            source = spot if hops else job.cut(ins[number], part)
            for a, d, sem in sends:
                there = dict(off)
                there[a] = (-d) % sizes[a]
                dst = job.cut(job.spot(outs[number], moved(off), there, sizes), part)
                cp = copy(source, dst, sem, moved({a: d}))
                cp.start()
                sent.append(cp)
                arrivals[number, part, tuple(sorted(there.items()))] = cp

        for number, job in enumerate(jobs):
            none = {a: 0 for a in AXES}
            if isinstance(job, Gather):
                src, dst = ins[number], job.spot(outs[number], here, none, sizes)
            else:
                src, dst = job.pair(ins[number], outs[number], here, here, none, sizes)
            load = pltpu.make_async_copy(src, stages[number], local_sem.at[number, 0])
            load.start()
            local.append((load, pltpu.make_async_copy(stages[number], dst, local_sem.at[number, 1])))
        for step in steps:
            if not step[1]:
                pass_on(step)
        for number, off, sem in swaps:
            to = moved(off)
            src, dst = jobs[number].pair(ins[number], outs[number], here, to, off, sizes)
            cp = copy(src, dst, sem, to)
            cp.start()
            sent.append(cp)
            received.append(cp)
        for load, store in local:
            load.wait()
            store.start()
        for step in steps:
            if step[1]:
                pass_on(step)
        for cp in received:
            cp.wait_recv()
        for cp in sent:
            cp.wait_send()
        for _, store in local:
            store.wait()

    return pl.pallas_call(
        kernel,
        out_shape=[jax.ShapeDtypeStruct(job.out_shape(sizes), job.x.dtype) for job in jobs],
        in_specs=[pl.BlockSpec(memory_space=pl.ANY)] * count,
        out_specs=[pl.BlockSpec(memory_space=pl.ANY)] * count,
        scratch_shapes=[pltpu.VMEM(job.own_shape(sizes), job.x.dtype) for job in jobs]
        + [
            pltpu.SemaphoreType.DMA((n_sems,)),
            pltpu.SemaphoreType.DMA((n_sems,)),
            pltpu.SemaphoreType.DMA((count, 2)),
        ],
        cost_estimate=pl.CostEstimate(
            flops=0, bytes_accessed=micros * 3_000_000, transcendentals=0
        ),
        compiler_params=pltpu.CompilerParams(
            collective_id=collective_id, has_side_effects=True, vmem_limit_bytes=VMEM_LIMIT
        ),
    )(*[job.x for job in jobs])


def sum_over(term, axis):
    size = lax.axis_size(axis)
    me = lax.axis_index(axis)
    while size > 1:
        size //= 2
        rows = term.shape[0] // 2
        pairs = [(i, i ^ size) for i in range(lax.axis_size(axis))]
        side = (me // size) % 2
        kept = lax.dynamic_slice_in_dim(term, side * rows, rows)
        other = lax.ppermute(
            lax.dynamic_slice_in_dim(term, (1 - side) * rows, rows), axis, pairs
        )
        term = kept.astype(F32) + other.astype(F32)
        if size > 1:
            term = term.astype(BF16)
    return term


def dot(a, b, dims=None):
    if dims is None:
        return jnp.dot(a, b, preferred_element_type=F32)
    return lax.dot_general(a, b, dims, preferred_element_type=F32)


def rotate(t, cos, sin):
    half = t.shape[-1] // 2
    front, back = t[..., :half], t[..., half:]
    return jnp.concatenate([front * cos - back * sin, back * cos + front * sin], axis=-1)


def rms_scale(values):
    return lax.rsqrt(jnp.mean(values * values, axis=-1, keepdims=True) + EPS)


def positions(members):
    total = lax.axis_size("zh") * lax.axis_size("zl")
    half = jnp.arange(2)[None, :, None]
    row = jnp.arange(BLK)[None, None, :]
    j = members[:, None, None]
    return (jnp.where(half == 0, j, 2 * total - 1 - j) * BLK + row).reshape(-1)


OUTWARD = ("zh", "x", "c")
TO_TEAM = (("zl", "y", "c"), ("zl", "y", "c"))
TO_TEAM_EVEN = (("zl", "y", "c"), ("y", "zl", "c"))


def on_device(
    inputs,
    lengths,
    attn_gain,
    query_weight,
    key_matrix,
    value_matrix,
    output_weight,
    ffn_gain,
    gate_weight,
    up_weight,
    down_weight,
    cotangent,
):
    size = {a: lax.axis_size(a) for a in AXES}
    at = {a: lax.axis_index(a) for a in AXES}
    width = inputs.shape[3]
    own = inputs.shape[1] * inputs.shape[2]
    rows = query_weight.shape[0]
    n_dev = width // rows
    team = size["y"] * size["zl"]
    q_cols = query_weight.shape[1] // team
    kv_cols = key_matrix.shape[1] // team
    ff_rows = down_weight.shape[0]
    ff = gate_weight.shape[1] // team
    heads = q_cols // HEAD
    n_tok = team * own
    scaling = HEAD**-0.5

    def by_team(w):
        return w.reshape(rows, team, -1).transpose(1, 0, 2)

    def ff_by_team(w):
        cut = w.reshape(rows, *(size[a] for a in AXES), ff_rows)
        return cut.transpose(2, 3, 0, 5, 4, 1, 6).reshape(team, rows, ff)

    attn_cut = jnp.concatenate(
        [by_team(query_weight), by_team(key_matrix), by_team(value_matrix)], axis=2
    )
    tile = jnp.zeros((8, 128), F32)
    tile = tile.at[0, :rows].set(attn_gain.astype(F32))
    tile = tile.at[0, 64 : 64 + rows].set(ffn_gain.astype(F32))
    tile = tile.at[1].set(lengths[0].astype(F32))
    tiles, attn_part, gate_part, up_part = exchange(
        [
            Gather(tile, AXES, ("c", "x", "y", "zl", "zh"), rank=0),
            Swap(attn_cut, TEAM),
            Swap(ff_by_team(gate_weight), TEAM),
            Swap(ff_by_team(up_weight), TEAM),
        ],
        1,
    )
    w_down = lax.all_gather(down_weight, SHARES, axis=0, tiled=True)
    gain_one = tiles[:, 0, :rows].reshape(1, width)
    gain_two = tiles[:, 0, 64 : 64 + rows].reshape(1, width)
    slots = tiles[: n_dev // (size["zh"] * size["zl"]), 1, 0].reshape(
        size["y"], size["x"], size["c"]
    )
    lens = slots[:, at["x"], at["c"]].astype(jnp.int32)

    per_head = n_dev // team

    def head_home(i):
        f, t = i // per_head, i % per_head
        zl, y = f // size["y"], f % size["y"]
        zh, t = t % size["zh"], t // size["zh"]
        x, c = t % size["x"], t // size["x"]
        return (((zh * size["zl"] + zl) * size["y"] + y) * size["x"] + x) * size["c"] + c

    homes = [(i, head_home(i)) for i in range(n_dev)]
    out_part = lax.ppermute(output_weight, AXES, homes)

    def row_gather(part):
        part = part.reshape(size["zl"], size["y"], rows, -1)
        return RowGather(part, None, OUTWARD, chunks=rows // 16, dim=2)

    def spread(v):
        cut = v.reshape(own, size["zh"], size["zl"], size["y"], size["x"], size["c"] * rows)
        return cut.transpose(0, 4, 1, 2, 3, 5).reshape(own, width)

    def natural(v):
        cut = v.reshape(own, size["x"], size["zh"], size["zl"], size["y"], size["c"] * rows)
        return cut.transpose(0, 2, 3, 4, 1, 5).reshape(own, width)

    my_pos = positions((at["zh"] * size["zl"] + at["zl"])[None])
    valid = (my_pos < lengths[0]).astype(F32)[:, None]
    q_pos = positions(at["zh"] * size["zl"] + jnp.arange(size["zl"]))
    k_pos = positions(jnp.arange(size["zh"] * size["zl"]))
    half = HEAD // 2
    freq = ROPE_BASE ** (-2.0 * jnp.arange(half).astype(F32) / HEAD)
    angles = q_pos.astype(F32)[:, None] * freq[None, :]
    cos = jnp.tile(jnp.cos(angles), (size["y"], 1))[:, None, :]
    sin = jnp.tile(jnp.sin(angles), (size["y"], 1))[:, None, :]

    tokens = inputs.reshape(own, width).astype(F32)
    scale_one = rms_scale(tokens)
    norm_one = (tokens * scale_one * gain_one).astype(BF16)
    norm_one_pair, w_attn, w_out = exchange(
        [
            PairGather(spread(norm_one), SLOTS, TO_TEAM),
            row_gather(attn_part),
            Gather(out_part, SHARES, OUTWARD, chunks=rows // 16),
        ],
        2,
    )
    norm_one_pair = norm_one_pair.reshape(2, n_tok, width)
    w_attn = w_attn.reshape(width, -1)
    w_out = w_out.reshape(q_cols, width)
    qkv = dot(norm_one_pair[0], w_attn)
    q = rotate(qkv[:, :q_cols].reshape(n_tok, heads, HEAD), cos, sin).astype(BF16)
    k = rotate(qkv[:, q_cols : q_cols + kv_cols].reshape(n_tok, 1, HEAD), cos, sin).astype(BF16)
    v = qkv[:, q_cols + kv_cols :].astype(BF16)
    kv = jnp.concatenate([k.reshape(n_tok, kv_cols), v], axis=1)
    gy = valid * cotangent.reshape(own, width).astype(F32)
    kv_all, gd_pair = exchange(
        [Gather(kv, ("zh",), ("zh",)), PairGather(gy.astype(BF16), SLOTS, TO_TEAM)], 3
    )
    gd_pair = gd_pair.reshape(2, n_tok, width)
    n_slot = size["y"]
    n_q = n_tok // n_slot
    q = q.reshape(n_slot, n_q, heads, HEAD)
    kv_all = kv_all.reshape(size["zh"], n_slot, n_q, 2 * kv_cols).transpose(1, 0, 2, 3)
    kv_all = kv_all.reshape(n_slot, size["zh"] * n_q, 2 * kv_cols)
    k_all, v_all = kv_all[:, :, :kv_cols], kv_all[:, :, kv_cols:]
    allowed = (k_pos[None, None, :] <= q_pos[None, :, None]) & (
        k_pos[None, None, :] < lens[:, None, None]
    )
    scores = jnp.einsum("bqgd,bkd->bgqk", q, k_all, preferred_element_type=F32) * scaling
    scores = jnp.where(allowed[:, None], scores, -jnp.inf)
    peak = jnp.max(scores, axis=-1, keepdims=True)
    exps = jnp.exp(scores - peak)
    prob = exps / jnp.sum(exps, axis=-1, keepdims=True)
    prob_b = prob.astype(BF16)
    o = jnp.einsum("bgqk,bkd->bqgd", prob_b, v_all, preferred_element_type=F32)
    o = o.reshape(n_tok, q_cols).astype(BF16)

    def team_sum(parts):
        return sum(parts[i].astype(F32) for i in range(team))

    def blocks(partial):
        return partial.astype(BF16).reshape(team, own, width)

    o_parts, w_gate = exchange(
        [Swap(blocks(dot(o, w_out)), SLOTS), row_gather(gate_part)], 4
    )
    w_gate = w_gate.reshape(width, ff)
    h1 = tokens + team_sum(o_parts)
    scale_two = rms_scale(h1)
    norm_two = (h1 * scale_two * gain_two).astype(BF16)
    norm_two_pair, w_up = exchange(
        [PairGather(spread(norm_two), SLOTS, TO_TEAM), row_gather(up_part)], 5
    )
    w_up = w_up.reshape(width, ff)
    norm_two_pair = norm_two_pair.reshape(2, n_tok, width)

    gate = dot(norm_two_pair[0], w_gate)
    up = dot(norm_two_pair[0], w_up)
    sg = jax.nn.sigmoid(gate)
    mixed = (gate * sg * up).astype(BF16)
    gm = dot(gd_pair[0], w_down, COLS_T)
    g_gate = (gm * up * sg * (1.0 + gate * (1.0 - sg))).astype(BF16)
    g_up = (gm * gate * sg).astype(BF16)
    gate_half, up_half, mixed_half = exchange(
        [Halves(g_gate), Halves(g_up), Halves(mixed)], 6, micros=10
    )
    tie = lax.optimization_barrier
    down_term = dot(mixed_half, gd_pair, PAIR_ROWS_T).astype(BF16)
    gn2_parts = blocks(dot(g_gate, w_gate, COLS_T) + dot(g_up, w_up, COLS_T))
    gn2_parts, down_term = tie((gn2_parts, down_term))
    down_x = sum_over(down_term, "x").astype(BF16)
    (gn2_parts,) = exchange([Swap(gn2_parts, SLOTS)], 7)
    gn2_parts, down_x = tie((gn2_parts, down_x))
    gn2 = natural(team_sum(gn2_parts)) * gain_two
    gh1 = gy + scale_two * gn2 - h1 * scale_two**3 * jnp.mean(h1 * gn2, axis=-1, keepdims=True)

    gate_term = dot(norm_two_pair, gate_half, PAIR_ROWS_T).astype(BF16)
    up_term = dot(norm_two_pair, up_half, PAIR_ROWS_T).astype(BF16)
    ga, gate_term, up_term, down_x = tie((gh1.astype(BF16), gate_term, up_term, down_x))
    gate_x = sum_over(gate_term, "x").astype(BF16)
    down_grad = sum_over(down_x, "zh")
    ga_pair, o_half = exchange([PairGather(ga, SLOTS, TO_TEAM_EVEN), Halves(o)], 8)
    ga_pair, gate_x, down_grad = tie((ga_pair, gate_x, down_grad))
    ga_pair = ga_pair.reshape(2, n_tok, width)

    go = dot(ga_pair[0], w_out, COLS_T).astype(BF16).reshape(n_slot, n_q, heads, HEAD)
    gp = jnp.einsum("bqgd,bkd->bgqk", go, v_all, preferred_element_type=F32)
    delta = jnp.sum(prob * gp, axis=-1, keepdims=True)
    gs = (prob * (gp - delta)).astype(BF16)
    gq_rot = jnp.einsum("bgqk,bkd->bqgd", gs, k_all, preferred_element_type=F32) * scaling
    gk_rot = jnp.einsum("bgqk,bqgd->bkd", gs, q, preferred_element_type=F32) * scaling
    gv_sum = jnp.einsum("bgqk,bqgd->bkd", prob_b, go, preferred_element_type=F32)
    gkv = jnp.concatenate([gk_rot, gv_sum], axis=-1).astype(BF16)
    gkv = gkv.reshape(n_slot, size["zh"], n_q, 2 * kv_cols).transpose(1, 0, 2, 3)
    gkv = gkv.reshape(size["zh"], n_tok, 2 * kv_cols)
    out_parts = blocks(dot(mixed, w_down))
    out_term = dot(o_half, ga_pair, PAIR_ROWS_T).astype(BF16)
    gkv, out_parts, gate_x, up_term, out_term = tie((gkv, out_parts, gate_x, up_term, out_term))
    up_x = sum_over(up_term, "x").astype(BF16)
    out_x = sum_over(out_term, "x").astype(BF16)
    gate_sum = sum_over(gate_x, "zh").astype(BF16)
    gkv_parts, out_parts = exchange([Swap(gkv, ("zh",)), Swap(out_parts, SLOTS)], 9)
    gkv_parts, up_x, out_x, gate_sum = tie((gkv_parts, up_x, out_x, gate_sum))
    gkv = sum(gkv_parts[i].astype(F32) for i in range(size["zh"]))
    gq = rotate(gq_rot.reshape(n_tok, heads, HEAD), cos, -sin).astype(BF16)
    gk = rotate(gkv[:, :kv_cols].reshape(n_tok, 1, HEAD), cos, -sin).astype(BF16)
    g_qkv = jnp.concatenate(
        [gq.reshape(n_tok, q_cols), gk.reshape(n_tok, kv_cols), gkv[:, kv_cols:].astype(BF16)],
        axis=1,
    )
    cols = g_qkv.shape[1] // 2
    mine = lax.dynamic_slice_in_dim(g_qkv, at["c"] * cols, cols, axis=1)
    other = lax.dynamic_slice_in_dim(g_qkv, (1 - at["c"]) * cols, cols, axis=1)
    g_qkv_half = jnp.stack([mine, lax.ppermute(other, "c", [(0, 1), (1, 0)])])
    attn_term = dot(norm_one_pair, g_qkv_half, PAIR_ROWS_T).astype(BF16)
    gn1_parts = blocks(dot(g_qkv, w_attn, COLS_T))
    gn1_parts, attn_term, up_x, out_x = tie((gn1_parts, attn_term, up_x, out_x))
    attn_x = sum_over(attn_term, "x").astype(BF16)
    up_sum = sum_over(up_x, "zh").astype(BF16)
    out_sum = sum_over(out_x, "zh").astype(BF16)
    (gn1_parts,) = exchange([Swap(gn1_parts, SLOTS)], 10)
    gn1_parts, attn_x, up_sum, out_sum = tie((gn1_parts, attn_x, up_sum, out_sum))
    attn_sum = sum_over(attn_x, "zh")
    out_sum = lax.ppermute(out_sum, AXES, [(b, a) for a, b in homes])
    outputs = (valid * (h1 + team_sum(out_parts))).astype(BF16).reshape(inputs.shape)
    n_owners = math.prod(size[a] for a in OWNERS)

    def by_owner(total):
        return total.astype(BF16).reshape(n_owners, rows, -1)

    gate_sum, up_sum = exchange([Swap(by_owner(t), OWNERS) for t in (gate_sum, up_sum)], 11)
    attn_sum, gate_sum, up_sum = tie((attn_sum, gate_sum, up_sum))
    (attn_sum,) = exchange([Swap(by_owner(attn_sum), OWNERS)], 12)
    gn1 = natural(team_sum(gn1_parts)) * gain_one
    g_tokens = (
        gh1
        + scale_one * gn1
        - tokens * scale_one**3 * jnp.mean(tokens * gn1, axis=-1, keepdims=True)
    )
    input_grad = g_tokens.astype(BF16).reshape(inputs.shape)

    def ff_natural(total):
        cut = total.reshape(
            size["zl"], size["y"], size["c"], rows, size["x"], size["zh"], ff_rows
        )
        return cut.transpose(3, 5, 0, 1, 4, 2, 6).reshape(rows, -1).astype(F32)

    def side(part):
        return part.transpose(1, 0, 2).reshape(rows, -1).astype(F32)

    attn_sum = attn_sum.reshape(team, 2, rows, -1)
    query_grad = side(attn_sum[:, 0])
    key_grad = side(attn_sum[:, 1, :, :kv_cols])
    value_grad = side(attn_sum[:, 1, :, kv_cols:])
    gate_grad = ff_natural(gate_sum)
    up_grad = ff_natural(up_sum)

    def against(w, g):
        return jnp.sum(w.astype(F32) * g, axis=1)

    attn_gain_grad = (
        against(query_weight, query_grad)
        + against(key_matrix, key_grad)
        + against(value_matrix, value_grad)
    ) / attn_gain.astype(F32)
    ffn_gain_grad = (against(gate_weight, gate_grad) + against(up_weight, up_grad)) / (
        ffn_gain.astype(F32)
    )
    return (
        outputs,
        input_grad,
        attn_gain_grad,
        query_grad,
        key_grad,
        value_grad,
        out_sum.astype(F32),
        ffn_gain_grad,
        gate_grad,
        up_grad,
        down_grad,
    )


def solution(mesh):
    ctx, fsdp = mesh.shape["ctx"], mesh.shape["fsdp"]
    grid = Mesh(mesh.devices.reshape(ctx // 2, 2, 2, fsdp // 4, 2), AXES)
    act = P(("y", "x", "c"), None, ("zh", "zl"), None)
    row = P(AXES)
    return jax.shard_map(
        on_device,
        mesh=grid,
        in_specs=(act, P(("y", "x", "c"))) + (row,) * 9 + (act,),
        out_specs=(act, act) + (row,) * 9,
        check_vma=False,
    )
```

time: 1390 us -> 1110 us (0.80)
  waiting for transfers between devices: 224 us -> 0.72 us
  Pallas kernels: 766 us -> 682 us
  local copies, waits for them, and re-layouts: 110 us -> 136 us
  starting transfers between devices: 2.65 us -> 17.4 us
    reduce_scatter x4 -> x0, waiting for transfers between devices: 223 us -> none  [the longest x1 187 us: on_device(): ffn_sum = lax.psum_scatter(ffn_term, PEERS, scatter_dimension=0, tiled=True)]
    pallas_call x9 -> x12, Pallas kernels: 766 us -> 682 us  [exchange(): pl.pallas_call(kernel, out_shape=[jax.ShapeDtypeStruct(job.out_shape(size...]
    convert_element_type x0 -> x11, local copies, waits for them, and re-layouts: none -> 26.4 us  [the longest x6 22.1 us: ff_natural(): return cut.transpose(3, 5, 0, 1, 4, 2, 6).reshape(rows, -1).astype(F32)]
    reshape x17 -> x12, local copies, waits for them, and re-layouts: 35.2 us -> 21 us  [the longest x3 10.7 us: natural(): return cut.transpose(0, 2, 3, 4, 1, 5).reshape(own, width)]
    ppermute x1 -> x12, starting transfers between devices: 1.6 us -> 15.7 us  [the longest x10 14.1 us: sum_over(): lax.ppermute(lax.dynamic_slice_in_dim(term, (1 - side) * rows, rows), axi...]
  transfers between devices with their start and end apart: 8 -> 14, of which waited for: 2 -> 0; matrix products, arithmetic and copies ran while one was open for 16% -> 18% of each run, Pallas kernels for 42% -> 60%
where the time goes in v2:
time: 1110 us; the launch traced here: 1100 us
  Pallas kernels  682 us (61%)
  matrix products  178 us (16%)
  local copies, waits for them, and re-layouts  136 us (12%)
  other arithmetic  70.9 us (6%)
  starting transfers between devices  17.4 us (2%)
  between operations  16.7 us (2%)
    pallas_call x12, Pallas kernels, exchange(): pl.pallas_call(kernel, out_shape=[jax.ShapeDtypeStruct(job.out_shape(size...  682 us
    dot_general x10, matrix products, dot(): return lax.dot_general(a, b, dims, preferred_element_type=F32)  100 us
    dot_general x5, matrix products, dot(): return jnp.dot(a, b, preferred_element_type=F32)  54.1 us
    unnamed x211, local copies, waits for them, and re-layouts  27.1 us
  transfers between devices with their start and end apart: 14, of which 0 were waited for; matrix products, arithmetic and copies ran while one was open for 18% of the time, Pallas kernels for 60%

profile of v2, /device:TPU:0, one launch (start us, length us, event | category | flops | bytes accessed | tf_op | source)
XLA Modules:
  0.0 1102.0 jit_solution(1722662950871579639)
XLA Ops:
  24.9 72.0 %shard_map.203 = (f32[32,8,128]{2,1,0:T(8,128)S(1)}, bf16[4,64,1024]{2,1,0:T(8,128)(2,1)S(1)}, bf16[4,64,2048]{2,1,0:T(8,128)(2,1)S(1)}, bf16[4,64,2048]{2,1,0:T(8,128)(2,1)S(1)}) custom-call(f32[8,128]{1,0:T(8,128)S(1)} %scatter.14.refs_0_, bf16[4,64,1024]{2,1,0:T(8,128)(2,1)S(1)} %pad_maximum_fusion.4.refs_1_, bf16[4,64,2048]{2,1,0:T(8,128)(2,1)S(1)} %reshape.1033.refs_2_, ...), custom_call_target="tpu_custom_call" | custom-call | bytes 150000000 | tf_op jit(solution)/shard_map/pallas_call | solution.py:227
  116.7 58.1 %shard_map.204 = (bf16[2,4,256,2048]{3,2,1,0:T(8,128)(2,1)}, bf16[2,2,2,2,2,64,1024]{6,5,4,3,2,1,0:T(8,128)(2,1)}, bf16[8,64,2048]{2,1,0:T(8,128)(2,1)S(1)}) custom-call(bf16[256,2048]{1,0:T(8,128)(2,1)S(1)} %reshape.1036.refs_0_, bf16[2,2,64,1024]{3,2,1,0:T(8,128)(2,1)S(1)} %bitcast.309, bf16[64,2048]{1,0:T(8,128)(2,1)S(1)} %collective-permute-done.refs_2_), custom_call_target="tpu_custom_call" | custom-call | bytes 150000000 | tf_op jit(solution)/shard_map/pallas_call | solution.py:227
  179.0 4.5 fusion.59
  192.0 76.5 %shard_map.205 = (bf16[2,1024,512]{2,1,0:T(8,128)(2,1)S(1)}, bf16[2,4,256,2048]{3,2,1,0:T(8,128)(2,1)}) custom-call(bf16[1024,512]{1,0:T(8,128)(2,1)S(1)} %pad_maximum_fusion.2.refs_0_, bf16[256,2048]{1,0:T(8,128)(2,1)S(1)} %fusion.21.refs_1_), custom_call_target="tpu_custom_call" | custom-call | bytes 150000000 | tf_op jit(solution)/shard_map/pallas_call | solution.py:227
  278.1 6.6 fusion.58
  284.7 6.0 fusion.27
  300.3 72.2 %shard_map.206 = (bf16[4,256,2048]{2,1,0:T(8,128)(2,1)S(1)}, bf16[2,2,2,2,2,64,2048]{6,5,4,3,2,1,0:T(8,128)(2,1)}) custom-call(bf16[4,256,2048]{2,1,0:T(8,128)(2,1)} %bitcast.331, bf16[2,2,64,2048]{3,2,1,0:T(8,128)(2,1)S(1)} %bitcast.307), custom_call_target="tpu_custom_call" | custom-call | bytes 150000000 | tf_op jit(solution)/shard_map/pallas_call | solution.py:227
  384.3 77.2 %shard_map.207 = (bf16[2,4,256,2048]{3,2,1,0:T(8,128)(2,1)}, bf16[2,2,2,2,2,64,2048]{6,5,4,3,2,1,0:T(8,128)(2,1)}) custom-call(bf16[256,2048]{1,0:T(8,128)(2,1)S(1)} %reshape.1046.refs_0_, bf16[2,2,64,2048]{3,2,1,0:T(8,128)(2,1)S(1)} %bitcast.308), custom_call_target="tpu_custom_call" | custom-call | bytes 150000000 | tf_op jit(solution)/shard_map/pallas_call | solution.py:227
  464.1 6.4 slice.207
  471.1 11.4 %fusion.61 = f32[1024,2048]{1,0:T(8,128)} fusion(bf16[1024,2048]{1,0:T(8,128)(2,1)S(1)} %bitcast.334, bf16[2048,2048]{1,0:T(8,128)(2,1)S(1)} %bitcast.385), kind=kOutput, calls=%fused_computation.190 | convolution fusion | flops 8589934592 | bytes 20971520 | tf_op jit(solution)/shard_map/dot_general | solution.py:267
  482.5 14.6 %fusion.60 = f32[1024,2048]{1,0:T(8,128)} fusion(bf16[1024,2048]{1,0:T(8,128)(2,1)} %bitcast.337, bf16[2048,2048]{1,0:T(8,128)(2,1)} %all-gather.2.cloned.1.call-done), kind=kOutput, calls=%fused_computation.189 | convolution fusion | flops 8589934592 | bytes 20971520 | tf_op jit(solution)/shard_map/dot_general | solution.py:268
  497.0 21.2 %multiply_convert_fusion = (bf16[1024,2048]{1,0:T(8,128)(2,1)}, bf16[1024,2048]{1,0:T(8,128)(2,1)S(1)}, bf16[1024,2048]{1,0:T(8,128)(2,1)}) fusion(f32[1024,2048]{1,0:T(8,128)} %fusion.61, f32[1024,2048]{1,0:T(8,128)} %fusion.60, bf16[1024,2048]{1,0:T(8,128)(2,1)} %bitcast.335, bf16[2048,2048]{1,0:T(8,128)(2,1)} %bitcast.386), kind=kOutput, calls=%fused_computation.10 | convolution fusion | flops 8623489024 | bytes 41943040 | tf_op jit(solution)/shard_map/dot_general | solution.py:267
  518.3 14.8 %fusion.62 = f32[1024,2048]{1,0:T(8,128)} fusion(bf16[1024,2048]{1,0:T(8,128)(2,1)S(1)} %get-tuple-element.156.refs_0_, bf16[2048,2048]{1,0:T(8,128)(2,1)} %bitcast.382), kind=kOutput, calls=%fused_computation.191 | convolution fusion | flops 8589934592 | bytes 20971520 | tf_op jit(solution)/shard_map/dot_general | solution.py:268
  533.1 10.7 shard_map.208
  543.7 14.5 %add_convert_fusion = bf16[1024,2048]{1,0:T(8,128)(2,1)} fusion(f32[1024,2048]{1,0:T(8,128)} %fusion.62, bf16[1024,2048]{1,0:T(8,128)(2,1)S(1)} %copy-done.40, bf16[2048,2048]{1,0:T(8,128)(2,1)} %bitcast.387), kind=kOutput, calls=%fused_computation.11 | convolution fusion | flops 8594128896 | bytes 25165824 | tf_op jit(solution)/shard_map/dot_general | solution.py:268
  558.3 12.7 %bitcast_convert_fusion.2 = bf16[1024,2048]{1,0:T(8,128)(2,1)S(1)} fusion(bf16[2,1024,1024]{2,1,0:T(8,128)(2,1)} %get-tuple-element.113, bf16[2,1024,2048]{2,1,0:T(8,128)(2,1)} %bitcast.349), kind=kOutput, calls=%fused_computation.8 | convolution fusion | flops 8592031744 | bytes 16777216 | tf_op jit(solution)/shard_map/dot_general | solution.py:268
  574.0 12.9 %bitcast_convert_fusion = bf16[2048,1024]{1,0:T(8,128)(2,1)} fusion(bf16[2,1024,2048]{2,1,0:T(8,128)(2,1)} %bitcast.350, bf16[2,1024,1024]{2,1,0:T(8,128)(2,1)S(1)} %copy-done.96), kind=kOutput, calls=%fused_computation.6 | convolution fusion | flops 8592031744 | bytes 16777216 | tf_op jit(solution)/shard_map/dot_general | solution.py:268
  587.0 49.0 %shard_map.209 = bf16[4,256,2048]{2,1,0:T(8,128)(2,1)S(1)} custom-call(bf16[4,256,2048]{2,1,0:T(8,128)(2,1)} %bitcast.336), custom_call_target="tpu_custom_call" | custom-call | bytes 150000000 | tf_op jit(solution)/shard_map/pallas_call | solution.py:227
  636.0 12.7 %bitcast_convert_fusion.1 = bf16[2048,1024]{1,0:T(8,128)(2,1)} fusion(bf16[2,1024,2048]{2,1,0:T(8,128)(2,1)} %bitcast.351, bf16[2,1024,1024]{2,1,0:T(8,128)(2,1)S(1)} %get-tuple-element.117), kind=kOutput, calls=%fused_computation.7 | convolution fusion | flops 8592031744 | bytes 16777216 | tf_op jit(solution)/shard_map/dot_general | solution.py:268
  674.8 12.6 %convolution_convert_fusion = bf16[1024,2048]{1,0:T(8,128)(2,1)} fusion(bf16[1024,2048]{1,0:T(8,128)(2,1)S(1)} %copy-done.39, bf16[2048,2048]{1,0:T(8,128)(2,1)} %all-gather.2.cloned.1.call-done), kind=kOutput, calls=%fused_computation.25 | convolution fusion | flops 8592031744 | bytes 16777216 | tf_op jit(solution)/shard_map/dot_general | solution.py:267
  687.4 61.0 %shard_map.210 = (bf16[2,4,256,2048]{3,2,1,0:T(8,128)(2,1)}, bf16[2,1024,256]{2,1,0:T(8,128)(2,1)S(1)}) custom-call(bf16[256,2048]{1,0:T(8,128)(2,1)S(1)} %fusion.16.refs_0_, bf16[1024,512]{1,0:T(8,128)(2,1)S(1)} %bitcast.301), custom_call_target="tpu_custom_call" | custom-call | bytes 150000000 | tf_op jit(solution)/shard_map/pallas_call | solution.py:227
  760.5 5.5 fusion.1
  766.0 4.8 bitcast_convert_fusion.4
  770.9 4.8 fusion.3
  791.6 4.8 multiply_bitcast_fusion
  801.4 92.5 %shard_map.211 = (bf16[2,1024,512]{2,1,0:T(8,128)(2,1)S(1)}, bf16[4,256,2048]{2,1,0:T(8,128)(2,1)}) custom-call(bf16[2,1024,512]{2,1,0:T(8,128)(2,1)S(1)} %bitcast.298, bf16[4,256,2048]{2,1,0:T(8,128)(2,1)} %bitcast.332), custom_call_target="tpu_custom_call" | custom-call | bytes 150000000 | tf_op jit(solution)/shard_map/pallas_call | solution.py:227
  903.6 6.3 convolution_convert_fusion.2
  910.0 5.0 bitcast_convert_fusion.3
  920.7 73.6 %shard_map.212 = bf16[4,256,2048]{2,1,0:T(8,128)(2,1)S(1)} custom-call(bf16[4,256,2048]{2,1,0:T(8,128)(2,1)} %bitcast.333), custom_call_target="tpu_custom_call" | custom-call | bytes 150000000 | tf_op jit(solution)/shard_map/pallas_call | solution.py:227
  1017.1 5.7 subtract_convert_fusion
  1022.7 30.4 %shard_map.213 = (bf16[8,64,1024]{2,1,0:T(8,128)(2,1)S(1)}, bf16[8,64,1024]{2,1,0:T(8,128)(2,1)S(1)}) custom-call(bf16[8,64,1024]{2,1,0:T(8,128)(2,1)S(1)} %bitcast.299, bf16[8,64,1024]{2,1,0:T(8,128)(2,1)S(1)} %bitcast.302), custom_call_target="tpu_custom_call" | custom-call | bytes 150000000 | tf_op jit(solution)/shard_map/pallas_call | solution.py:227
  1056.2 9.3 shard_map.214
  (387 shorter events, 215.0 us)
Async XLA Ops:
  7.2 475.3 %all-gather.2.cloned.1.call-start = ((), (), s32[]{:S(2)}) async-start(), calls=%async_computation | async-start | bytes 9437184 | tf_op jit(solution)/shard_map/all_gather | solution.py:346
  7.9 107.7 %collective-permute-start = (bf16[64,2048]{1,0:T(8,128)(2,1)}, bf16[64,2048]{1,0:T(8,128)(2,1)S(1)}, u32[]{:S(2)}, u32[]{:S(2)}) collective-permute-start(bf16[64,2048]{1,0:T(8,128)(2,1)} %param.24), channel_id=1, source_target_pairs={{0,0},{1,16},{2,2},{3,18},{4,1},{5,17},{6,3},{7,19},{8,4},{9,20},{... | collective-permute-start | bytes 786440 | tf_op jit(solution)/shard_map/ppermute | solution.py:364
  15.4 7.5 copy-start.70
  284.7 6.0 copy-start.81
  461.4 9.6 slice-start.4
  464.1 7.0 copy-start.46
  464.1 7.0 slice-start.5
  518.3 14.8 %copy-start.41 = (bf16[1024,2048]{1,0:T(8,128)(2,1)}, bf16[1024,2048]{1,0:T(8,128)(2,1)S(1)}, u32[]{:S(2)}) copy-start(bf16[1024,2048]{1,0:T(8,128)(2,1)S(1)} %get-tuple-element.156.refs_0_) | copy-start | bytes 12582916
  533.1 10.7 copy-start.40
  572.5 76.1 %collective-permute-start.1 = (bf16[512,2048]{1,0:T(8,128)(2,1)}, bf16[512,2048]{1,0:T(8,128)(2,1)S(1)}, u32[]{:S(2)}, u32[]{:S(2)}) collective-permute-start(bf16[512,2048]{1,0:T(8,128)(2,1)} %constant_dynamic-slice_fusion.10), channel_id=1, source_target_pairs={{0,2},{2,0},{1,3},{3,1},{4,6},{6,4},{5,7},{7,5},{8,10},{10,8},{9,1... | collective-permute-start | bytes 6291464 | tf_op jit(solution)/shard_map/ppermute | solution.py:256
  671.6 76.8 %collective-permute-start.3 = (bf16[256,2048]{1,0:T(8,128)(2,1)S(1)}, bf16[256,2048]{1,0:T(8,128)(2,1)S(1)}, u32[]{:S(2)}, u32[]{:S(2)}) collective-permute-start(bf16[256,2048]{1,0:T(8,128)(2,1)S(1)} %constant_dynamic-slice_fusion.8), channel_id=1, source_target_pairs={{0,16},{16,0},{1,17},{17,1},{2,18},{18,2},{3,19},{19,3},{4,20},{20... | collective-permute-start | bytes 3145736 | tf_op jit(solution)/shard_map/ppermute | solution.py:256
  673.8 13.6 %copy-start.3 = (bf16[128,8,2,256]{3,1,2,0:T(8,128)(2,1)S(1)}, bf16[128,8,2,256]{3,1,2,0:T(8,128)(2,1)}, u32[]{:S(2)}) copy-start(bf16[128,8,2,256]{3,1,2,0:T(8,128)(2,1)} %copy-done.2) | copy-start | bytes 3145732
  673.8 76.3 %collective-permute-start.2 = (bf16[1024,1024]{1,0:T(8,128)(2,1)S(1)}, bf16[1024,1024]{1,0:T(8,128)(2,1)S(1)}, u32[]{:S(2)}, u32[]{:S(2)}) collective-permute-start(bf16[1024,1024]{1,0:T(8,128)(2,1)S(1)} %constant_dynamic-slice_fusion.9), channel_id=1, source_target_pairs={{0,2},{2,0},{1,3},{3,1},{4,6},{6,4},{5,7},{7,5},{8,10},{10,8},{9,1... | collective-permute-start | bytes 6291464 | tf_op jit(solution)/shard_map/ppermute | solution.py:256
  766.0 12.0 %slice-start = ((s8[8388608]{0:T(1024)(128)(4,1)}), s8[4194304]{0:T(1024)(128)(4,1)S(1)}, s32[]{:S(2)}) async-start(s8[8388608]{0:T(1024)(128)(4,1)} %bitcast.314), calls=%async_computation.1 | async-start | bytes 8388608
  770.9 7.2 slice-start.1
  782.9 6.1 copy-start.54
  782.9 114.0 %collective-permute-start.4 = (bf16[1024,1024]{1,0:T(8,128)(2,1)}, bf16[1024,1024]{1,0:T(8,128)(2,1)}, u32[]{:S(2)}, u32[]{:S(2)}) collective-permute-start(bf16[1024,1024]{1,0:T(8,128)(2,1)} %constant_dynamic-slice_fusion.7), channel_id=1, source_target_pairs={{0,2},{2,0},{1,3},{3,1},{4,6},{6,4},{5,7},{7,5},{8,10},{10,8},{9,1... | collective-permute-start | bytes 6291464 | tf_op jit(solution)/shard_map/ppermute | solution.py:256
  785.2 6.4 copy-start.31
  787.6 107.7 %collective-permute-start.6 = (bf16[512,1024]{1,0:T(8,128)(2,1)}, bf16[512,1024]{1,0:T(8,128)(2,1)}, u32[]{:S(2)}, u32[]{:S(2)}) collective-permute-start(bf16[512,1024]{1,0:T(8,128)(2,1)} %constant_dynamic-slice_fusion.5), channel_id=1, source_target_pairs={{0,16},{16,0},{1,17},{17,1},{2,18},{18,2},{3,19},{19,3},{4,20},{20... | collective-permute-start | bytes 3145736 | tf_op jit(solution)/shard_map/ppermute | solution.py:256
  789.8 104.1 %collective-permute-start.5 = (bf16[128,2048]{1,0:T(8,128)(2,1)}, bf16[128,2048]{1,0:T(8,128)(2,1)}, u32[]{:S(2)}, u32[]{:S(2)}) collective-permute-start(bf16[128,2048]{1,0:T(8,128)(2,1)} %constant_dynamic-slice_fusion.6), channel_id=1, source_target_pairs={{0,2},{2,0},{1,3},{3,1},{4,6},{6,4},{5,7},{7,5},{8,10},{10,8},{9,1... | collective-permute-start | bytes 1572872 | tf_op jit(solution)/shard_map/ppermute | solution.py:256
  801.4 92.5 %copy-start.55 = (bf16[256,2048]{1,0:T(8,128)(2,1)S(1)}, bf16[256,2048]{1,0:T(8,128)(2,1)}, u32[]{:S(2)}) copy-start(bf16[256,2048]{1,0:T(8,128)(2,1)} %fusion.8) | copy-start | bytes 3145732
  801.4 93.9 %copy-start.32 = (bf16[1024,1024]{1,0:T(8,128)(2,1)S(1)}, bf16[1024,1024]{1,0:T(8,128)(2,1)}, u32[]{:S(2)}) copy-start(bf16[1024,1024]{1,0:T(8,128)(2,1)} %add_convert_fusion.2) | copy-start | bytes 6291460
  901.0 9.0 slice-start.2
  901.6 8.4 collective-permute-start.7
  903.6 6.3 slice-start.3
  915.1 79.2 %collective-permute-start.10 = (bf16[64,2048]{1,0:T(8,128)(2,1)S(1)}, bf16[64,2048]{1,0:T(8,128)(2,1)S(1)}, u32[]{:S(2)}, u32[]{:S(2)}) collective-permute-start(bf16[64,2048]{1,0:T(8,128)(2,1)S(1)} %constant_dynamic-slice_fusion.1), channel_id=1, source_target_pairs={{0,16},{16,0},{1,17},{17,1},{2,18},{18,2},{3,19},{19,3},{4,20},{20... | collective-permute-start | bytes 786440 | tf_op jit(solution)/shard_map/ppermute | solution.py:256
  915.8 79.3 %collective-permute-start.9 = (bf16[512,1024]{1,0:T(8,128)(2,1)S(1)}, bf16[512,1024]{1,0:T(8,128)(2,1)S(1)}, u32[]{:S(2)}, u32[]{:S(2)}) collective-permute-start(bf16[512,1024]{1,0:T(8,128)(2,1)S(1)} %constant_dynamic-slice_fusion.2), channel_id=1, source_target_pairs={{0,16},{16,0},{1,17},{17,1},{2,18},{18,2},{3,19},{19,3},{4,20},{20... | collective-permute-start | bytes 3145736 | tf_op jit(solution)/shard_map/ppermute | solution.py:256
  918.3 77.2 %collective-permute-start.8 = (bf16[1024,512]{1,0:T(8,128)(2,1)S(1)}, bf16[1024,512]{1,0:T(8,128)(2,1)S(1)}, u32[]{:S(2)}, u32[]{:S(2)}) collective-permute-start(bf16[1024,512]{1,0:T(8,128)(2,1)S(1)} %constant_dynamic-slice_fusion.3), channel_id=1, source_target_pairs={{0,2},{2,0},{1,3},{3,1},{4,6},{6,4},{5,7},{7,5},{8,10},{10,8},{9,1... | collective-permute-start | bytes 3145736 | tf_op jit(solution)/shard_map/ppermute | solution.py:256
  997.6 57.3 %collective-permute-start.11 = (bf16[512,512]{1,0:T(8,128)(2,1)}, bf16[512,512]{1,0:T(8,128)(2,1)}, u32[]{:S(2)}, u32[]{:S(2)}) collective-permute-start(bf16[512,512]{1,0:T(8,128)(2,1)} %constant_dynamic-slice_fusion), channel_id=1, source_target_pairs={{0,16},{16,0},{1,17},{17,1},{2,18},{18,2},{3,19},{19,3},{4,20},{20... | collective-permute-start | bytes 1572872 | tf_op jit(solution)/shard_map/ppermute | solution.py:256
  1015.4 38.7 %collective-permute-start.12 = (bf16[64,2048]{1,0:T(8,128)(2,1)}, bf16[64,2048]{1,0:T(8,128)(2,1)S(1)}, u32[]{:S(2)}, u32[]{:S(2)}) collective-permute-start(bf16[64,2048]{1,0:T(8,128)(2,1)} %add_convert_fusion.10), channel_id=1, source_target_pairs={{0,0},{16,1},{2,2},{18,3},{1,4},{17,5},{3,6},{19,7},{4,8},{20,9},{... | collective-permute-start | bytes 786440 | tf_op jit(solution)/shard_map/ppermute | solution.py:516
  1022.7 32.2 %copy-start.52 = (bf16[1024,512]{1,0:T(8,128)(2,1)S(1)}, bf16[1024,512]{1,0:T(8,128)(2,1)}, u32[]{:S(2)}) copy-start(bf16[1024,512]{1,0:T(8,128)(2,1)} %copy-done.51) | copy-start | bytes 3145732
  1054.9 12.2 %copy-start.5 = (bf16[8,64,1024]{2,1,0:T(8,128)(2,1)S(1)}, bf16[8,64,1024]{2,1,0:T(8,128)(2,1)}, u32[]{:S(2)}) copy-start(bf16[8,64,1024]{2,1,0:T(8,128)(2,1)} %copy-done.4) | copy-start | bytes 3145732
  (85 other events, 241.9 us)
Sparse Core Ops, SparseCore 0:
  9.9 94.5 all-gather.1

commit v3 on v2

v3 whole, which is shorter than its diff:
```python
import itertools
import math

import jax
import jax.numpy as jnp
from jax import lax
from jax.experimental import pallas as pl
from jax.experimental.pallas import tpu as pltpu
from jax.sharding import Mesh
from jax.sharding import PartitionSpec as P

HEAD = 256
VMEM_LIMIT = 48 << 20
FFN_VMEM_LIMIT = 62 << 20
BLK = 128
EPS = 1e-06
ROPE_BASE = 1000042.0
AXES = ("zh", "zl", "y", "x", "c")
TEAM = ("zl", "y")
SLOTS = ("y", "zl")
PAIRED_SLOTS = ("c", "y", "zl")
SHARES = ("c", "x", "zh")
OWNERS = ("zl", "y", "c")
ROWS_T = (((0,), (0,)), ((), ()))
PAIR_ROWS_T = (((0, 1), (0, 1)), ((), ()))
COLS_T = (((1,), (1,)), ((), ()))
F32 = jnp.float32
BF16 = jnp.bfloat16


def offsets(sizes, axes):
    return [dict(zip(axes, o)) for o in itertools.product(*(range(sizes[a]) for a in axes))]


def place(at, layout, sizes):
    index = 0
    for a in layout:
        index = index * sizes[a] + at[a]
    return index


class Gather:
    def __init__(self, x, layout, orders, rank=1):
        self.x, self.layout, self.orders, self.rank = x, layout, orders, rank

    def shape(self, sizes):
        return (math.prod(sizes[a] for a in self.layout),) + self.x.shape

    def cut(self, ref, part):
        rows = self.x.shape[0] // len(self.orders)
        return ref.at[pl.ds(part * rows, rows)]

    def spot(self, out, owner, off, part, sizes):
        return self.cut(out.at[place(owner, self.layout, sizes)], part)


class NearGather(Gather):
    def shape(self, sizes):
        return tuple(sizes[a] for a in self.layout) + self.x.shape

    def spot(self, out, owner, off, part, sizes):
        return self.cut(out.at[tuple(off[a] for a in self.layout)], part)


class RowGather(Gather):
    def shape(self, sizes):
        team, rows, columns = self.x.shape
        return (sizes["x"] * sizes["zh"] * team * sizes["c"] * rows, columns)

    def cut(self, ref, part):
        return ref.at[part]

    def spot(self, out, owner, off, part, sizes):
        team, rows, _ = self.x.shape
        block = place(owner, ("x", "zh"), sizes) * team + part
        start = pl.multiple_of((block * sizes["c"] + owner["c"]) * rows, rows)
        return out.at[pl.ds(start, rows)]


class Swap:
    def __init__(self, x, layout):
        self.x, self.layout = x, layout

    def shape(self, sizes):
        return self.x.shape

    def own_shape(self):
        return self.x.shape[1:]

    def offsets(self, sizes):
        return offsets(sizes, self.layout)

    def pair(self, x, out, here, to, off, sizes):
        return x.at[place(to, self.layout, sizes)], out.at[place(here, self.layout, sizes)]


class NearSwap(Swap):
    def pair(self, x, out, here, to, off, sizes):
        i = off[self.layout[0]]
        return x.at[i], out.at[i]


class Halves:
    def __init__(self, x):
        self.x = x

    def shape(self, sizes):
        rows, columns = self.x.shape
        return (2, rows, columns // 2)

    def own_shape(self):
        rows, columns = self.x.shape
        return (rows, columns // 2)

    def offsets(self, sizes):
        return offsets(sizes, ("c",))

    def pair(self, x, out, here, to, off, sizes):
        width = self.x.shape[1] // 2
        start = pl.multiple_of(to["c"] * width, width)
        return x.at[:, pl.ds(start, width)], out.at[off["c"]]


CHUNKS = 4


class TeamSum:
    def __init__(self, x, y_first=2):
        self.x, self.y_first = x, y_first

    def shape(self, sizes):
        return (2,) + self.x.shape[2:]


class Net:
    def __init__(self, sizes):
        self.sizes, self.count, self.reached = sizes, 0, set()

    def wire(self, off):
        self.reached.add(tuple(off.get(a, 0) for a in AXES))
        self.count += 1
        return self.count - 1, off

    def open(self, send_sem, recv_sem):
        self.send_sem, self.recv_sem = send_sem, recv_sem
        self.here = {a: lax.axis_index(a) for a in AXES}
        self.sent = []
        barrier = pltpu.get_barrier_semaphore()
        for off in sorted(self.reached):
            pl.semaphore_signal(
                barrier,
                inc=1,
                device_id=self.device(self.moved(dict(zip(AXES, off)))),
                device_id_type=pl.DeviceIdType.MESH,
            )
        pl.semaphore_wait(barrier, len(self.reached))

    def moved(self, off):
        return {
            a: lax.rem(self.here[a] + off[a], self.sizes[a]) if off.get(a, 0) else self.here[a]
            for a in AXES
        }

    def device(self, at):
        return tuple(at[a] for a in AXES)

    def send(self, src, dst, wire):
        sem, off = wire
        cp = pltpu.make_async_remote_copy(
            src_ref=src,
            dst_ref=dst,
            send_sem=self.send_sem.at[sem],
            recv_sem=self.recv_sem.at[sem],
            device_id=self.device(self.moved(off)),
            device_id_type=pl.DeviceIdType.MESH,
        )
        cp.start()
        self.sent.append(cp)
        return cp

    def settle(self, cp):
        cp.wait_send()
        self.sent = [other for other in self.sent if other is not cp]

    def close(self):
        for cp in self.sent:
            cp.wait_send()


class Relay:
    def __init__(self, job, number, net):
        self.job, self.net, self.sizes = job, net, net.sizes
        self.steps = []
        for part, order in enumerate(job.orders):
            for off in offsets(self.sizes, order):
                used = [i for i, a in enumerate(order) if off[a]]
                sends = [
                    net.wire({a: d})
                    for a in order[used[-1] + 1 if used else 0 :]
                    for d in range(1, self.sizes[a])
                ]
                hops = len(used)
                key = (job.rank, part + 2 * hops, hops, number, part)
                self.steps.append((key, self, hops, part, off, sends))

    def open(self, x, out):
        self.x, self.out, self.arrivals = x, out, {}

    def run(self, hops, part, off, sends):
        job, net = self.job, self.net
        owner = net.moved(off)
        if hops:
            self.arrivals[part, tuple(sorted(off.items()))].wait_recv()
            source = job.spot(self.out, owner, off, part, self.sizes)
        else:
            source = job.cut(self.x, part)
        for wire in sends:
            ((a, d),) = wire[1].items()
            there = dict(off)
            there[a] = (-d) % self.sizes[a]
            dst = job.spot(self.out, owner, there, part, self.sizes)
            self.arrivals[part, tuple(sorted(there.items()))] = net.send(source, dst, wire)

    def own(self, part):
        return self.job.spot(self.out, self.net.here, {a: 0 for a in AXES}, part, self.sizes)


class Adder:
    def __init__(self, job, number, net):
        self.job, self.net = job, net
        rows = job.x.shape[2] // CHUNKS
        self.steps = []
        self.parts = []
        for part in range(CHUNKS):
            first, second = ("y", "zl") if part < job.y_first else ("zl", "y")
            wires = net.wire({first: 1}), net.wire({first: 1}), net.wire({second: 1})
            self.parts.append((pl.ds(part * rows, rows), first, second, wires))
            self.steps.append(((0, part, 0, number, part), self, 0, part, None, None))
            self.steps.append(((1, part + 2, 1, number, part), self, 1, part, None, None))

    def scratch(self):
        shape = self.job.x.shape[2:]
        return [pltpu.VMEM(shape, self.job.x.dtype)] * 2 + [pltpu.SemaphoreType.DMA((CHUNKS,))]

    def open(self, x, out, term, far, sem):
        self.x, self.out, self.term, self.far, self.sem = x, out, term, far, sem
        self.waits, self.direct, self.summed = {}, [], []

    def run(self, hops, part, *_):
        window, first, second, wires = self.parts[part]
        y_first = first == "y"
        if not hops:
            self.waits[part] = self.net.send(
                self.x.at[1, 1, window], self.far.at[window], wires[0]
            )
            near = self.x.at[1, 0, window] if y_first else self.x.at[0, 1, window]
            self.direct.append(
                self.net.send(near, self.out.at[0 if y_first else 1, window], wires[1])
            )
            mine = self.x.at[0, 1, window] if y_first else self.x.at[1, 0, window]
            load = pltpu.make_async_copy(mine, self.term.at[window], self.sem.at[part])
            load.start()
            self.waits[part] = self.waits[part], load
            return
        far, load = self.waits[part]
        load.wait()
        far.wait_recv()
        total = self.term[window].astype(F32) + self.far[window].astype(F32)
        self.term[window] = total.astype(self.term.dtype)
        self.summed.append(
            self.net.send(
                self.term.at[window], self.out.at[1 if y_first else 0, window], wires[2]
            )
        )

    def finish(self):
        for cp in self.direct + self.summed:
            cp.wait_recv()


def exchange(jobs, collective_id, micros=50):
    net = Net({a: lax.axis_size(a) for a in AXES})
    sizes = net.sizes
    count = len(jobs)
    steps, swaps, runners, scratch = [], [], [], []
    for number, job in enumerate(jobs):
        if isinstance(job, Gather):
            runner = Relay(job, number, net)
            steps += runner.steps
            stage = [pltpu.VMEM(job.x.shape, job.x.dtype)]
        elif isinstance(job, TeamSum):
            runner = Adder(job, number, net)
            steps += runner.steps
            stage = runner.scratch()
        else:
            runner = None
            swaps += [(number, off, net.wire(off)) for off in job.offsets(sizes) if any(off.values())]
            stage = [pltpu.VMEM(job.own_shape(), job.x.dtype)]
        runners.append((runner, len(scratch), len(scratch) + len(stage)))
        scratch += stage
    steps.sort(key=lambda s: s[0])

    def kernel(*refs):
        ins, outs, rest = refs[:count], refs[count : 2 * count], refs[2 * count :]
        send_sem, recv_sem, local_sem = rest[-3:]
        net.open(send_sem, recv_sem)
        loads, stores = [], []
        for number, job in enumerate(jobs):
            runner, lo, hi = runners[number]
            if isinstance(job, TeamSum):
                runner.open(ins[number], outs[number], *rest[lo:hi])
                continue
            (stage,) = rest[lo:hi]
            if runner:
                runner.open(ins[number], outs[number])
                src = ins[number]
                puts = [
                    (job.cut(stage, part), runner.own(part)) for part in range(len(job.orders))
                ]
            else:
                none = {a: 0 for a in AXES}
                src, dst = job.pair(ins[number], outs[number], net.here, net.here, none, sizes)
                puts = [(stage, dst)]
            load = pltpu.make_async_copy(src, stage, local_sem.at[number, 0])
            load.start()
            loads.append((load, number, puts))
        for _, runner, hops, *what in steps:
            if not hops:
                runner.run(hops, *what)
        received = []
        for number, off, wire in swaps:
            to = net.moved(off)
            src, dst = jobs[number].pair(ins[number], outs[number], net.here, to, off, sizes)
            received.append(net.send(src, dst, wire))
        for load, number, puts in loads:
            load.wait()
            for i, (src, dst) in enumerate(puts):
                store = pltpu.make_async_copy(src, dst, local_sem.at[number, 1 + i])
                store.start()
                stores.append(store)
        for _, runner, hops, *what in steps:
            if hops:
                runner.run(hops, *what)
        for cp in received:
            cp.wait_recv()
        for runner, _, _ in runners:
            if isinstance(runner, Adder):
                runner.finish()
        net.close()
        for store in stores:
            store.wait()

    return pl.pallas_call(
        kernel,
        out_shape=[jax.ShapeDtypeStruct(job.shape(sizes), job.x.dtype) for job in jobs],
        in_specs=[pl.BlockSpec(memory_space=pl.ANY)] * count,
        out_specs=[pl.BlockSpec(memory_space=pl.ANY)] * count,
        scratch_shapes=scratch
        + [
            pltpu.SemaphoreType.DMA((net.count,)),
            pltpu.SemaphoreType.DMA((net.count,)),
            pltpu.SemaphoreType.DMA((count, 1 + CHUNKS)),
        ],
        cost_estimate=pl.CostEstimate(
            flops=0, bytes_accessed=micros * 3_000_000, transcendentals=0
        ),
        compiler_params=pltpu.CompilerParams(
            collective_id=collective_id, has_side_effects=True, vmem_limit_bytes=VMEM_LIMIT
        ),
    )(*[job.x for job in jobs])


def sum_over(term, axis):
    size = lax.axis_size(axis)
    me = lax.axis_index(axis)
    while size > 1:
        size //= 2
        rows = term.shape[0] // 2
        pairs = [(i, i ^ size) for i in range(lax.axis_size(axis))]
        side = (me // size) % 2
        kept = lax.dynamic_slice_in_dim(term, side * rows, rows)
        other = lax.ppermute(
            lax.dynamic_slice_in_dim(term, (1 - side) * rows, rows), axis, pairs
        )
        term = kept.astype(F32) + other.astype(F32)
        if size > 1:
            term = term.astype(BF16)
    return term


def dot(a, b, dims=None):
    if dims is None:
        return jnp.dot(a, b, preferred_element_type=F32)
    return lax.dot_general(a, b, dims, preferred_element_type=F32)


def rotate(t, cos, sin):
    half = t.shape[-1] // 2
    front, back = t[..., :half], t[..., half:]
    return jnp.concatenate([front * cos - back * sin, back * cos + front * sin], axis=-1)


def rms_scale(values):
    return lax.rsqrt(jnp.mean(values * values, axis=-1, keepdims=True) + EPS)


def positions(members):
    total = lax.axis_size("zh") * lax.axis_size("zl")
    half = jnp.arange(2)[None, :, None]
    row = jnp.arange(BLK)[None, None, :]
    j = members[:, None, None]
    return (jnp.where(half == 0, j, 2 * total - 1 - j) * BLK + row).reshape(-1)


OUTWARD = ("zh", "x", "c")
TILE = 512
TO_TEAM = [("zl", "y", "c")] * CHUNKS
TO_TEAM_EVEN = [("zl", "y", "c"), ("y", "zl", "c")] * (CHUNKS // 2)


def feed_forward(norm, gd, w_gate, w_down, up_part, collective_id):
    net = Net({a: lax.axis_size(a) for a in AXES})
    sizes = net.sizes
    own, width = norm.shape
    ff = w_gate.shape[1]
    half = ff // 2
    norm_job = NearGather(norm, PAIRED_SLOTS, TO_TEAM_EVEN)
    up_job = RowGather(up_part, None, [OUTWARD] * up_part.shape[0])
    norms, ups = Relay(norm_job, 0, net), Relay(up_job, 1, net)
    steps = sorted(norms.steps + ups.steps, key=lambda s: s[0])
    y_rows, zl_rows = pl.ds(0, own // 2), pl.ds(own // 2, own // 2)
    far_wires = net.wire({"y": 1}), net.wire({"zl": 1})
    near_wires = net.wire({"y": 1}), net.wire({"zl": 1})
    half_wires = [[net.wire({"c": 1}) for _ in range(3)] for _ in range(4)]
    n_local = 64

    def kernel(
        norm_ref, gd_ref, w_gate_ref, w_down_ref, up_ref,
        norms_ref, gate_half, up_half, mixed_half, gn2_ref, out_ref,
        wg, wu, wd, nv, gdv, gate, gm, gg, gu, mx, far, send_sem, recv_sem, local_sem,
    ):
        net.open(send_sem, recv_sem)
        norms.open(norm_ref, norms_ref)
        ups.open(up_ref, wu)
        used = iter(range(n_local))

        def local(src, dst):
            cp = pltpu.make_async_copy(src, dst, local_sem.at[next(used)])
            cp.start()
            return cp

        got_norm = local(norm_ref, nv.at[0])
        for _, runner, hops, *what in steps:
            if not hops:
                runner.run(hops, *what)
        got_gate = local(w_gate_ref, wg)
        got_gd = [local(gd_ref.at[0, 0, 0], gdv.at[0]), local(gd_ref.at[0, 1, 0], gdv.at[1])]
        got_down = local(w_down_ref, wd)
        got_up = [local(ups.job.cut(up_ref, p), ups.own(p)) for p in range(len(up_job.orders))]
        got_norm.wait()
        kept_norm = [local(norm_job.cut(nv.at[0], p), norms.own(p)) for p in range(CHUNKS)]

        def tiles(n, body):
            def step(t, _):
                body(pl.ds(pl.multiple_of(t * TILE, TILE), TILE))
                return 0

            lax.fori_loop(0, n // TILE, step, 0)

        gd_turn = [(0, 0), (1, 0), (0, 1), (1, 1)]

        def begin(turn):
            i, j = gd_turn[turn]
            r = 2 * i + j

            def one(t):
                gate[r, :, t] = dot(nv[r], wg[:, t])

            tiles(ff, one)
            got_gd[turn].wait()

            def two(t):
                gm[r, :, t] = dot(gdv[turn % 2], wd[t, :], COLS_T)

            tiles(ff, two)
            if turn + 2 < 4:
                got_gd.append(local(gd_ref.at[(0, *gd_turn[turn + 2])], gdv.at[turn % 2]))

        got_gate.wait()
        got_down.wait()
        begin(0)
        late = []
        arrived = {(1, 0): 0, (0, 1): 0, (1, 1): 0}
        turn = 1
        for _, runner, hops, part, off, sends in steps:
            if not hops:
                continue
            if runner is norms and off["c"]:
                late.append((hops, part, off, sends))
                continue
            runner.run(hops, part, off, sends)
            if runner is norms:
                arrived[off["y"], off["zl"]] += 1
                while turn < 4 and arrived[gd_turn[turn]] == CHUNKS:
                    i, j = gd_turn[turn]
                    local(norms_ref.at[0, i, j], nv.at[2 * i + j]).wait()
                    begin(turn)
                    turn += 1
        for cp in got_up + kept_norm:
            cp.wait()

        halves, busy = [], {}

        def finish(r, buf):
            for cp, remote in busy.pop(buf, []):
                net.settle(cp) if remote else cp.wait()

            def one(t):
                up = dot(nv[r], wu[:, t])
                g, m = gate[r, :, t], gm[r, :, t]
                s = 1.0 / (1.0 + jnp.exp(-g))
                gs = g * s
                mx[r, :, t] = (gs * up).astype(BF16)
                gg[buf, :, t] = (m * up * s * (1.0 + g * (1.0 - s))).astype(BF16)
                gu[buf, :, t] = (m * gs).astype(BF16)

            tiles(ff, one)
            mine = pl.ds(pl.multiple_of(net.here["c"] * half, half), half)
            other = pl.ds(pl.multiple_of((1 - net.here["c"]) * half, half), half)
            rows = pl.ds(r * own, own)
            for n, (ref, out) in enumerate(
                ((gg.at[buf], gate_half), (gu.at[buf], up_half), (mx.at[r], mixed_half))
            ):
                cp = local(ref.at[:, mine], out.at[0, rows])
                sent = net.send(ref.at[:, other], out.at[1, rows], half_wires[r][n])
                halves.append(sent)
                busy.setdefault(buf if n < 2 else "mixed", []).extend([(cp, False), (sent, True)])

            def two(t):
                term = dot(gg[buf], wg[t, :], COLS_T) + dot(gu[buf], wu[t, :], COLS_T)
                nv[r, :, t] = term.astype(BF16)

            tiles(width, two)

        def add(r, window):
            nv[r, window] = (nv[r, window].astype(F32) + far[window].astype(F32)).astype(BF16)

        finish(3, 0)
        to_far = (
            net.send(nv.at[3, y_rows], far.at[y_rows], far_wires[0]),
            net.send(nv.at[3, zl_rows], far.at[zl_rows], far_wires[1]),
        )
        finish(2, 1)
        to_far[1].wait_recv()
        add(2, zl_rows)
        to_y = net.send(nv.at[2], gn2_ref.at[1], near_wires[0])
        finish(1, 0)
        to_far[0].wait_recv()
        add(1, y_rows)
        to_zl = net.send(nv.at[1], gn2_ref.at[2], near_wires[1])
        finish(0, 1)
        stored = [local(nv.at[0], gn2_ref.at[0])]
        for n, r in enumerate((3, 2, 1, 0)):
            buf = n % 2
            for cp, remote in busy.pop(buf, []):
                net.settle(cp) if remote else cp.wait()

            def down(t):
                gg[buf, :, t] = dot(mx[r], wd[:, t]).astype(BF16)

            tiles(width, down)
            busy[buf] = [(local(gg.at[buf], out_ref.at[r // 2, r % 2]), False)]
        for hops, part, off, sends in late:
            norms.run(hops, part, off, sends)
        to_y.wait_recv()
        to_zl.wait_recv()
        for cp in halves:
            cp.wait_recv()
        net.close()
        for cps in busy.values():
            for cp, remote in cps:
                if not remote:
                    cp.wait()
        for cp in stored:
            cp.wait()

    shape = jax.ShapeDtypeStruct
    weight = pltpu.VMEM((width, ff), BF16)
    return pl.pallas_call(
        kernel,
        out_shape=[
            shape((2, 2, 2, own, width), BF16),
            *[shape((2, 4 * own, half), BF16)] * 3,
            shape((3, own, width), BF16),
            shape((2, 2, own, width), BF16),
        ],
        in_specs=[pl.BlockSpec(memory_space=pl.ANY)] * 5,
        out_specs=[pl.BlockSpec(memory_space=pl.ANY)] * 6,
        scratch_shapes=[
            weight,
            weight,
            pltpu.VMEM((ff, width), BF16),
            pltpu.VMEM((4, own, width), BF16),
            pltpu.VMEM((2, own, width), BF16),
            pltpu.VMEM((4, own, ff), F32),
            pltpu.VMEM((4, own, ff), F32),
            pltpu.VMEM((2, own, ff), BF16),
            pltpu.VMEM((2, own, ff), BF16),
            pltpu.VMEM((4, own, ff), BF16),
            pltpu.VMEM((own, width), BF16),
            pltpu.SemaphoreType.DMA((net.count,)),
            pltpu.SemaphoreType.DMA((net.count,)),
            pltpu.SemaphoreType.DMA((n_local,)),
        ],
        cost_estimate=pl.CostEstimate(
            flops=0, bytes_accessed=130 * 3_000_000, transcendentals=0
        ),
        compiler_params=pltpu.CompilerParams(
            collective_id=collective_id, has_side_effects=True, vmem_limit_bytes=FFN_VMEM_LIMIT
        ),
    )(norm, gd, w_gate, w_down, up_part)


def on_device(
    inputs,
    lengths,
    attn_gain,
    query_weight,
    key_matrix,
    value_matrix,
    output_weight,
    ffn_gain,
    gate_weight,
    up_weight,
    down_weight,
    cotangent,
):
    size = {a: lax.axis_size(a) for a in AXES}
    at = {a: lax.axis_index(a) for a in AXES}
    width = inputs.shape[3]
    own = inputs.shape[1] * inputs.shape[2]
    rows = query_weight.shape[0]
    n_dev = width // rows
    team = size["y"] * size["zl"]
    q_cols = query_weight.shape[1] // team
    kv_cols = key_matrix.shape[1] // team
    ff_rows = down_weight.shape[0]
    ff = gate_weight.shape[1] // team
    heads = q_cols // HEAD
    n_tok = team * own
    scaling = HEAD**-0.5

    def by_team(w):
        return w.reshape(rows, team, -1).transpose(1, 0, 2)

    def ff_by_team(w):
        cut = w.reshape(rows, *(size[a] for a in AXES), ff_rows)
        return cut.transpose(2, 3, 0, 5, 4, 1, 6).reshape(team, rows, ff)

    attn_cut = jnp.concatenate(
        [by_team(query_weight), by_team(key_matrix), by_team(value_matrix)], axis=2
    )
    tile = jnp.zeros((8, 128), F32)
    tile = tile.at[0, :rows].set(attn_gain.astype(F32))
    tile = tile.at[0, 64 : 64 + rows].set(ffn_gain.astype(F32))
    tile = tile.at[1].set(lengths[0].astype(F32))
    tiles, attn_part, gate_part, up_part = exchange(
        [
            Gather(tile, AXES, [("c", "x", "y", "zl", "zh")], rank=0),
            Swap(attn_cut, TEAM),
            Swap(ff_by_team(gate_weight), TEAM),
            Swap(ff_by_team(up_weight), TEAM),
        ],
        1,
    )
    w_down = lax.all_gather(down_weight, SHARES, axis=0, tiled=True)
    gain_one = tiles[:, 0, :rows].reshape(1, width)
    gain_two = tiles[:, 0, 64 : 64 + rows].reshape(1, width)
    slots = tiles[: n_dev // (size["zh"] * size["zl"]), 1, 0].reshape(
        size["y"], size["x"], size["c"]
    )
    lens = slots[at["y"] ^ jnp.arange(2), at["x"], at["c"]].astype(jnp.int32)

    per_head = n_dev // team

    def head_home(i):
        f, t = i // per_head, i % per_head
        zl, y = f // size["y"], f % size["y"]
        zh, t = t % size["zh"], t // size["zh"]
        x, c = t % size["x"], t // size["x"]
        return (((zh * size["zl"] + zl) * size["y"] + y) * size["x"] + x) * size["c"] + c

    homes = [(i, head_home(i)) for i in range(n_dev)]
    out_part = lax.ppermute(output_weight, AXES, homes)

    def row_gather(part):
        return RowGather(part, None, [OUTWARD] * team)

    def spread(v):
        cut = v.reshape(own, size["zh"], size["zl"], size["y"], size["x"], size["c"] * rows)
        return cut.transpose(0, 4, 1, 2, 3, 5).reshape(own, width)

    def natural(v):
        cut = v.reshape(own, size["x"], size["zh"], size["zl"], size["y"], size["c"] * rows)
        return cut.transpose(0, 2, 3, 4, 1, 5).reshape(own, width)

    my_pos = positions((at["zh"] * size["zl"] + at["zl"])[None])
    valid = (my_pos < lengths[0]).astype(F32)[:, None]
    near_zl = at["zl"] ^ jnp.arange(2)
    near_zh = (at["zh"] + jnp.arange(size["zh"])) % size["zh"]
    q_pos = positions(at["zh"] * 2 + near_zl)
    k_pos = positions((near_zh[:, None] * 2 + near_zl[None, :]).reshape(-1))
    half = HEAD // 2
    freq = ROPE_BASE ** (-2.0 * jnp.arange(half).astype(F32) / HEAD)
    angles = q_pos.astype(F32)[:, None] * freq[None, :]
    cos = jnp.tile(jnp.cos(angles), (size["y"], 1))[:, None, :]
    sin = jnp.tile(jnp.sin(angles), (size["y"], 1))[:, None, :]

    tokens = inputs.reshape(own, width).astype(F32)
    scale_one = rms_scale(tokens)
    norm_one = (tokens * scale_one * gain_one).astype(BF16)
    norm_one_pair, w_attn, w_out = exchange(
        [
            NearGather(spread(norm_one), PAIRED_SLOTS, TO_TEAM),
            row_gather(attn_part),
            Gather(out_part, SHARES, [OUTWARD] * (rows // 16)),
        ],
        2,
    )
    norm_one_pair = norm_one_pair.reshape(2, n_tok, width)
    w_attn = w_attn.reshape(width, -1)
    w_out = w_out.reshape(q_cols, width)
    qkv = dot(norm_one_pair[0], w_attn)
    q = rotate(qkv[:, :q_cols].reshape(n_tok, heads, HEAD), cos, sin).astype(BF16)
    k = rotate(qkv[:, q_cols : q_cols + kv_cols].reshape(n_tok, 1, HEAD), cos, sin).astype(BF16)
    v = qkv[:, q_cols + kv_cols :].astype(BF16)
    kv = jnp.concatenate([k.reshape(n_tok, kv_cols), v], axis=1)
    gy = valid * cotangent.reshape(own, width).astype(F32)
    kv_all, gd_pair = exchange(
        [
            NearGather(kv, ("zh",), [("zh",)]),
            NearGather(gy.astype(BF16), PAIRED_SLOTS, TO_TEAM_EVEN),
        ],
        3,
    )
    n_slot = size["y"]
    n_q = n_tok // n_slot
    q = q.reshape(n_slot, n_q, heads, HEAD)
    kv_all = kv_all.reshape(size["zh"], n_slot, n_q, 2 * kv_cols).transpose(1, 0, 2, 3)
    kv_all = kv_all.reshape(n_slot, size["zh"] * n_q, 2 * kv_cols)
    k_all, v_all = kv_all[:, :, :kv_cols], kv_all[:, :, kv_cols:]
    allowed = (k_pos[None, None, :] <= q_pos[None, :, None]) & (
        k_pos[None, None, :] < lens[:, None, None]
    )
    scores = jnp.einsum("bqgd,bkd->bgqk", q, k_all, preferred_element_type=F32) * scaling
    scores = jnp.where(allowed[:, None], scores, -jnp.inf)
    peak = jnp.max(scores, axis=-1, keepdims=True)
    exps = jnp.exp(scores - peak)
    prob = exps / jnp.sum(exps, axis=-1, keepdims=True)
    prob_b = prob.astype(BF16)
    o = jnp.einsum("bgqk,bkd->bqgd", prob_b, v_all, preferred_element_type=F32)
    o = o.reshape(n_tok, q_cols).astype(BF16)

    o_parts = dot(o, w_out).astype(BF16).reshape(2, 2, own, width)
    o_added, w_gate, o_half = exchange(
        [TeamSum(o_parts, 4), row_gather(gate_part), Halves(o)], 4, micros=70
    )

    def added(term, others):
        return term.astype(F32) + others[0].astype(F32) + others[1].astype(F32)

    h1 = tokens + added(o_parts[0, 0], o_added)
    scale_two = rms_scale(h1)
    norm_two = (h1 * scale_two * gain_two).astype(BF16)
    norm_two_pair, gate_half, up_half, mixed_half, gn2_terms, out_parts = feed_forward(
        spread(norm_two), gd_pair, w_gate, w_down, up_part, 5
    )
    norm_two_pair = norm_two_pair.reshape(2, n_tok, width)
    gd_pair = gd_pair.reshape(2, n_tok, width)
    gn2 = natural(added(gn2_terms[0], gn2_terms[1:])) * gain_two
    gh1 = gy + scale_two * gn2 - h1 * scale_two**3 * jnp.mean(h1 * gn2, axis=-1, keepdims=True)

    tie = lax.optimization_barrier
    down_term = dot(mixed_half, gd_pair, PAIR_ROWS_T).astype(BF16)
    gate_term = dot(norm_two_pair, gate_half, PAIR_ROWS_T).astype(BF16)
    up_term = dot(norm_two_pair, up_half, PAIR_ROWS_T).astype(BF16)
    ga, down_term, gate_term, up_term = tie((gh1.astype(BF16), down_term, gate_term, up_term))
    down_x = sum_over(down_term, "x").astype(BF16)
    (ga_pair,) = exchange([NearGather(ga, PAIRED_SLOTS, TO_TEAM_EVEN)], 8)
    ga_pair, down_x, gate_term = tie((ga_pair, down_x, gate_term))
    gate_x = sum_over(gate_term, "x").astype(BF16)
    down_grad = sum_over(down_x, "zh")
    ga_pair = ga_pair.reshape(2, n_tok, width)

    go = dot(ga_pair[0], w_out, COLS_T).astype(BF16).reshape(n_slot, n_q, heads, HEAD)
    gp = jnp.einsum("bqgd,bkd->bgqk", go, v_all, preferred_element_type=F32)
    delta = jnp.sum(prob * gp, axis=-1, keepdims=True)
    gs = (prob * (gp - delta)).astype(BF16)
    gq_rot = jnp.einsum("bgqk,bkd->bqgd", gs, k_all, preferred_element_type=F32) * scaling
    gk_rot = jnp.einsum("bgqk,bqgd->bkd", gs, q, preferred_element_type=F32) * scaling
    gv_sum = jnp.einsum("bgqk,bqgd->bkd", prob_b, go, preferred_element_type=F32)
    gkv = jnp.concatenate([gk_rot, gv_sum], axis=-1).astype(BF16)
    gkv = gkv.reshape(n_slot, size["zh"], n_q, 2 * kv_cols).transpose(1, 0, 2, 3)
    gkv = gkv.reshape(size["zh"], n_tok, 2 * kv_cols)
    out_term = dot(o_half, ga_pair, PAIR_ROWS_T).astype(BF16)
    gkv, gate_x, down_grad, up_term, out_term = tie(
        (gkv, gate_x, down_grad, up_term, out_term)
    )
    up_x = sum_over(up_term, "x").astype(BF16)
    out_x = sum_over(out_term, "x").astype(BF16)
    gate_sum = sum_over(gate_x, "zh").astype(BF16)
    gkv_parts, out_added = exchange([NearSwap(gkv, ("zh",)), TeamSum(out_parts, 4)], 9)
    gkv_parts, up_x, out_x, gate_sum = tie((gkv_parts, up_x, out_x, gate_sum))
    gkv = sum(gkv_parts[i].astype(F32) for i in range(size["zh"]))
    gq = rotate(gq_rot.reshape(n_tok, heads, HEAD), cos, -sin).astype(BF16)
    gk = rotate(gkv[:, :kv_cols].reshape(n_tok, 1, HEAD), cos, -sin).astype(BF16)
    g_qkv = jnp.concatenate(
        [gq.reshape(n_tok, q_cols), gk.reshape(n_tok, kv_cols), gkv[:, kv_cols:].astype(BF16)],
        axis=1,
    )
    cols = g_qkv.shape[1] // 2
    mine = lax.dynamic_slice_in_dim(g_qkv, at["c"] * cols, cols, axis=1)
    other = lax.dynamic_slice_in_dim(g_qkv, (1 - at["c"]) * cols, cols, axis=1)
    g_qkv_half = jnp.stack([mine, lax.ppermute(other, "c", [(0, 1), (1, 0)])])
    attn_term = dot(norm_one_pair, g_qkv_half, PAIR_ROWS_T).astype(BF16)
    gn1_parts = dot(g_qkv, w_attn, COLS_T).astype(BF16).reshape(2, 2, own, width)
    gn1_parts, attn_term, up_x, out_x = tie((gn1_parts, attn_term, up_x, out_x))
    attn_x = sum_over(attn_term, "x").astype(BF16)
    up_sum = sum_over(up_x, "zh").astype(BF16)
    out_sum = sum_over(out_x, "zh").astype(BF16)
    (gn1_added,) = exchange([TeamSum(gn1_parts, 4)], 10)
    gn1_added, attn_x, up_sum, out_sum = tie((gn1_added, attn_x, up_sum, out_sum))
    attn_sum = sum_over(attn_x, "zh")
    out_sum = lax.ppermute(out_sum, AXES, [(b, a) for a, b in homes])
    outputs = valid * (h1 + added(out_parts[0, 0], out_added))
    outputs = outputs.astype(BF16).reshape(inputs.shape)
    n_owners = math.prod(size[a] for a in OWNERS)

    def by_owner(total):
        return total.astype(BF16).reshape(n_owners, rows, -1)

    gate_sum, up_sum = exchange([Swap(by_owner(t), OWNERS) for t in (gate_sum, up_sum)], 11)
    attn_sum, gate_sum, up_sum = tie((attn_sum, gate_sum, up_sum))
    (attn_sum,) = exchange([Swap(by_owner(attn_sum), OWNERS)], 12)
    gn1 = natural(added(gn1_parts[0, 0], gn1_added)) * gain_one
    g_tokens = (
        gh1
        + scale_one * gn1
        - tokens * scale_one**3 * jnp.mean(tokens * gn1, axis=-1, keepdims=True)
    )
    input_grad = g_tokens.astype(BF16).reshape(inputs.shape)

    def ff_natural(total):
        cut = total.reshape(
            size["zl"], size["y"], size["c"], rows, size["x"], size["zh"], ff_rows
        )
        return cut.transpose(3, 5, 0, 1, 4, 2, 6).reshape(rows, -1).astype(F32)

    def side(part):
        return part.transpose(1, 0, 2).reshape(rows, -1).astype(F32)

    attn_sum = attn_sum.reshape(team, 2, rows, -1)
    query_grad = side(attn_sum[:, 0])
    key_grad = side(attn_sum[:, 1, :, :kv_cols])
    value_grad = side(attn_sum[:, 1, :, kv_cols:])
    gate_grad = ff_natural(gate_sum)
    up_grad = ff_natural(up_sum)

    def against(w, g):
        return jnp.sum(w.astype(F32) * g, axis=1)

    attn_gain_grad = (
        against(query_weight, query_grad)
        + against(key_matrix, key_grad)
        + against(value_matrix, value_grad)
    ) / attn_gain.astype(F32)
    ffn_gain_grad = (against(gate_weight, gate_grad) + against(up_weight, up_grad)) / (
        ffn_gain.astype(F32)
    )
    return (
        outputs,
        input_grad,
        attn_gain_grad,
        query_grad,
        key_grad,
        value_grad,
        out_sum.astype(F32),
        ffn_gain_grad,
        gate_grad,
        up_grad,
        down_grad,
    )


def solution(mesh):
    ctx, fsdp = mesh.shape["ctx"], mesh.shape["fsdp"]
    grid = Mesh(mesh.devices.reshape(ctx // 2, 2, 2, fsdp // 4, 2), AXES)
    act = P(("y", "x", "c"), None, ("zh", "zl"), None)
    row = P(AXES)
    return jax.shard_map(
        on_device,
        mesh=grid,
        in_specs=(act, P(("y", "x", "c"))) + (row,) * 9 + (act,),
        out_specs=(act, act) + (row,) * 9,
        check_vma=False,
    )
```

time: 1110 us -> 1040 us (0.937)
  matrix products: 178 us -> 87.9 us
  Pallas kernels: 682 us -> 631 us
  waiting for transfers between devices: 0.72 us -> 41.5 us
  other arithmetic: 70.9 us -> 94 us
  local copies, waits for them, and re-layouts: 136 us -> 148 us
    pallas_call x12 -> x10, Pallas kernels: 682 us -> 631 us  [the longest x9 503 us: exchange(): pl.pallas_call(kernel, out_shape=[jax.ShapeDtypeStruct(job.shape(sizes),...]
    dot_general x10 -> x7, matrix products: 100 us -> 53.9 us  [dot(): return lax.dot_general(a, b, dims, preferred_element_type=F32)]
    dot_general x5 -> x2, matrix products: 54.1 us -> 8.97 us  [dot(): return jnp.dot(a, b, preferred_element_type=F32)]
    ppermute x10, waiting for transfers between devices: 0.03 us -> 40.8 us  [sum_over(): lax.ppermute(lax.dynamic_slice_in_dim(term, (1 - side) * rows, rows), axi...]
    convert_element_type x0 -> x6, local copies, waits for them, and re-layouts: none -> 23 us  [added(): return term.astype(F32) + others[0].astype(F32) + others[1].astype(F32)]
    unnamed x211 -> x199, local copies, waits for them, and re-layouts: 27.1 us -> 21.7 us
  transfers between devices with their start and end apart: 14 -> 14, of which waited for: 0 -> 2; matrix products, arithmetic and copies ran while one was open for 18% -> 16% of each run, Pallas kernels for 60% -> 47%
where the time goes in v3:
time: 1040 us; the launch traced here: 1030 us
  Pallas kernels  631 us (61%)
  local copies, waits for them, and re-layouts  148 us (14%)
  other arithmetic  94 us (9%)
  matrix products  87.9 us (8%)
  waiting for transfers between devices  41.5 us (4%)
  between operations  16.6 us (2%)
    pallas_call x9, Pallas kernels, exchange(): pl.pallas_call(kernel, out_shape=[jax.ShapeDtypeStruct(job.shape(sizes),...  503 us
    pallas_call x1, Pallas kernels, feed_forward(): pl.pallas_call(kernel, out_shape=[shape((2, 2, 2, own, width), BF16), *[s...  128 us
    dot_general x7, matrix products, dot(): return lax.dot_general(a, b, dims, preferred_element_type=F32)  53.9 us
    ppermute x10, waiting for transfers between devices, sum_over(): lax.ppermute(lax.dynamic_slice_in_dim(term, (1 - side) * rows, rows), axi...  40.8 us
    convert_element_type x6, local copies, waits for them, and re-layouts, added(): return term.astype(F32) + others[0].astype(F32) + others[1].astype(F32)  23 us
    unnamed x199, local copies, waits for them, and re-layouts  21.7 us
    convert_element_type x6, local copies, waits for them, and re-layouts, ff_natural(): return cut.transpose(3, 5, 0, 1, 4, 2, 6).reshape(rows, -1).astype(F32)  21.1 us
  transfers between devices with their start and end apart: 14, of which 2 were waited for; matrix products, arithmetic and copies ran while one was open for 16% of the time, Pallas kernels for 47%

profile of v3, /device:TPU:0, one launch (start us, length us, event | category | flops | bytes accessed | tf_op | source)
XLA Modules:
  0.0 1028.2 jit_solution(9608266351006819341)
XLA Ops:
  29.9 69.4 %shard_map.203 = (f32[32,8,128]{2,1,0:T(8,128)S(1)}, bf16[4,64,1024]{2,1,0:T(8,128)(2,1)S(1)}, bf16[4,64,2048]{2,1,0:T(8,128)(2,1)S(1)}, bf16[4,64,2048]{2,1,0:T(8,128)(2,1)S(1)}) custom-call(f32[8,128]{1,0:T(8,128)S(1)} %scatter.14.refs_0_, bf16[4,64,1024]{2,1,0:T(8,128)(2,1)S(1)} %pad_maximum_fusion.4.refs_1_, bf16[4,64,2048]{2,1,0:T(8,128)(2,1)S(1)} %reshape.1035.refs_2_, ...), custom_call_target="tpu_custom_call" | custom-call | bytes 150000000 | tf_op jit(solution)/shard_map/pallas_call | solution.py:353
  102.0 4.1 reshape.1062
  116.8 52.3 %shard_map.204 = (bf16[2,2,2,256,2048]{4,3,2,1,0:T(8,128)(2,1)}, bf16[2048,1024]{1,0:T(8,128)(2,1)}, bf16[8,64,2048]{2,1,0:T(8,128)(2,1)S(1)}) custom-call(bf16[256,2048]{1,0:T(8,128)(2,1)S(1)} %reshape.1038.refs_0_, bf16[4,64,1024]{2,1,0:T(8,128)(2,1)S(1)} %get-tuple-element.97.refs_1_, bf16[64,2048]{1,0:T(8,128)(2,1)S(1)} %collective-permute-done.refs_2_), custom_call_target="tpu_custom_call" | custom-call | bytes 150000000 | tf_op jit(solution)/shard_map/pallas_call | solution.py:353
  173.3 4.6 fusion.69
  183.3 65.1 %shard_map.205 = (bf16[2,1024,512]{2,1,0:T(8,128)(2,1)S(1)}, bf16[2,2,2,256,2048]{4,3,2,1,0:T(8,128)(2,1)}) custom-call(bf16[1024,512]{1,0:T(8,128)(2,1)S(1)} %pad_maximum_fusion.2.refs_0_, bf16[256,2048]{1,0:T(8,128)(2,1)S(1)} %fusion.25.refs_1_), custom_call_target="tpu_custom_call" | custom-call | bytes 150000000 | tf_op jit(solution)/shard_map/pallas_call | solution.py:353
  262.6 7.7 fusion.68
  270.3 5.7 fusion.31
  278.9 4.4 convolution_convert_fusion
  283.4 63.0 %shard_map.206 = (bf16[2,256,2048]{2,1,0:T(8,128)(2,1)S(1)}, bf16[2048,2048]{1,0:T(8,128)(2,1)}, bf16[2,1024,256]{2,1,0:T(8,128)(2,1)S(1)}) custom-call(bf16[2,2,256,2048]{3,2,1,0:T(8,128)(2,1)} %bitcast.315, bf16[4,64,2048]{2,1,0:T(8,128)(2,1)S(1)} %copy-done.4, bf16[1024,512]{1,0:T(8,128)(2,1)S(1)} %bitcast.299), custom_call_target="tpu_custom_call" | custom-call | bytes 210000000 | tf_op jit(solution)/shard_map/pallas_call | solution.py:353
  359.8 4.1 reshape.1068
  363.9 4.7 multiply_reduce_fusion.4
  374.7 128.0 %shard_map.207 = (bf16[2,2,2,256,2048]{4,3,2,1,0:T(8,128)(2,1)}, bf16[2,1024,1024]{2,1,0:T(8,128)(2,1)}, bf16[2,1024,1024]{2,1,0:T(8,128)(2,1)}, bf16[2,1024,102...) custom-call(bf16[256,2048]{1,0:T(8,128)(2,1)} %reshape.1045.norm_ref, ...), custom_call_target="tpu_custom_call" | custom-call | bytes 390000000 | tf_op jit(solution)/shard_map/pallas_call | solution.py:589
  525.5 14.1 %bitcast_convert_fusion.1 = bf16[2048,1024]{1,0:T(8,128)(2,1)} fusion(bf16[2,1024,2048]{2,1,0:T(8,128)(2,1)} %bitcast.379, bf16[2,1024,1024]{2,1,0:T(8,128)(2,1)} %get-tuple-element.111), kind=kOutput, calls=%fused_computation.8 | convolution fusion | flops 8592031744 | bytes 16777216 | tf_op jit(solution)/shard_map/dot_general | solution.py:394
  539.7 11.1 %bitcast_convert_fusion = bf16[2048,1024]{1,0:T(8,128)(2,1)} fusion(bf16[2,1024,2048]{2,1,0:T(8,128)(2,1)S(1)} %bitcast.382, bf16[2,1024,1024]{2,1,0:T(8,128)(2,1)S(1)} %copy-done.85), kind=kOutput, calls=%fused_computation.7 | convolution fusion | flops 8592031744 | bytes 16777216 | tf_op jit(solution)/shard_map/dot_general | solution.py:394
  550.8 9.6 bitcast_convert_fusion.2
  565.7 40.5 %shard_map.208 = bf16[2,2,2,256,2048]{4,3,2,1,0:T(8,128)(2,1)} custom-call(bf16[256,2048]{1,0:T(8,128)(2,1)S(1)} %fusion.20.refs_0_), custom_call_target="tpu_custom_call" | custom-call | bytes 150000000 | tf_op jit(solution)/shard_map/pallas_call | solution.py:353
  606.2 6.9 collective-permute-done.1
  624.4 5.8 bitcast_convert_fusion.4
  630.2 7.2 fusion.1
  640.7 5.6 fusion.3
  653.4 33.9 %collective-permute-done.3 = bf16[256,2048]{1,0:T(8,128)(2,1)} collective-permute-done((bf16[256,2048]{1,0:T(8,128)(2,1)}, bf16[256,2048]{1,0:T(8,128)(2,1)}, u32[]{:S(2)}, u32[]{:S(2)}) %collective-permute-start.3) | collective-permute-done | bytes 1048608 | tf_op jit(solution)/shard_map/ppermute | solution.py:382
  710.9 90.2 %shard_map.209 = (bf16[2,1024,512]{2,1,0:T(8,128)(2,1)S(1)}, bf16[2,256,2048]{2,1,0:T(8,128)(2,1)S(1)}) custom-call(bf16[2,1024,512]{2,1,0:T(8,128)(2,1)} %bitcast.322, bf16[2,2,256,2048]{3,2,1,0:T(8,128)(2,1)} %get-tuple-element.107.refs_1_), custom_call_target="tpu_custom_call" | custom-call | bytes 150000000 | tf_op jit(solution)/shard_map/pallas_call | solution.py:353
  810.8 7.3 convolution_convert_fusion.1
  818.2 5.1 bitcast_convert_fusion.3
  830.6 66.5 %shard_map.210 = bf16[2,256,2048]{2,1,0:T(8,128)(2,1)S(1)} custom-call(bf16[2,2,256,2048]{3,2,1,0:T(8,128)(2,1)} %bitcast.333), custom_call_target="tpu_custom_call" | custom-call | bytes 150000000 | tf_op jit(solution)/shard_map/pallas_call | solution.py:353
  910.4 4.1 reshape.1079
  917.2 4.5 add_bitcast_fusion
  932.3 4.6 subtract_convert_fusion
  936.8 41.5 %shard_map.211 = (bf16[8,64,1024]{2,1,0:T(8,128)(2,1)S(1)}, bf16[8,64,1024]{2,1,0:T(8,128)(2,1)S(1)}) custom-call(bf16[8,64,1024]{2,1,0:T(8,128)(2,1)S(1)} %bitcast.296, bf16[8,64,1024]{2,1,0:T(8,128)(2,1)S(1)} %bitcast.297), custom_call_target="tpu_custom_call" | custom-call | bytes 150000000 | tf_op jit(solution)/shard_map/pallas_call | solution.py:353
  979.3 15.0 %shard_map.212 = bf16[8,64,512]{2,1,0:T(8,128)(2,1)S(1)} custom-call(bf16[8,64,512]{2,1,0:T(8,128)(2,1)S(1)} %bitcast.303), custom_call_target="tpu_custom_call" | custom-call | bytes 150000000 | tf_op jit(solution)/shard_map/pallas_call | solution.py:353
  998.8 4.5 copy.90
  1011.7 4.5 copy.91
  (380 shorter events, 216.2 us)
Async XLA Ops:
  7.2 367.5 %all-gather.2.cloned.1.call-start = ((), (), s32[]{:S(2)}) async-start(), calls=%async_computation | async-start | bytes 9437184 | tf_op jit(solution)/shard_map/all_gather | solution.py:676
  7.9 108.8 %collective-permute-start = (bf16[64,2048]{1,0:T(8,128)(2,1)}, bf16[64,2048]{1,0:T(8,128)(2,1)S(1)}, u32[]{:S(2)}, u32[]{:S(2)}) collective-permute-start(bf16[64,2048]{1,0:T(8,128)(2,1)} %param.24), channel_id=1, source_target_pairs={{0,0},{1,16},{2,2},{3,18},{4,1},{5,17},{6,3},{7,19},{8,4},{9,20},{... | collective-permute-start | bytes 786440 | tf_op jit(solution)/shard_map/ppermute | solution.py:694
  116.7 140.7 %copy-start.36 = (f32[512,128]{1,0:T(8,128)}, f32[512,128]{1,0:T(8,128)S(1)}, u32[]{:S(2)}) copy-start(f32[512,128]{1,0:T(8,128)S(1)} %get-tuple-element.176) | copy-start | bytes 786436
  116.7 140.7 %copy-start.50 = (f32[512,128]{1,0:T(8,128)}, f32[512,128]{1,0:T(8,128)S(1)}, u32[]{:S(2)}) copy-start(f32[512,128]{1,0:T(8,128)S(1)} %get-tuple-element.175) | copy-start | bytes 786436
  248.6 21.7 %copy-start.23 = (bf16[2,2,512,512]{3,2,1,0:T(8,128)(2,1)}, bf16[2,2,512,512]{3,2,1,0:T(8,128)(2,1)S(1)}, u32[]{:S(2)}) copy-start(bf16[2,2,512,512]{3,2,1,0:T(8,128)(2,1)S(1)} %copy.63) | copy-start | bytes 6291460
  522.3 17.4 %slice-start.9 = ((s8[8388608]{0:T(1024)(128)(4,1)}), s8[4194304]{0:T(1024)(128)(4,1)S(1)}, s32[]{:S(2)}) async-start(s8[8388608]{0:T(1024)(128)(4,1)} %bitcast.380), calls=%async_computation.10 | async-start | bytes 8388608
  525.5 14.1 %slice-start.10 = ((s8[8388608]{0:T(1024)(128)(4,1)}), s8[4194304]{0:T(1024)(128)(4,1)S(1)}, s32[]{:S(2)}) async-start(s8[8388608]{0:T(1024)(128)(4,1)} %bitcast.380), calls=%async_computation.11 | async-start | bytes 8388608
  525.5 14.1 %copy-start.85 = (bf16[2,1024,1024]{2,1,0:T(8,128)(2,1)S(1)}, bf16[2,1024,1024]{2,1,0:T(8,128)(2,1)}, u32[]{:S(2)}) copy-start(bf16[2,1024,1024]{2,1,0:T(8,128)(2,1)} %get-tuple-element.112) | copy-start | bytes 12582916
  525.5 25.3 %slice-start.5 = ((s8[8388608]{0:T(1024)(128)(4,1)}), s8[4194304]{0:T(1024)(128)(4,1)S(1)}, s32[]{:S(2)}) async-start(s8[8388608]{0:T(1024)(128)(4,1)} %bitcast.325), calls=%async_computation.6 | async-start | bytes 8388608
  539.6 11.1 %slice-start.6 = ((s8[8388608]{0:T(1024)(128)(4,1)}), s8[4194304]{0:T(1024)(128)(4,1)S(1)}, s32[]{:S(2)}) async-start(s8[8388608]{0:T(1024)(128)(4,1)} %bitcast.325), calls=%async_computation.7 | async-start | bytes 8388608
  539.7 11.1 %copy-start.84 = (bf16[2,1024,1024]{2,1,0:T(8,128)(2,1)S(1)}, bf16[2,1024,1024]{2,1,0:T(8,128)(2,1)}, u32[]{:S(2)}) copy-start(bf16[2,1024,1024]{2,1,0:T(8,128)(2,1)} %get-tuple-element.109) | copy-start | bytes 12582916
  565.2 47.9 %collective-permute-start.1 = (bf16[512,2048]{1,0:T(8,128)(2,1)}, bf16[512,2048]{1,0:T(8,128)(2,1)}, u32[]{:S(2)}, u32[]{:S(2)}) collective-permute-start(bf16[512,2048]{1,0:T(8,128)(2,1)} %constant_dynamic-slice_fusion.10), channel_id=1, source_target_pairs={{0,2},{2,0},{1,3},{3,1},{4,6},{6,4},{5,7},{7,5},{8,10},{10,8},{9,1... | collective-permute-start | bytes 6291464 | tf_op jit(solution)/shard_map/ppermute | solution.py:382
  565.7 47.3 %copy-start.44 = (bf16[1024,2048]{1,0:T(8,128)(2,1)S(1)}, bf16[1024,2048]{1,0:T(8,128)(2,1)}, u32[]{:S(2)}) copy-start(bf16[1024,2048]{1,0:T(8,128)(2,1)} %copy-done.43) | copy-start | bytes 12582916
  624.4 16.3 %slice-start.3 = ((s8[8388608]{0:T(1024)(128)(4,1)}), s8[4194304]{0:T(1024)(128)(4,1)S(1)}, s32[]{:S(2)}) async-start(s8[8388608]{0:T(1024)(128)(4,1)} %bitcast.323), calls=%async_computation.4 | async-start | bytes 8388608
  637.6 52.7 %collective-permute-start.2 = (bf16[1024,1024]{1,0:T(8,128)(2,1)S(1)}, bf16[1024,1024]{1,0:T(8,128)(2,1)}, u32[]{:S(2)}, u32[]{:S(2)}) collective-permute-start(bf16[1024,1024]{1,0:T(8,128)(2,1)S(1)} %constant_dynamic-slice_fusion.9), channel_id=1, source_target_pairs={{0,2},{2,0},{1,3},{3,1},{4,6},{6,4},{5,7},{7,5},{8,10},{10,8},{9,1... | collective-permute-start | bytes 6291464 | tf_op jit(solution)/shard_map/ppermute | solution.py:382
  640.7 46.7 %collective-permute-start.3 = (bf16[256,2048]{1,0:T(8,128)(2,1)}, bf16[256,2048]{1,0:T(8,128)(2,1)}, u32[]{:S(2)}, u32[]{:S(2)}) collective-permute-start(bf16[256,2048]{1,0:T(8,128)(2,1)} %constant_dynamic-slice_fusion.8), channel_id=1, source_target_pairs={{0,16},{16,0},{1,17},{17,1},{2,18},{18,2},{3,19},{19,3},{4,20},{20... | collective-permute-start | bytes 3145736 | tf_op jit(solution)/shard_map/ppermute | solution.py:382
  694.6 109.7 %collective-permute-start.4 = (bf16[1024,1024]{1,0:T(8,128)(2,1)}, bf16[1024,1024]{1,0:T(8,128)(2,1)}, u32[]{:S(2)}, u32[]{:S(2)}) collective-permute-start(bf16[1024,1024]{1,0:T(8,128)(2,1)} %constant_dynamic-slice_fusion.7), channel_id=1, source_target_pairs={{0,2},{2,0},{1,3},{3,1},{4,6},{6,4},{5,7},{7,5},{8,10},{10,8},{9,1... | collective-permute-start | bytes 6291464 | tf_op jit(solution)/shard_map/ppermute | solution.py:382
  700.2 100.9 %collective-permute-start.5 = (bf16[128,2048]{1,0:T(8,128)(2,1)}, bf16[128,2048]{1,0:T(8,128)(2,1)}, u32[]{:S(2)}, u32[]{:S(2)}) collective-permute-start(bf16[128,2048]{1,0:T(8,128)(2,1)} %constant_dynamic-slice_fusion.6), channel_id=1, source_target_pairs={{0,2},{2,0},{1,3},{3,1},{4,6},{6,4},{5,7},{7,5},{8,10},{10,8},{9,1... | collective-permute-start | bytes 1572872 | tf_op jit(solution)/shard_map/ppermute | solution.py:382
  702.0 100.5 %collective-permute-start.6 = (bf16[512,1024]{1,0:T(8,128)(2,1)}, bf16[512,1024]{1,0:T(8,128)(2,1)}, u32[]{:S(2)}, u32[]{:S(2)}) collective-permute-start(bf16[512,1024]{1,0:T(8,128)(2,1)} %constant_dynamic-slice_fusion.5), channel_id=1, source_target_pairs={{0,16},{16,0},{1,17},{17,1},{2,18},{18,2},{3,19},{19,3},{4,20},{20... | collective-permute-start | bytes 3145736 | tf_op jit(solution)/shard_map/ppermute | solution.py:382
  710.9 90.2 %copy-start.53 = (bf16[256,2048]{1,0:T(8,128)(2,1)S(1)}, bf16[256,2048]{1,0:T(8,128)(2,1)}, u32[]{:S(2)}) copy-start(bf16[256,2048]{1,0:T(8,128)(2,1)} %fusion.8) | copy-start | bytes 3145732
  802.4 23.7 %copy-start.55 = (bf16[128,2048]{1,0:T(8,128)(2,1)}, bf16[128,2048]{1,0:T(8,128)(2,1)S(1)}, u32[]{:S(2)}) copy-start(bf16[128,2048]{1,0:T(8,128)(2,1)S(1)} %add_convert_fusion.6) | copy-start | bytes 1572868
  806.9 18.0 %copy-start.25 = (bf16[1024,1024]{1,0:T(8,128)(2,1)}, bf16[1024,1024]{1,0:T(8,128)(2,1)S(1)}, u32[]{:S(2)}) copy-start(bf16[1024,1024]{1,0:T(8,128)(2,1)S(1)} %add_convert_fusion) | copy-start | bytes 6291460
  809.1 9.0 collective-permute-start.7
  818.1 10.9 %copy-start.35 = (bf16[1024,2048]{1,0:T(8,128)(2,1)}, bf16[1024,2048]{1,0:T(8,128)(2,1)S(1)}, u32[]{:S(2)}) copy-start(bf16[1024,2048]{1,0:T(8,128)(2,1)S(1)} %convolution_convert_fusion.1) | copy-start | bytes 12582916
  824.4 77.9 %collective-permute-start.8 = (bf16[1024,512]{1,0:T(8,128)(2,1)}, bf16[1024,512]{1,0:T(8,128)(2,1)}, u32[]{:S(2)}, u32[]{:S(2)}) collective-permute-start(bf16[1024,512]{1,0:T(8,128)(2,1)} %constant_dynamic-slice_fusion.3), channel_id=1, source_target_pairs={{0,2},{2,0},{1,3},{3,1},{4,6},{6,4},{5,7},{7,5},{8,10},{10,8},{9,1... | collective-permute-start | bytes 3145736 | tf_op jit(solution)/shard_map/ppermute | solution.py:382
  826.0 79.2 %collective-permute-start.9 = (bf16[512,1024]{1,0:T(8,128)(2,1)}, bf16[512,1024]{1,0:T(8,128)(2,1)}, u32[]{:S(2)}, u32[]{:S(2)}) collective-permute-start(bf16[512,1024]{1,0:T(8,128)(2,1)} %constant_dynamic-slice_fusion.2), channel_id=1, source_target_pairs={{0,16},{16,0},{1,17},{17,1},{2,18},{18,2},{3,19},{19,3},{4,20},{20... | collective-permute-start | bytes 3145736 | tf_op jit(solution)/shard_map/ppermute | solution.py:382
  826.2 74.9 %collective-permute-start.10 = (bf16[64,2048]{1,0:T(8,128)(2,1)S(1)}, bf16[64,2048]{1,0:T(8,128)(2,1)}, u32[]{:S(2)}, u32[]{:S(2)}) collective-permute-start(bf16[64,2048]{1,0:T(8,128)(2,1)S(1)} %constant_dynamic-slice_fusion.1), channel_id=1, source_target_pairs={{0,16},{16,0},{1,17},{17,1},{2,18},{18,2},{3,19},{19,3},{4,20},{20... | collective-permute-start | bytes 786440 | tf_op jit(solution)/shard_map/ppermute | solution.py:382
  931.4 47.7 %collective-permute-start.11 = (bf16[512,512]{1,0:T(8,128)(2,1)S(1)}, bf16[512,512]{1,0:T(8,128)(2,1)S(1)}, u32[]{:S(2)}, u32[]{:S(2)}) collective-permute-start(bf16[512,512]{1,0:T(8,128)(2,1)S(1)} %constant_dynamic-slice_fusion), channel_id=1, source_target_pairs={{0,16},{16,0},{1,17},{17,1},{2,18},{18,2},{3,19},{19,3},{4,20},{20... | collective-permute-start | bytes 1572872 | tf_op jit(solution)/shard_map/ppermute | solution.py:382
  931.5 46.8 %collective-permute-start.12 = (bf16[64,2048]{1,0:T(8,128)(2,1)S(1)}, bf16[64,2048]{1,0:T(8,128)(2,1)S(1)}, u32[]{:S(2)}, u32[]{:S(2)}) collective-permute-start(bf16[64,2048]{1,0:T(8,128)(2,1)S(1)} %add_convert_fusion.9), channel_id=1, source_target_pairs={{0,0},{16,1},{2,2},{18,3},{1,4},{17,5},{3,6},{19,7},{4,8},{20,9},{... | collective-permute-start | bytes 786440 | tf_op jit(solution)/shard_map/ppermute | solution.py:834
  936.8 42.3 %copy-start.48 = (bf16[1024,512]{1,0:T(8,128)(2,1)S(1)}, bf16[1024,512]{1,0:T(8,128)(2,1)}, u32[]{:S(2)}) copy-start(bf16[1024,512]{1,0:T(8,128)(2,1)} %add_convert_fusion.4) | copy-start | bytes 3145732
  979.1 15.3 %copy-start.68 = (bf16[64,1024]{1,0:T(8,128)(2,1)S(1)}, bf16[64,1024]{1,0:T(8,128)(2,1)}, u32[]{:S(2)}) copy-start(bf16[64,1024]{1,0:T(8,128)(2,1)} %param.23) | copy-start | bytes 393220
  979.3 16.1 %copy-start.65 = (bf16[64,2048]{1,0:T(8,128)(2,1)S(1)}, bf16[64,2048]{1,0:T(8,128)(2,1)}, u32[]{:S(2)}) copy-start(bf16[64,2048]{1,0:T(8,128)(2,1)} %param.21) | copy-start | bytes 786436
  (80 other events, 355.6 us)
Sparse Core Ops, SparseCore 0:
  9.9 94.5 all-gather.1

commit v4 on v3

--- a/solution.py
+++ b/solution.py
@@ -72,7 +72,7 @@
 
     def spot(self, out, owner, off, part, sizes):
         team, rows, _ = self.x.shape
-        block = place(owner, ("x", "zh"), sizes) * team + part
+        block = (owner["zh"] * team + part) * sizes["x"] + owner["x"]
         start = pl.multiple_of((block * sizes["c"] + owner["c"]) * rows, rows)
         return out.at[pl.ds(start, rows)]
 
@@ -84,7 +84,7 @@
     def shape(self, sizes):
         return self.x.shape
 
-    def own_shape(self):
+    def own_shape(self, sizes):
         return self.x.shape[1:]
 
     def offsets(self, sizes):
@@ -92,6 +92,31 @@
 
     def pair(self, x, out, here, to, off, sizes):
         return x.at[place(to, self.layout, sizes)], out.at[place(here, self.layout, sizes)]
+
+
+class ColumnSwap:
+    def __init__(self, x, block):
+        self.x, self.block = x, block
+
+    def shape(self, sizes):
+        rows, columns = self.x.shape
+        team = sizes["zl"] * sizes["y"]
+        return (team, rows, columns // team)
+
+    def own_shape(self, sizes):
+        return self.shape(sizes)[1:]
+
+    def offsets(self, sizes):
+        return offsets(sizes, TEAM)
+
+    def pieces(self, x, out, to, sizes):
+        found = []
+        for i, share in enumerate(offsets(sizes, SHARES)):
+            start = pl.multiple_of(place({**share, **to}, AXES, sizes) * self.block, self.block)
+            found.append(
+                (x.at[:, pl.ds(start, self.block)], out.at[:, pl.ds(i * self.block, self.block)])
+            )
+        return found
 
 
 class NearSwap(Swap):
@@ -108,7 +133,7 @@
         rows, columns = self.x.shape
         return (2, rows, columns // 2)
 
-    def own_shape(self):
+    def own_shape(self, sizes):
         rows, columns = self.x.shape
         return (rows, columns // 2)
 
@@ -122,6 +147,7 @@
 
 
 CHUNKS = 4
+AHEAD = 2
 
 
 class TeamSum:
@@ -130,6 +156,15 @@
 
     def shape(self, sizes):
         return (2,) + self.x.shape[2:]
+
+
+class PeerSum:
+    def __init__(self, x, x_inside):
+        self.x, self.x_inside = x, x_inside
+
+    def shape(self, sizes):
+        rows, columns = self.x.shape
+        return (rows // (sizes["x"] * sizes["zh"]), columns)
 
 
 class Net:
@@ -192,12 +227,14 @@
         self.job, self.net, self.sizes = job, net, net.sizes
         self.steps = []
         for part, order in enumerate(job.orders):
-            for off in offsets(self.sizes, order):
-                used = [i for i, a in enumerate(order) if off[a]]
+            groups = [(axes,) if isinstance(axes, str) else axes for axes in order]
+            for off in offsets(self.sizes, [a for axes in groups for a in axes]):
+                used = [i for i, axes in enumerate(groups) if any(off[a] for a in axes)]
                 sends = [
-                    net.wire({a: d})
-                    for a in order[used[-1] + 1 if used else 0 :]
-                    for d in range(1, self.sizes[a])
+                    net.wire(to)
+                    for axes in groups[used[-1] + 1 if used else 0 :]
+                    for to in offsets(self.sizes, axes)
+                    if any(to.values())
                 ]
                 hops = len(used)
                 key = (job.rank, part + 2 * hops, hops, number, part)
@@ -215,14 +252,100 @@
         else:
             source = job.cut(self.x, part)
         for wire in sends:
-            ((a, d),) = wire[1].items()
             there = dict(off)
-            there[a] = (-d) % self.sizes[a]
+            for a, d in wire[1].items():
+                there[a] = -d % self.sizes[a]
             dst = job.spot(self.out, owner, there, part, self.sizes)
             self.arrivals[part, tuple(sorted(there.items()))] = net.send(source, dst, wire)
 
     def own(self, part):
         return self.job.spot(self.out, self.net.here, {a: 0 for a in AXES}, part, self.sizes)
+
+
+class Stream:
+    def __init__(self, net, shape, x_inside):
+        self.net, self.x_inside = net, x_inside
+        self.nx, self.nz = net.sizes["x"], net.sizes["zh"]
+        self.columns, self.dtype = shape[1], BF16
+        self.rows = shape[0] // (self.nx * self.nz * CHUNKS)
+        self.chunks = [(z, q) for z in [*range(1, self.nz), 0] for q in range(CHUNKS)]
+        self.x_wires = [[net.wire({"x": d}) for d in range(1, self.nx)] for _ in self.chunks]
+        self.z_wires = [net.wire({"zh": z}) if z else None for z, _ in self.chunks]
+
+    def shape(self):
+        return jax.ShapeDtypeStruct((CHUNKS * self.rows, self.columns), self.dtype)
+
+    def scratch(self):
+        n, chunk = len(self.chunks), (self.rows, self.columns)
+        return [
+            pltpu.VMEM((n, *chunk), self.dtype),
+            pltpu.VMEM((self.nx - 1, n, *chunk), self.dtype),
+            pltpu.VMEM((self.nz - 1, CHUNKS, *chunk), self.dtype),
+            pltpu.SemaphoreType.DMA((n,)),
+            pltpu.SemaphoreType.DMA((CHUNKS,)),
+        ]
+
+    def open(self, term, out, mine, from_x, from_z, load_sem, store_sem):
+        self.term, self.out, self.mine = term, out, mine
+        self.from_x, self.from_z = from_x, from_z
+        self.load_sem, self.store_sem = load_sem, store_sem
+        self.loads, self.x_sent, self.z_sent, self.stores = {}, {}, {}, []
+
+    def window(self, x, z, q):
+        zh = self.net.moved({"zh": z})["zh"]
+        if self.x_inside:
+            block = (zh * CHUNKS + q) * self.nx + x
+        else:
+            block = (x * self.nz + zh) * CHUNKS + q
+        return self.term.at[pl.ds(pl.multiple_of(block * self.rows, self.rows), self.rows)]
+
+    def run(self, step, k):
+        (self.issue, self.merge, self.last)[step](k)
+
+    def issue(self, k):
+        z, q = self.chunks[k]
+        self.x_sent[k] = []
+        for d, wire in enumerate(self.x_wires[k], 1):
+            x = self.net.moved({"x": d})["x"]
+            self.x_sent[k].append(
+                self.net.send(self.window(x, z, q), self.from_x.at[d - 1, k], wire)
+            )
+        load = pltpu.make_async_copy(
+            self.window(self.net.here["x"], z, q), self.mine.at[k], self.load_sem.at[k]
+        )
+        load.start()
+        self.loads[k] = load
+
+    def merge(self, k):
+        z, q = self.chunks[k]
+        self.loads[k].wait()
+        for cp in self.x_sent[k]:
+            cp.wait_recv()
+        total = self.mine[k].astype(F32)
+        for d in range(self.nx - 1):
+            total += self.from_x[d, k].astype(F32)
+        self.mine[k] = total.astype(self.dtype)
+        if z:
+            self.z_sent[z, q] = self.net.send(
+                self.mine.at[k], self.from_z.at[z - 1, q], self.z_wires[k]
+            )
+
+    def last(self, q):
+        k = self.chunks.index((0, q))
+        total = self.mine[k].astype(F32)
+        for z in range(1, self.nz):
+            self.z_sent[z, q].wait_recv()
+            total += self.from_z[z - 1, q].astype(F32)
+        self.mine[k] = total.astype(self.dtype)
+        store = pltpu.make_async_copy(
+            self.mine.at[k], self.out.at[pl.ds(q * self.rows, self.rows)], self.store_sem.at[q]
+        )
+        store.start()
+        self.stores.append(store)
+
+    def close(self):
+        for store in self.stores:
+            store.wait()
 
 
 class Adder:
@@ -292,22 +415,33 @@
             runner = Adder(job, number, net)
             steps += runner.steps
             stage = runner.scratch()
+        elif isinstance(job, PeerSum):
+            runner = Stream(net, job.x.shape, job.x_inside)
+            for k in range(len(runner.chunks)):
+                steps.append(((0, k, 0, number, k), runner, 0, k))
+                steps.append(((1, k + 2, 1, number, k), runner, 1, k))
+            for k in range(CHUNKS):
+                steps.append(((1, k + len(runner.chunks) + 2, 2, number, k), runner, 2, k))
+            stage = runner.scratch()
         else:
             runner = None
-            swaps += [(number, off, net.wire(off)) for off in job.offsets(sizes) if any(off.values())]
-            stage = [pltpu.VMEM(job.own_shape(), job.x.dtype)]
+            n = math.prod(sizes[a] for a in SHARES) if isinstance(job, ColumnSwap) else 1
+            for off in job.offsets(sizes):
+                if any(off.values()):
+                    swaps.append((number, off, [net.wire(off) for _ in range(n)]))
+            stage = [pltpu.VMEM(job.own_shape(sizes), job.x.dtype)]
         runners.append((runner, len(scratch), len(scratch) + len(stage)))
         scratch += stage
     steps.sort(key=lambda s: s[0])
 
     def kernel(*refs):
         ins, outs, rest = refs[:count], refs[count : 2 * count], refs[2 * count :]
-        send_sem, recv_sem, local_sem = rest[-3:]
+        send_sem, recv_sem, local_sem, piece_sem = rest[-4:]
         net.open(send_sem, recv_sem)
         loads, stores = [], []
         for number, job in enumerate(jobs):
             runner, lo, hi = runners[number]
-            if isinstance(job, TeamSum):
+            if isinstance(job, (TeamSum, PeerSum)):
                 runner.open(ins[number], outs[number], *rest[lo:hi])
                 continue
             (stage,) = rest[lo:hi]
@@ -317,6 +451,14 @@
                 puts = [
                     (job.cut(stage, part), runner.own(part)) for part in range(len(job.orders))
                 ]
+            elif isinstance(job, ColumnSwap):
+                mine = {a: net.here[a] for a in TEAM}
+                for i, (src, dst) in enumerate(job.pieces(ins[number], stage, mine, sizes)):
+                    load = pltpu.make_async_copy(src, dst, piece_sem.at[number, i])
+                    load.start()
+                    loads.append((load, number, []))
+                loads[-1][2].append((stage, outs[number].at[place(net.here, TEAM, sizes)]))
+                continue
             else:
                 none = {a: 0 for a in AXES}
                 src, dst = job.pair(ins[number], outs[number], net.here, net.here, none, sizes)
@@ -328,10 +470,16 @@
             if not hops:
                 runner.run(hops, *what)
         received = []
-        for number, off, wire in swaps:
+        for number, off, wires in swaps:
             to = net.moved(off)
-            src, dst = jobs[number].pair(ins[number], outs[number], net.here, to, off, sizes)
-            received.append(net.send(src, dst, wire))
+            job = jobs[number]
+            if isinstance(job, ColumnSwap):
+                mine = outs[number].at[place(net.here, TEAM, sizes)]
+                pairs = job.pieces(ins[number], mine, {a: to[a] for a in TEAM}, sizes)
+            else:
+                pairs = [job.pair(ins[number], outs[number], net.here, to, off, sizes)]
+            for (src, dst), wire in zip(pairs, wires, strict=True):
+                received.append(net.send(src, dst, wire))
         for load, number, puts in loads:
             load.wait()
             for i, (src, dst) in enumerate(puts):
@@ -347,6 +495,9 @@
             if isinstance(runner, Adder):
                 runner.finish()
         net.close()
+        for runner, _, _ in runners:
+            if isinstance(runner, Stream):
+                runner.close()
         for store in stores:
             store.wait()
 
@@ -360,6 +511,7 @@
             pltpu.SemaphoreType.DMA((net.count,)),
             pltpu.SemaphoreType.DMA((net.count,)),
             pltpu.SemaphoreType.DMA((count, 1 + CHUNKS)),
+            pltpu.SemaphoreType.DMA((count, math.prod(sizes[a] for a in SHARES))),
         ],
         cost_estimate=pl.CostEstimate(
             flops=0, bytes_accessed=micros * 3_000_000, transcendentals=0
@@ -370,22 +522,24 @@
     )(*[job.x for job in jobs])
 
 
-def sum_over(term, axis):
+def sum_over(term, axis, outer=1):
     size = lax.axis_size(axis)
     me = lax.axis_index(axis)
+    columns = term.shape[1]
+    term = term.reshape(outer, -1, columns)
     while size > 1:
         size //= 2
-        rows = term.shape[0] // 2
+        rows = term.shape[1] // 2
         pairs = [(i, i ^ size) for i in range(lax.axis_size(axis))]
         side = (me // size) % 2
-        kept = lax.dynamic_slice_in_dim(term, side * rows, rows)
+        kept = lax.dynamic_slice_in_dim(term, side * rows, rows, axis=1)
         other = lax.ppermute(
-            lax.dynamic_slice_in_dim(term, (1 - side) * rows, rows), axis, pairs
+            lax.dynamic_slice_in_dim(term, (1 - side) * rows, rows, axis=1), axis, pairs
         )
         term = kept.astype(F32) + other.astype(F32)
         if size > 1:
             term = term.astype(BF16)
-    return term
+    return term.reshape(-1, columns)
 
 
 def dot(a, b, dims=None):
@@ -402,6 +556,416 @@
 
 def rms_scale(values):
     return lax.rsqrt(jnp.mean(values * values, axis=-1, keepdims=True) + EPS)
+
+
+def attention(q, kv, q_pos, k_pos, scaling):
+    n_slot, n_zh, _, n = k_pos.shape
+    heads = q.shape[1] // HEAD
+
+    def kernel(q_ref, kv_ref, q_pos_ref, k_pos_ref, o_ref, lse_ref):
+        for s in range(n_slot):
+            rows = slice(s * n, (s + 1) * n)
+            for g in range(heads):
+                cols = slice(g * HEAD, (g + 1) * HEAD)
+                scores = []
+                for z in range(n_zh):
+                    score = dot(q_ref[rows, cols], kv_ref[z, rows, :HEAD], COLS_T) * scaling
+                    allowed = k_pos_ref[s, z] <= q_pos_ref[...]
+                    scores.append(jnp.where(allowed, score, -jnp.inf))
+                peak = scores[0].max(axis=1, keepdims=True)
+                for score in scores[1:]:
+                    peak = jnp.maximum(peak, score.max(axis=1, keepdims=True))
+                exps = [jnp.exp(score - peak) for score in scores]
+                total = sum(e.sum(axis=1, keepdims=True) for e in exps)
+                inverse = 1.0 / total
+                o_ref[rows, cols] = sum(
+                    dot((e * inverse).astype(BF16), kv_ref[z, rows, HEAD:])
+                    for z, e in enumerate(exps)
+                ).astype(BF16)
+                lse_ref[s, g] = peak + jnp.log(total)
+
+    vmem = pl.BlockSpec(memory_space=pltpu.VMEM)
+    return pl.pallas_call(
+        kernel,
+        out_shape=[
+            jax.ShapeDtypeStruct(q.shape, BF16),
+            jax.ShapeDtypeStruct((n_slot, heads, n, 1), F32),
+        ],
+        in_specs=[vmem] * 4,
+        out_specs=[vmem] * 2,
+        compiler_params=pltpu.CompilerParams(vmem_limit_bytes=VMEM_LIMIT),
+    )(q, kv, q_pos, k_pos)
+
+
+def attention_back(
+    ga, q, kv, lse, q_pos, k_pos, cos, sin, w_out, w_attn, out_parts, sums, scaling, collective_id
+):
+    net = Net({a: lax.axis_size(a) for a in AXES})
+    own, width = ga.shape
+    n_slot, n_zh, _, n = k_pos.shape
+    n_tok = n_slot * n
+    heads = q.shape[1] // HEAD
+    columns = w_attn.shape[1]
+    half = columns // 2
+    ga_job = NearGather(ga, PAIRED_SLOTS, TO_TEAM_EVEN)
+    gas = Relay(ga_job, 0, net)
+    ga_steps = sorted(gas.steps, key=lambda step: step[0])
+    adder = Adder(TeamSum(out_parts, CHUNKS), 1, net)
+    streams, made = [], []
+    if sums:
+        down, _, gate_half, _, o_half = sums
+        made = [(width, gate_half.shape[2])] * 2 + [(o_half.shape[2], width)]
+        streams = [Stream(net, down.shape, False)]
+        streams += [Stream(net, made[i], i < 2) for i in range(3)]
+    n_chunks = n_zh * CHUNKS
+    kv_wires = [[net.wire({"zh": z}) for z in range(1, n_zh)] for _ in range(n_slot)]
+    half_wires = [net.wire({"c": 1}) for _ in range(n_slot)]
+    y_rows, zl_rows = pl.ds(0, own // 2), pl.ds(own // 2, own // 2)
+    far_wires = net.wire({"y": 1}), net.wire({"zl": 1})
+    near_wires = net.wire({"y": 1}), net.wire({"zl": 1})
+    n_sums = len(sums) if sums else 0
+    n_local = 48
+
+    def kernel(*refs):
+        refs = iter(refs)
+
+        def take(count):
+            return list(itertools.islice(refs, count))
+
+        ga_ref, q_ref, kv_ref, lse_ref, q_pos_ref, k_pos_ref = take(6)
+        cos_ref, sin_ref, wo_ref, wa_ref, parts_ref = take(5)
+        sum_ins = take(n_sums)
+        gas_ref, half_ref, gn1_ref, added_ref = take(4)
+        sum_outs, made_refs = take(len(streams)), take(len(made))
+        gav, wo, wa, go, gkv, gkv_away, gkv_out, gkv_in, g_qkv, gn1, far = take(11)
+        send_sem, recv_sem, local_sem = take(3)
+        adder_scratch = take(3)
+        net.open(send_sem, recv_sem)
+        gas.open(ga_ref, gas_ref)
+        adder.open(parts_ref, added_ref, *adder_scratch)
+        for i, stream in enumerate(streams):
+            stream.open([*sum_ins[:1], *made_refs][i], sum_outs[i], *take(5))
+        used = iter(range(n_local))
+
+        def local(src, dst):
+            cp = pltpu.make_async_copy(src, dst, local_sem.at[next(used)])
+            cp.start()
+            return cp
+
+        plan = []
+        for i in range(len(streams)):
+            for k in range(n_chunks):
+                plan.append((i, k, False))
+                q_chunk = k - (n_chunks - CHUNKS)
+                if i and q_chunk >= 0:
+                    plan.append((i - 1, q_chunk, True))
+        plan += [(i, q_chunk, True) for i in range(len(streams))[-1:] for q_chunk in range(CHUNKS)]
+        issued, merged = [0] * len(streams), [0] * len(streams)
+        ready = [i == 0 for i in range(len(streams))]
+
+        def pump():
+            for i, stream in enumerate(streams):
+                allowed = min(n_chunks, merged[i - 1] + AHEAD) if i else n_chunks
+                while ready[i] and issued[i] < allowed:
+                    stream.issue(issued[i])
+                    issued[i] += 1
+
+        def there(i):
+            if sums:
+                ready[i] = True
+                pump()
+
+        def flow(steps):
+            while plan and steps:
+                i, k, last = plan[0]
+                if last:
+                    streams[i].last(k)
+                elif k < issued[i]:
+                    streams[i].merge(k)
+                    merged[i] += 1
+                    pump()
+                else:
+                    return
+                plan.pop(0)
+                steps -= 1
+
+        if sums:
+            wr, lt, ot, o_v, wr_sem, lt_sem, ot_sem = take(7)
+
+        def product(rhs_ref, term_ref, steps):
+            lhs_ref, n_cols = sum_ins[1], wr.shape[2]
+            n_tiles = width // own
+
+            def lhs(t, slot, c):
+                at = pl.ds(pl.multiple_of(t * own, own), own)
+                return pltpu.make_async_copy(
+                    lhs_ref.at[c, :, at], lt.at[slot, c], lt_sem.at[slot, c]
+                )
+
+            for part in range(rhs_ref.shape[2] // n_cols):
+                window = pl.ds(part * n_cols, n_cols)
+                rhs = [
+                    pltpu.make_async_copy(rhs_ref.at[c, :, window], wr.at[c], wr_sem.at[c])
+                    for c in range(2)
+                ]
+                for c in range(2):
+                    rhs[c].start()
+                    lhs(0, 0, c).start()
+                for c in range(2):
+                    rhs[c].wait()
+
+                def store(t, slot, window=window):
+                    at = pl.ds(pl.multiple_of(t * own, own), own)
+                    return pltpu.make_async_copy(
+                        ot.at[slot], term_ref.at[at, window], ot_sem.at[slot]
+                    )
+
+                def tile(t, _, store=store):
+                    slot = lax.rem(t, 2)
+
+                    @pl.when(t + 1 < n_tiles)
+                    def _():
+                        for c in range(2):
+                            lhs(t + 1, 1 - slot, c).start()
+
+                    for c in range(2):
+                        lhs(t, slot, c).wait()
+
+                    @pl.when(t >= 2)
+                    def _():
+                        store(t - 2, slot).wait()
+
+                    value = dot(lt[slot].reshape(2 * n_tok, own), wr[...].reshape(2 * n_tok, n_cols), ROWS_T)
+                    ot[slot] = value.astype(BF16)
+                    store(t, slot).start()
+                    return 0
+
+                lax.fori_loop(0, n_tiles, tile, 0)
+                store(n_tiles - 2, n_tiles % 2).wait()
+                store(n_tiles - 1, 1 - n_tiles % 2).wait()
+                flow(steps)
+
+        for _, _, hops, *what in ga_steps:
+            if not hops:
+                gas.run(hops, *what)
+        if sums:
+            pump()
+            got_o = local(sum_ins[4], o_v)
+        got_wo, got_wa = local(wo_ref, wo), local(wa_ref, wa)
+        got_ga = local(ga_ref, gav.at[0, 0])
+        got_ga.wait()
+        kept = [local(ga_job.cut(gav.at[0, 0], p), gas.own(p)) for p in range(CHUNKS)]
+        got_wo.wait()
+        got_wa.wait()
+        if sums:
+            product(sum_ins[2], made_refs[0], 1)
+            there(1)
+
+        def turn_back(t, rows):
+            h = HEAD // 2
+            c, sn = cos_ref[rows], sin_ref[rows]
+            front, back = t[:, :h], t[:, h:]
+            return jnp.concatenate([front * c + back * sn, back * c - front * sn], axis=1).astype(
+                BF16
+            )
+
+        def slot(s):
+            keys = slice(s * n, (s + 1) * n)
+            for j in range(2):
+                at = pl.ds(s * n + j * own, own)
+                go[at, :] = dot(gav[s, j], wo[...], COLS_T).astype(BF16)
+            for turn, (g, j) in enumerate(itertools.product(range(heads), range(n // own))):
+                rows = slice(s * n + j * own, s * n + (j + 1) * own)
+                here = slice(j * own, (j + 1) * own)
+                cols = slice(g * HEAD, (g + 1) * HEAD)
+                q_g, go_g, lse_g = q_ref[rows, cols], go[rows, cols], lse_ref[s, g, here]
+                probs, gps = [], []
+                for z in range(n_zh):
+                    score = dot(q_g, kv_ref[z, keys, :HEAD], COLS_T) * scaling
+                    allowed = k_pos_ref[s, z] <= q_pos_ref[here]
+                    probs.append(jnp.where(allowed, jnp.exp(score - lse_g), 0.0))
+                    gps.append(dot(go_g, kv_ref[z, keys, HEAD:], COLS_T))
+                delta = sum((p * gp).sum(axis=1, keepdims=True) for p, gp in zip(probs, gps))
+                gq = 0.0
+                for z in range(n_zh):
+                    gs = (probs[z] * (gps[z] - delta)).astype(BF16)
+                    gq += dot(gs, kv_ref[z, keys, :HEAD])
+                    gk = dot(gs, q_g, ROWS_T) * scaling
+                    gv = dot(probs[z].astype(BF16), go_g, ROWS_T)
+                    total = gkv_away.at[z - 1] if z else gkv.at[s]
+                    if turn:
+                        gk, gv = gk + total[:, :HEAD], gv + total[:, HEAD:]
+                    total[:, :HEAD] = gk
+                    total[:, HEAD:] = gv
+                g_qkv[rows, cols] = turn_back(gq * scaling, rows)
+            sent = []
+            for z in range(n_zh - 1):
+                gkv_out[s, z] = gkv_away[z].astype(BF16)
+                sent.append(net.send(gkv_out.at[s, z], gkv_in.at[s, z], kv_wires[s][z]))
+            return sent
+
+        def keys(s, sent):
+            rows = slice(s * n, (s + 1) * n)
+            q_cols = heads * HEAD
+            mine = gkv[s]
+            for z, cp in enumerate(sent):
+                cp.wait_recv()
+                mine = mine + gkv_in[s, z].astype(F32)
+            g_qkv[rows, q_cols : q_cols + HEAD] = turn_back(mine[:, :HEAD], rows)
+            g_qkv[rows, q_cols + HEAD :] = mine[:, HEAD:].astype(BF16)
+            away = pl.ds(pl.multiple_of((1 - net.here["c"]) * half, half), half)
+            here = pl.ds(pl.multiple_of(net.here["c"] * half, half), half)
+            window = pl.ds(s * n, n)
+            halves.append(
+                net.send(g_qkv.at[window, away], half_ref.at[1, window], half_wires[s])
+            )
+            kept.append(local(g_qkv.at[window, here], half_ref.at[0, window]))
+
+        def term(r):
+            def tile(t, _):
+                at = pl.ds(pl.multiple_of(t * TILE, TILE), TILE)
+                value = dot(g_qkv[r * own : (r + 1) * own], wa[at, :], COLS_T)
+                gn1[r, :, at] = value.astype(BF16)
+                return 0
+
+            lax.fori_loop(0, width // TILE, tile, 0)
+
+        def add(r, window):
+            gn1[r, window] = (gn1[r, window].astype(F32) + far[window].astype(F32)).astype(BF16)
+
+        def add_out(hops):
+            for _, _, at, *what in sorted(adder.steps, key=lambda step: step[0]):
+                if at == hops:
+                    adder.run(at, *what)
+
+        halves, late, arrived, sent = [], [], set(), {}
+        for _, _, hops, part, off, sends in ga_steps:
+            if not hops:
+                continue
+            if off["c"]:
+                late.append((hops, part, off, sends))
+                continue
+            gas.run(hops, part, off, sends)
+            if part == CHUNKS - 1:
+                i, j = off["y"], off["zl"]
+                local(gas_ref.at[0, i, j], gav.at[i, j]).wait()
+                arrived.add((i, j))
+                if arrived >= {(0, 1), (1, 0)} and 0 not in sent:
+                    flow(2)
+                    sent[0] = slot(0)
+                    flow(1)
+        flow(1)
+        sent[1] = slot(1)
+        add_out(0)
+        flow(2)
+        if sums:
+            product(sum_ins[3], made_refs[1], 2)
+            there(2)
+        keys(0, sent[0])
+        term(1)
+        term(0)
+        add_out(1)
+        flow(4)
+        keys(1, sent[1])
+        term(3)
+        to_far = (
+            net.send(gn1.at[3, y_rows], far.at[y_rows], far_wires[0]),
+            net.send(gn1.at[3, zl_rows], far.at[zl_rows], far_wires[1]),
+        )
+        term(2)
+        kept_gn1 = local(gn1.at[0], gn1_ref.at[0])
+        flow(2)
+        to_far[1].wait_recv()
+        add(2, zl_rows)
+        to_y = net.send(gn1.at[2], gn1_ref.at[1], near_wires[0])
+        to_far[0].wait_recv()
+        add(1, y_rows)
+        to_zl = net.send(gn1.at[1], gn1_ref.at[2], near_wires[1])
+        for hops, part, off, sends in late:
+            gas.run(hops, part, off, sends)
+        flow(2)
+        if sums:
+            for cp in (*to_far, to_y, to_zl):
+                net.settle(cp)
+            kept_gn1.wait()
+            got_o.wait()
+            others = [
+                local(gas_ref.at[1, i, j], gn1.at[2 * i + j]) for i in range(2) for j in range(2)
+            ]
+            for cp in others:
+                cp.wait()
+
+            def output(t, _):
+                at = pl.ds(pl.multiple_of(t * TILE, TILE), TILE)
+                value = dot(o_v[0], gav[:, :, :, at].reshape(n_tok, TILE), ROWS_T)
+                value += dot(o_v[1], gn1[:, :, at].reshape(n_tok, TILE), ROWS_T)
+                far[:, at] = value.astype(BF16)
+                return 0
+
+            lax.fori_loop(0, width // TILE, output, 0)
+            local(far, made_refs[2]).wait()
+            there(3)
+        else:
+            kept_gn1.wait()
+        flow(100)
+        assert not plan
+        for cp in halves + [to_y, to_zl]:
+            cp.wait_recv()
+        adder.finish()
+        net.close()
+        for stream in streams:
+            stream.close()
+        for cp in kept:
+            cp.wait()
+
+    shape = jax.ShapeDtypeStruct
+    vmem, hbm = pl.BlockSpec(memory_space=pltpu.VMEM), pl.BlockSpec(memory_space=pl.ANY)
+    scratch = [
+        pltpu.VMEM((2, 2, own, width), BF16),
+        pltpu.VMEM(w_out.shape, BF16),
+        pltpu.VMEM(w_attn.shape, BF16),
+        pltpu.VMEM((n_tok, heads * HEAD), BF16),
+        pltpu.VMEM((n_slot, n, 2 * HEAD), F32),
+        pltpu.VMEM((n_zh - 1, n, 2 * HEAD), F32),
+        pltpu.VMEM((n_slot, n_zh - 1, n, 2 * HEAD), BF16),
+        pltpu.VMEM((n_slot, n_zh - 1, n, 2 * HEAD), BF16),
+        pltpu.VMEM((n_tok, columns), BF16),
+        pltpu.VMEM((4, own, width), BF16),
+        pltpu.VMEM((own, width), BF16),
+        pltpu.SemaphoreType.DMA((net.count,)),
+        pltpu.SemaphoreType.DMA((net.count,)),
+        pltpu.SemaphoreType.DMA((n_local,)),
+        *adder.scratch(),
+    ]
+    for stream in streams:
+        scratch += stream.scratch()
+    if sums:
+        scratch += [
+            pltpu.VMEM((2, n_tok, TILE), BF16),
+            pltpu.VMEM((2, 2, n_tok, own), BF16),
+            pltpu.VMEM((2, own, TILE), BF16),
+            pltpu.VMEM(o_half.shape, BF16),
+            pltpu.SemaphoreType.DMA((2,)),
+            pltpu.SemaphoreType.DMA((2, 2)),
+            pltpu.SemaphoreType.DMA((2,)),
+        ]
+    return pl.pallas_call(
+        kernel,
+        out_shape=[
+            shape((2, 2, 2, own, width), BF16),
+            shape((2, n_tok, half), BF16),
+            shape((3, own, width), BF16),
+            shape((2, own, width), BF16),
+            *[stream.shape() for stream in streams],
+            *[shape(dims, BF16) for dims in made],
+        ],
+        in_specs=[hbm] + [vmem] * 7 + [hbm] * (3 + n_sums),
+        out_specs=[hbm] * (4 + len(streams) + len(made)),
+        scratch_shapes=scratch,
+        compiler_params=pltpu.CompilerParams(
+            collective_id=collective_id, has_side_effects=True, vmem_limit_bytes=FFN_VMEM_LIMIT
+        ),
+    )(ga, q, kv, lse, q_pos, k_pos, cos, sin, w_out, w_attn, out_parts, *(sums or ()))
 
 
 def positions(members):
@@ -653,23 +1217,25 @@
     def by_team(w):
         return w.reshape(rows, team, -1).transpose(1, 0, 2)
 
-    def ff_by_team(w):
+    def ff_cut(w):
+        if ff_rows % 128 == 0:
+            return ColumnSwap(w, ff_rows)
         cut = w.reshape(rows, *(size[a] for a in AXES), ff_rows)
-        return cut.transpose(2, 3, 0, 5, 4, 1, 6).reshape(team, rows, ff)
+        return Swap(cut.transpose(2, 3, 0, 5, 4, 1, 6).reshape(team, rows, ff), TEAM)
 
     attn_cut = jnp.concatenate(
         [by_team(query_weight), by_team(key_matrix), by_team(value_matrix)], axis=2
     )
-    tile = jnp.zeros((8, 128), F32)
-    tile = tile.at[0, :rows].set(attn_gain.astype(F32))
-    tile = tile.at[0, 64 : 64 + rows].set(ffn_gain.astype(F32))
-    tile = tile.at[1].set(lengths[0].astype(F32))
+    row = [jnp.pad(gain.astype(F32), (0, 64 - rows)) for gain in (attn_gain, ffn_gain)]
+    tile = jnp.concatenate(
+        [jnp.concatenate(row)[None], jnp.full((7, 128), lengths[0].astype(F32))]
+    )
     tiles, attn_part, gate_part, up_part = exchange(
         [
-            Gather(tile, AXES, [("c", "x", "y", "zl", "zh")], rank=0),
+            Gather(tile, AXES, [(("c", "x", "y"), ("zl", "zh"))], rank=0),
             Swap(attn_cut, TEAM),
-            Swap(ff_by_team(gate_weight), TEAM),
-            Swap(ff_by_team(up_weight), TEAM),
+            ff_cut(gate_weight),
+            ff_cut(up_weight),
         ],
         1,
     )
@@ -696,32 +1262,29 @@
     def row_gather(part):
         return RowGather(part, None, [OUTWARD] * team)
 
-    def spread(v):
-        cut = v.reshape(own, size["zh"], size["zl"], size["y"], size["x"], size["c"] * rows)
-        return cut.transpose(0, 4, 1, 2, 3, 5).reshape(own, width)
-
-    def natural(v):
-        cut = v.reshape(own, size["x"], size["zh"], size["zl"], size["y"], size["c"] * rows)
-        return cut.transpose(0, 2, 3, 4, 1, 5).reshape(own, width)
-
     my_pos = positions((at["zh"] * size["zl"] + at["zl"])[None])
     valid = (my_pos < lengths[0]).astype(F32)[:, None]
     near_zl = at["zl"] ^ jnp.arange(2)
     near_zh = (at["zh"] + jnp.arange(size["zh"])) % size["zh"]
     q_pos = positions(at["zh"] * 2 + near_zl)
+    n_q = q_pos.shape[0]
     k_pos = positions((near_zh[:, None] * 2 + near_zl[None, :]).reshape(-1))
+    past = size["zh"] * n_q
+    k_pos = jnp.where(k_pos[None] < lens[:, None], k_pos[None], past)
+    k_pos = k_pos.reshape(2, size["zh"], 1, n_q)
     half = HEAD // 2
     freq = ROPE_BASE ** (-2.0 * jnp.arange(half).astype(F32) / HEAD)
     angles = q_pos.astype(F32)[:, None] * freq[None, :]
-    cos = jnp.tile(jnp.cos(angles), (size["y"], 1))[:, None, :]
-    sin = jnp.tile(jnp.sin(angles), (size["y"], 1))[:, None, :]
+    q_pos = q_pos[:, None]
+    cos = jnp.tile(jnp.cos(angles), (size["y"], 1))
+    sin = jnp.tile(jnp.sin(angles), (size["y"], 1))
 
     tokens = inputs.reshape(own, width).astype(F32)
     scale_one = rms_scale(tokens)
     norm_one = (tokens * scale_one * gain_one).astype(BF16)
     norm_one_pair, w_attn, w_out = exchange(
         [
-            NearGather(spread(norm_one), PAIRED_SLOTS, TO_TEAM),
+            NearGather(norm_one, PAIRED_SLOTS, TO_TEAM),
             row_gather(attn_part),
             Gather(out_part, SHARES, [OUTWARD] * (rows // 16)),
         ],
@@ -731,10 +1294,11 @@
     w_attn = w_attn.reshape(width, -1)
     w_out = w_out.reshape(q_cols, width)
     qkv = dot(norm_one_pair[0], w_attn)
-    q = rotate(qkv[:, :q_cols].reshape(n_tok, heads, HEAD), cos, sin).astype(BF16)
-    k = rotate(qkv[:, q_cols : q_cols + kv_cols].reshape(n_tok, 1, HEAD), cos, sin).astype(BF16)
-    v = qkv[:, q_cols + kv_cols :].astype(BF16)
-    kv = jnp.concatenate([k.reshape(n_tok, kv_cols), v], axis=1)
+    turned = [
+        rotate(qkv[:, h * HEAD : (h + 1) * HEAD], cos, sin).astype(BF16) for h in range(heads + 1)
+    ]
+    q = jnp.concatenate(turned[:heads], axis=1)
+    kv = jnp.concatenate([turned[heads], qkv[:, q_cols + kv_cols :].astype(BF16)], axis=1)
     gy = valid * cotangent.reshape(own, width).astype(F32)
     kv_all, gd_pair = exchange(
         [
@@ -743,23 +1307,7 @@
         ],
         3,
     )
-    n_slot = size["y"]
-    n_q = n_tok // n_slot
-    q = q.reshape(n_slot, n_q, heads, HEAD)
-    kv_all = kv_all.reshape(size["zh"], n_slot, n_q, 2 * kv_cols).transpose(1, 0, 2, 3)
-    kv_all = kv_all.reshape(n_slot, size["zh"] * n_q, 2 * kv_cols)
-    k_all, v_all = kv_all[:, :, :kv_cols], kv_all[:, :, kv_cols:]
-    allowed = (k_pos[None, None, :] <= q_pos[None, :, None]) & (
-        k_pos[None, None, :] < lens[:, None, None]
-    )
-    scores = jnp.einsum("bqgd,bkd->bgqk", q, k_all, preferred_element_type=F32) * scaling
-    scores = jnp.where(allowed[:, None], scores, -jnp.inf)
-    peak = jnp.max(scores, axis=-1, keepdims=True)
-    exps = jnp.exp(scores - peak)
-    prob = exps / jnp.sum(exps, axis=-1, keepdims=True)
-    prob_b = prob.astype(BF16)
-    o = jnp.einsum("bgqk,bkd->bqgd", prob_b, v_all, preferred_element_type=F32)
-    o = o.reshape(n_tok, q_cols).astype(BF16)
+    o, lse = attention(q, kv_all, q_pos, k_pos, scaling)
 
     o_parts = dot(o, w_out).astype(BF16).reshape(2, 2, own, width)
     o_added, w_gate, o_half = exchange(
@@ -773,76 +1321,53 @@
     scale_two = rms_scale(h1)
     norm_two = (h1 * scale_two * gain_two).astype(BF16)
     norm_two_pair, gate_half, up_half, mixed_half, gn2_terms, out_parts = feed_forward(
-        spread(norm_two), gd_pair, w_gate, w_down, up_part, 5
+        norm_two, gd_pair, w_gate, w_down, up_part, 5
     )
     norm_two_pair = norm_two_pair.reshape(2, n_tok, width)
     gd_pair = gd_pair.reshape(2, n_tok, width)
-    gn2 = natural(added(gn2_terms[0], gn2_terms[1:])) * gain_two
+    gn2 = added(gn2_terms[0], gn2_terms[1:]) * gain_two
     gh1 = gy + scale_two * gn2 - h1 * scale_two**3 * jnp.mean(h1 * gn2, axis=-1, keepdims=True)
 
-    tie = lax.optimization_barrier
     down_term = dot(mixed_half, gd_pair, PAIR_ROWS_T).astype(BF16)
-    gate_term = dot(norm_two_pair, gate_half, PAIR_ROWS_T).astype(BF16)
-    up_term = dot(norm_two_pair, up_half, PAIR_ROWS_T).astype(BF16)
-    ga, down_term, gate_term, up_term = tie((gh1.astype(BF16), down_term, gate_term, up_term))
-    down_x = sum_over(down_term, "x").astype(BF16)
-    (ga_pair,) = exchange([NearGather(ga, PAIRED_SLOTS, TO_TEAM_EVEN)], 8)
-    ga_pair, down_x, gate_term = tie((ga_pair, down_x, gate_term))
-    gate_x = sum_over(gate_term, "x").astype(BF16)
-    down_grad = sum_over(down_x, "zh")
-    ga_pair = ga_pair.reshape(2, n_tok, width)
-
-    go = dot(ga_pair[0], w_out, COLS_T).astype(BF16).reshape(n_slot, n_q, heads, HEAD)
-    gp = jnp.einsum("bqgd,bkd->bgqk", go, v_all, preferred_element_type=F32)
-    delta = jnp.sum(prob * gp, axis=-1, keepdims=True)
-    gs = (prob * (gp - delta)).astype(BF16)
-    gq_rot = jnp.einsum("bgqk,bkd->bqgd", gs, k_all, preferred_element_type=F32) * scaling
-    gk_rot = jnp.einsum("bgqk,bqgd->bkd", gs, q, preferred_element_type=F32) * scaling
-    gv_sum = jnp.einsum("bgqk,bqgd->bkd", prob_b, go, preferred_element_type=F32)
-    gkv = jnp.concatenate([gk_rot, gv_sum], axis=-1).astype(BF16)
-    gkv = gkv.reshape(n_slot, size["zh"], n_q, 2 * kv_cols).transpose(1, 0, 2, 3)
-    gkv = gkv.reshape(size["zh"], n_tok, 2 * kv_cols)
-    out_term = dot(o_half, ga_pair, PAIR_ROWS_T).astype(BF16)
-    gkv, gate_x, down_grad, up_term, out_term = tie(
-        (gkv, gate_x, down_grad, up_term, out_term)
+    pairs = size["x"] == size["zh"] == 2
+    sums = (down_term, norm_two_pair, gate_half, up_half, o_half) if pairs else None
+    ga_pair, g_qkv_half, gn1_terms, out_added, *totals = attention_back(
+        gh1.astype(BF16), q, kv_all, lse, q_pos, k_pos, cos, sin, w_out, w_attn, out_parts, sums,
+        scaling, 8,
     )
-    up_x = sum_over(up_term, "x").astype(BF16)
-    out_x = sum_over(out_term, "x").astype(BF16)
-    gate_sum = sum_over(gate_x, "zh").astype(BF16)
-    gkv_parts, out_added = exchange([NearSwap(gkv, ("zh",)), TeamSum(out_parts, 4)], 9)
-    gkv_parts, up_x, out_x, gate_sum = tie((gkv_parts, up_x, out_x, gate_sum))
-    gkv = sum(gkv_parts[i].astype(F32) for i in range(size["zh"]))
-    gq = rotate(gq_rot.reshape(n_tok, heads, HEAD), cos, -sin).astype(BF16)
-    gk = rotate(gkv[:, :kv_cols].reshape(n_tok, 1, HEAD), cos, -sin).astype(BF16)
-    g_qkv = jnp.concatenate(
-        [gq.reshape(n_tok, q_cols), gk.reshape(n_tok, kv_cols), gkv[:, kv_cols:].astype(BF16)],
-        axis=1,
-    )
-    cols = g_qkv.shape[1] // 2
-    mine = lax.dynamic_slice_in_dim(g_qkv, at["c"] * cols, cols, axis=1)
-    other = lax.dynamic_slice_in_dim(g_qkv, (1 - at["c"]) * cols, cols, axis=1)
-    g_qkv_half = jnp.stack([mine, lax.ppermute(other, "c", [(0, 1), (1, 0)])])
-    attn_term = dot(norm_one_pair, g_qkv_half, PAIR_ROWS_T).astype(BF16)
-    gn1_parts = dot(g_qkv, w_attn, COLS_T).astype(BF16).reshape(2, 2, own, width)
-    gn1_parts, attn_term, up_x, out_x = tie((gn1_parts, attn_term, up_x, out_x))
-    attn_x = sum_over(attn_term, "x").astype(BF16)
-    up_sum = sum_over(up_x, "zh").astype(BF16)
-    out_sum = sum_over(out_x, "zh").astype(BF16)
-    (gn1_added,) = exchange([TeamSum(gn1_parts, 4)], 10)
-    gn1_added, attn_x, up_sum, out_sum = tie((gn1_added, attn_x, up_sum, out_sum))
-    attn_sum = sum_over(attn_x, "zh")
-    out_sum = lax.ppermute(out_sum, AXES, [(b, a) for a, b in homes])
     outputs = valid * (h1 + added(out_parts[0, 0], out_added))
     outputs = outputs.astype(BF16).reshape(inputs.shape)
+    attn_term = dot(norm_one_pair, g_qkv_half, PAIR_ROWS_T).astype(BF16)
     n_owners = math.prod(size[a] for a in OWNERS)
 
     def by_owner(total):
-        return total.astype(BF16).reshape(n_owners, rows, -1)
-
-    gate_sum, up_sum = exchange([Swap(by_owner(t), OWNERS) for t in (gate_sum, up_sum)], 11)
-    attn_sum, gate_sum, up_sum = tie((attn_sum, gate_sum, up_sum))
-    (attn_sum,) = exchange([Swap(by_owner(attn_sum), OWNERS)], 12)
-    gn1 = natural(added(gn1_parts[0, 0], gn1_added)) * gain_one
+        return Swap(total.astype(BF16).reshape(n_owners, rows, -1), OWNERS)
+
+    homeward = [(b, a) for a, b in homes]
+    if pairs:
+        down_grad, gate_sum, up_sum, out_sum = totals[:4]
+        output_grad = lax.ppermute(out_sum, AXES, homeward)
+        attn_sum, gate_sum, up_sum = exchange(
+            [PeerSum(attn_term, True), by_owner(gate_sum), by_owner(up_sum)], 9
+        )
+        attn_sum, output_grad = lax.optimization_barrier((attn_sum, output_grad))
+        (attn_sum,) = exchange([by_owner(attn_sum)], 10, micros=10)
+    else:
+        outer = size["zh"] * team
+
+        def sum_peers(term, outer=1):
+            return sum_over(sum_over(term, "x", outer).astype(BF16), "zh").astype(BF16)
+
+        gate_term = dot(norm_two_pair, gate_half, PAIR_ROWS_T).astype(BF16)
+        up_term = dot(norm_two_pair, up_half, PAIR_ROWS_T).astype(BF16)
+        out_term = dot(o_half, ga_pair.reshape(2, n_tok, width), PAIR_ROWS_T).astype(BF16)
+        down_grad = sum_peers(down_term)
+        output_grad = lax.ppermute(sum_peers(out_term), AXES, homeward)
+        terms = (attn_term, gate_term, up_term)
+        attn_sum, gate_sum, up_sum = exchange(
+            [by_owner(sum_peers(term, outer)) for term in terms], 9
+        )
+    gn1 = added(gn1_terms[0], gn1_terms[1:]) * gain_one
     g_tokens = (
         gh1
         + scale_one * gn1
@@ -850,33 +1375,42 @@
     )
     input_grad = g_tokens.astype(BF16).reshape(inputs.shape)
 
-    def ff_natural(total):
-        cut = total.reshape(
-            size["zl"], size["y"], size["c"], rows, size["x"], size["zh"], ff_rows
+    if ff_rows % 128 == 0:
+        (query_grad, key_grad, value_grad, gate_grad, up_grad, attn_against, ffn_against) = finish(
+            (attn_sum, gate_sum, up_sum),
+            (query_weight, key_matrix, value_matrix, gate_weight, up_weight),
+            ff_rows,
         )
-        return cut.transpose(3, 5, 0, 1, 4, 2, 6).reshape(rows, -1).astype(F32)
-
-    def side(part):
-        return part.transpose(1, 0, 2).reshape(rows, -1).astype(F32)
-
-    attn_sum = attn_sum.reshape(team, 2, rows, -1)
-    query_grad = side(attn_sum[:, 0])
-    key_grad = side(attn_sum[:, 1, :, :kv_cols])
-    value_grad = side(attn_sum[:, 1, :, kv_cols:])
-    gate_grad = ff_natural(gate_sum)
-    up_grad = ff_natural(up_sum)
-
-    def against(w, g):
-        return jnp.sum(w.astype(F32) * g, axis=1)
-
-    attn_gain_grad = (
-        against(query_weight, query_grad)
-        + against(key_matrix, key_grad)
-        + against(value_matrix, value_grad)
-    ) / attn_gain.astype(F32)
-    ffn_gain_grad = (against(gate_weight, gate_grad) + against(up_weight, up_grad)) / (
-        ffn_gain.astype(F32)
-    )
+        attn_against, ffn_against = attn_against[:, 0], ffn_against[:, 0]
+    else:
+
+        def ff_natural(total):
+            cut = total.reshape(
+                size["zl"], size["y"], size["c"], rows, size["x"], size["zh"], ff_rows
+            )
+            return cut.transpose(3, 5, 0, 1, 4, 2, 6).reshape(rows, -1).astype(F32)
+
+        def side(part):
+            return part.transpose(1, 0, 2).reshape(rows, -1).astype(F32)
+
+        attn_sum = attn_sum.reshape(team, 2, rows, -1)
+        query_grad = side(attn_sum[:, 0])
+        key_grad = side(attn_sum[:, 1, :, :kv_cols])
+        value_grad = side(attn_sum[:, 1, :, kv_cols:])
+        gate_grad = ff_natural(gate_sum)
+        up_grad = ff_natural(up_sum)
+
+        def against(w, g):
+            return jnp.sum(w.astype(F32) * g, axis=1)
+
+        attn_against = (
+            against(query_weight, query_grad)
+            + against(key_matrix, key_grad)
+            + against(value_matrix, value_grad)
+        )
+        ffn_against = against(gate_weight, gate_grad) + against(up_weight, up_grad)
+    attn_gain_grad = attn_against / attn_gain.astype(F32)
+    ffn_gain_grad = ffn_against / ffn_gain.astype(F32)
     return (
         outputs,
         input_grad,
@@ -884,12 +1418,59 @@
         query_grad,
         key_grad,
         value_grad,
-        out_sum.astype(F32),
+        output_grad.astype(F32),
         ffn_gain_grad,
         gate_grad,
         up_grad,
-        down_grad,
+        down_grad.astype(F32),
     )
+
+
+def finish(sums, weights, block):
+    sizes = {a: lax.axis_size(a) for a in AXES}
+    rows = weights[0].shape[0]
+    members = offsets(sizes, OWNERS)
+    shares = offsets(sizes, ("x", "zh"))
+
+    def kernel(
+        attn, gate, up, wq, wk, wv, wg, wu, gq, gk, gv, gg, gu, attn_total, ffn_total
+    ):
+        totals = []
+
+        def put(value, out, weight, start):
+            value = value.astype(F32)
+            width = value.shape[1]
+            out[:, start : start + width] = value
+            totals.append(
+                jnp.sum(weight[:, start : start + width].astype(F32) * value, axis=1, keepdims=True)
+            )
+
+        q_width, kv_width = gq.shape[1] // 4, gk.shape[1] // 4
+        for i, owner in enumerate(members):
+            f = place(owner, TEAM, sizes)
+            if owner["c"] == 0:
+                put(attn[i], gq, wq, f * q_width)
+            else:
+                put(attn[i, :, :kv_width], gk, wk, f * kv_width)
+                put(attn[i, :, kv_width:], gv, wv, f * kv_width)
+        attn_total[...] = sum(totals)
+        totals.clear()
+        for i, owner in enumerate(members):
+            for n, share in enumerate(shares):
+                start = place({**owner, **share}, AXES, sizes) * block
+                window = slice(n * block, (n + 1) * block)
+                put(gate[i, :, window], gg, wg, start)
+                put(up[i, :, window], gu, wu, start)
+        ffn_total[...] = sum(totals)
+
+    shape = jax.ShapeDtypeStruct
+    return pl.pallas_call(
+        kernel,
+        out_shape=[shape(w.shape, F32) for w in weights] + [shape((rows, 1), F32)] * 2,
+        in_specs=[pl.BlockSpec(memory_space=pltpu.VMEM)] * 8,
+        out_specs=[pl.BlockSpec(memory_space=pltpu.VMEM)] * 7,
+        compiler_params=pltpu.CompilerParams(vmem_limit_bytes=VMEM_LIMIT),
+    )(*sums, *weights)
 
 
 def solution(mesh):

time: 1040 us -> 802 us (0.77)
  local copies, waits for them, and re-layouts: 148 us -> 19.1 us
  other arithmetic: 94 us -> 27.5 us
  Pallas kernels: 631 us -> 697 us
  matrix products: 87.9 us -> 31.7 us
  waiting for transfers between devices: 41.5 us -> 0.69 us
    pallas_call x0 -> x3, Pallas kernels: none -> 260 us  [the longest x1 253 us: attention_back(): pl.pallas_call(kernel, out_shape=[shape((2, 2, 2, own, width), BF16), sha...]
    pallas_call x9 -> x6, Pallas kernels: 503 us -> 309 us  [exchange(): pl.pallas_call(kernel, out_shape=[jax.ShapeDtypeStruct(job.shape(sizes),...]
    convert_element_type x18 -> x0, local copies, waits for them, and re-layouts: 51 us -> none  [the longest x6 23 us: added(): return term.astype(F32) + others[0].astype(F32) + others[1].astype(F32)]
    ppermute x12 -> x1, waiting for transfers between devices: 40.8 us -> 0.01 us  [on_device(): output_grad = lax.ppermute(out_sum, AXES, homeward)]
    dot_general x7 -> x2, matrix products: 53.9 us -> 22.9 us  [dot(): return lax.dot_general(a, b, dims, preferred_element_type=F32)]
    reshape x13 -> x0, local copies, waits for them, and re-layouts: 30.5 us -> none  [the longest x3 11.9 us: natural(): return cut.transpose(0, 2, 3, 4, 1, 5).reshape(own, width)]
    dot_general x6 -> x0, matrix products: 25 us -> none  [the longest x1 7.22 us: on_device(): gp = jnp.einsum('bqgd,bkd->bgqk', go, v_all, preferred_element_type=F32)]
    convert_element_type x11 -> x6, other arithmetic: 25.4 us -> 7.07 us  [the longest x1 1.84 us: on_device(): norm_two = (h1 * scale_two * gain_two).astype(BF16)]
  transfers between devices with their start and end apart: 14 -> 3, of which waited for: 2 -> 0; matrix products, arithmetic and copies ran while one was open for 16% -> 5% of each run, Pallas kernels for 47% -> 38%
where the time goes in v4:
time: 802 us; the launch traced here: 794 us
  Pallas kernels  697 us (87%)
  matrix products  31.7 us (4%)
  other arithmetic  27.5 us (3%)
  local copies, waits for them, and re-layouts  19.1 us (2%)
  between operations  15.6 us (2%)
    pallas_call x6, Pallas kernels, exchange(): pl.pallas_call(kernel, out_shape=[jax.ShapeDtypeStruct(job.shape(sizes),...  309 us
    pallas_call x1, Pallas kernels, attention_back(): pl.pallas_call(kernel, out_shape=[shape((2, 2, 2, own, width), BF16), sha...  253 us
    pallas_call x1, Pallas kernels, feed_forward(): pl.pallas_call(kernel, out_shape=[shape((2, 2, 2, own, width), BF16), *[s...  128 us
    dot_general x2, matrix products, dot(): return lax.dot_general(a, b, dims, preferred_element_type=F32)  22.9 us
  transfers between devices with their start and end apart: 3, of which 0 were waited for; matrix products, arithmetic and copies ran while one was open for 5% of the time, Pallas kernels for 38%

profile of v4, /device:TPU:0, one launch (start us, length us, event | category | flops | bytes accessed | tf_op | source)
XLA Modules:
  0.0 793.7 jit_solution(18122001391044707526)
XLA Ops:
  7.9 1.6 collective-permute-start
  11.5 1.0 copy.55
  12.6 1.0 bitcast_bitcast_fusion.1
  13.6 61.1 %shard_map.203 = (f32[32,8,128]{2,1,0:T(8,128)S(1)}, bf16[4,64,1024]{2,1,0:T(8,128)(2,1)S(1)}, bf16[4,64,2048]{2,1,0:T(8,128)(2,1)S(1)}, bf16[4,64,2048]{2,1,0:T(8,128)(2,1)S(1)}) custom-call(f32[8,128]{1,0:T(8,128)S(1)} %concatenate.27.refs_0_, bf16[4,64,1024]{2,1,0:T(8,128)(2,1)S(1)} %pad_maximum_fusion.2.refs_1_, bf16[64,8192]{1,0:T(8,128)(2,1)S(1)} %copy-done.4, ...), custom_call_target="tpu_custom_call" | custom-call | bytes 150000000 | tf_op jit(solution)/shard_map/pallas_call | solution.py:504
  75.7 1.0 copy-done.17
  78.2 1.5 fusion.8
  80.3 1.5 fusion.14.refs_0_
  82.1 1.0 multiply_cosine_fusion
  83.1 68.1 %shard_map.204 = (bf16[2,2,2,256,2048]{4,3,2,1,0:T(8,128)(2,1)}, bf16[2048,1024]{1,0:T(8,128)(2,1)}, bf16[8,64,2048]{2,1,0:T(8,128)(2,1)S(1)}) custom-call(bf16[256,2048]{1,0:T(8,128)(2,1)S(1)} %fusion.14.refs_0_, bf16[4,64,1024]{2,1,0:T(8,128)(2,1)S(1)} %get-tuple-element.51.refs_1_, bf16[64,2048]{1,0:T(8,128)(2,1)S(1)} %collective-permute-done.refs_2_), custom_call_target="tpu_custom_call" | custom-call | bytes 150000000 | tf_op jit(solution)/shard_map/pallas_call | solution.py:504
  151.2 3.6 slice.87
  155.4 4.5 fusion.40
  160.6 66.8 %shard_map.205 = (bf16[2,1024,512]{2,1,0:T(8,128)(2,1)S(1)}, bf16[2,2,2,256,2048]{4,3,2,1,0:T(8,128)(2,1)}) custom-call(bf16[1024,512]{1,0:T(8,128)(2,1)S(1)} %pad_maximum_fusion.1.refs_0_, bf16[256,2048]{1,0:T(8,128)(2,1)S(1)} %fusion.15.refs_1_), custom_call_target="tpu_custom_call" | custom-call | bytes 150000000 | tf_op jit(solution)/shard_map/pallas_call | solution.py:504
  227.5 4.4 shard_map.206
  232.0 4.3 convolution_convert_fusion
  236.3 62.7 %shard_map.207 = (bf16[2,256,2048]{2,1,0:T(8,128)(2,1)S(1)}, bf16[2048,2048]{1,0:T(8,128)(2,1)}, bf16[2,1024,256]{2,1,0:T(8,128)(2,1)S(1)}) custom-call(bf16[2,2,256,2048]{3,2,1,0:T(8,128)(2,1)} %bitcast.180, bf16[4,64,2048]{2,1,0:T(8,128)(2,1)S(1)} %copy-done.14, bf16[1024,512]{1,0:T(8,128)(2,1)S(1)} %get-tuple-element.55.refs_2_), custom_call_target="tpu_custom_call" | custom-call | bytes 210000000 | tf_op jit(solution)/shard_map/pallas_call | solution.py:504
  300.1 1.3 copy-done.21
  301.3 1.7 multiply_reduce_fusion.1
  303.1 1.8 multiply_convert_fusion.norm_ref
  304.9 127.9 %shard_map.208 = (bf16[2,2,2,256,2048]{4,3,2,1,0:T(8,128)(2,1)}, bf16[2,1024,1024]{2,1,0:T(8,128)(2,1)}, bf16[2,1024,1024]{2,1,0:T(8,128)(2,1)}, bf16[2,1024,102...) custom-call(bf16[256,2048]{1,0:T(8,128)(2,1)} %multiply_convert_fusion.norm_ref, ...), custom_call_target="tpu_custom_call" | custom-call | bytes 390000000 | tf_op jit(solution)/shard_map/pallas_call | solution.py:1153
  432.9 2.5 convert_add_fusion.4
  435.8 2.5 slice.100
  439.1 3.6 fusion.6.refs_0_
  442.7 13.1 %bitcast_convert_fusion.refs_11_ = bf16[1024,2048]{1,0:T(8,128)(2,1)} fusion(bf16[2,1024,1024]{2,1,0:T(8,128)(2,1)S(1)} %copy-done.39, bf16[2,1024,2048]{2,1,0:T(8,128)(2,1)} %bitcast.188), kind=kOutput, calls=%fused_computation.1 | convolution fusion | flops 8592031744 | bytes 16777216 | tf_op jit(solution)/shard_map/dot_general | solution.py:548
  457.5 252.6 %shard_map.209 = (bf16[2,2,2,256,2048]{4,3,2,1,0:T(8,128)(2,1)}, bf16[2,1024,512]{2,1,0:T(8,128)(2,1)}, bf16[3,256,2048]{2,1,0:T(8,128)(2,1)}, bf16[2,256,2048]{...) custom-call(bf16[256,2048]{1,0:T(8,128)(2,1)} %fusion.6.refs_0_, ...), custom_call_target="tpu_custom_call" | custom-call | tf_op jit(solution)/shard_map/pallas_call | solution.py:952
  710.1 2.4 convert_add_fusion.3
  712.9 1.2 copy-done.37
  715.8 9.8 %bitcast_convert_fusion.1.refs_0_ = bf16[2048,512]{1,0:T(8,128)(2,1)} fusion(bf16[2,1024,2048]{2,1,0:T(8,128)(2,1)} %bitcast.197, bf16[2,1024,512]{2,1,0:T(8,128)(2,1)S(1)} %copy-done.40), kind=kOutput, calls=%fused_computation.2 | convolution fusion | flops 4296015872 | bytes 12582912 | tf_op jit(solution)/shard_map/dot_general | solution.py:548
  725.7 3.3 fusion.11
  729.0 1.6 convert_element_type.351
  731.3 40.3 %shard_map.210 = (bf16[512,512]{1,0:T(8,128)(2,1)S(1)}, bf16[8,64,1024]{2,1,0:T(8,128)(2,1)S(1)}, bf16[8,64,1024]{2,1,0:T(8,128)(2,1)S(1)}) custom-call(bf16[2048,512]{1,0:T(8,128)(2,1)} %bitcast_convert_fusion.1.refs_0_, bf16[8,64,1024]{2,1,0:T(8,128)(2,1)S(1)} %bitcast.175, bf16[8,64,1024]{2,1,0:T(8,128)(2,1)S(1)} %bitcast.176), custom_call_target="tpu_custom_call" | custom-call | bytes 150000000 | tf_op jit(solution)/shard_map/pallas_call | solution.py:504
  771.6 10.0 %shard_map.211.attn = bf16[8,64,512]{2,1,0:T(8,128)(2,1)S(1)} custom-call(bf16[8,64,512]{2,1,0:T(8,128)(2,1)S(1)} %bitcast.177), custom_call_target="tpu_custom_call" | custom-call | bytes 30000000 | tf_op jit(solution)/shard_map/pallas_call | solution.py:504
  781.7 2.8 shard_map.212
  (144 shorter events, 15.6 us)
Async XLA Ops:
  7.2 6.4 copy-start.4
  7.2 6.4 copy-start.6
  7.2 297.7 %all-gather.2.cloned.1.call-start = ((), (), s32[]{:S(2)}) async-start(), calls=%async_computation | async-start | bytes 9437184 | tf_op jit(solution)/shard_map/all_gather | solution.py:1242
  7.9 75.2 %collective-permute-start = (bf16[64,2048]{1,0:T(8,128)(2,1)}, bf16[64,2048]{1,0:T(8,128)(2,1)S(1)}, u32[]{:S(2)}, u32[]{:S(2)}) collective-permute-start(bf16[64,2048]{1,0:T(8,128)(2,1)} %param.18), channel_id=1, source_target_pairs={{0,0},{1,16},{2,2},{3,18},{4,1},{5,17},{6,3},{7,19},{8,4},{9,20},{... | collective-permute-start | bytes 786440 | tf_op jit(solution)/shard_map/ppermute | solution.py:1260
  76.7 3.3 copy-start.28
  80.1 147.5 %copy-start.20 = (s32[2,2,1,512]{3,2,1,0:T(1,128)}, s32[2,2,1,512]{3,2,1,0:T(1,128)S(1)}, u32[]{:S(2)}) copy-start(s32[2,2,1,512]{3,2,1,0:T(1,128)S(1)} %compare_select_fusion.k_pos_ref.refs_5_) | copy-start | bytes 24580
  82.0 145.5 %copy-start.8 = (s32[512,1]{1,0:T(8,128)}, s32[512,1]{1,0:T(8,128)S(1)}, u32[]{:S(2)}) copy-start(s32[512,1]{1,0:T(8,128)S(1)} %copy.42.q_pos_ref.refs_4_) | copy-start | bytes 6148
  83.1 76.9 %copy-start.33 = (f32[512,128]{1,0:T(8,128)}, f32[512,128]{1,0:T(8,128)S(1)}, u32[]{:S(2)}) copy-start(f32[512,128]{1,0:T(8,128)S(1)} %get-tuple-element.108) | copy-start | bytes 786436
  83.1 76.9 %copy-start.35 = (f32[512,128]{1,0:T(8,128)}, f32[512,128]{1,0:T(8,128)S(1)}, u32[]{:S(2)}) copy-start(f32[512,128]{1,0:T(8,128)S(1)} %get-tuple-element.107) | copy-start | bytes 786436
  151.2 80.7 %copy-start.9 = (bf16[8,64,2048]{2,1,0:T(8,128)(2,1)}, bf16[8,64,2048]{2,1,0:T(8,128)(2,1)S(1)}, u32[]{:S(2)}) copy-start(bf16[8,64,2048]{2,1,0:T(8,128)(2,1)S(1)} %get-tuple-element.56) | copy-start | bytes 6291460
  151.2 4.2 copy-start.32
  227.4 4.5 copy-start.3
  227.5 8.8 %copy-start.2 = (bf16[1024,512]{1,0:T(8,128)(2,1)}, bf16[1024,512]{1,0:T(8,128)(2,1)S(1)}, u32[]{:S(2)}) copy-start(bf16[1024,512]{1,0:T(8,128)(2,1)S(1)} %pad_maximum_fusion.q_ref.refs_1_) | copy-start | bytes 3145732
  231.9 4.4 copy-start.10
  231.9 4.3 copy-start.14
  236.3 62.7 %copy-start.26 = (bf16[1024,2048]{1,0:T(8,128)(2,1)S(1)}, bf16[1024,2048]{1,0:T(8,128)(2,1)}, u32[]{:S(2)}) copy-start(bf16[1024,2048]{1,0:T(8,128)(2,1)} %convolution_convert_fusion) | copy-start | bytes 12582916
  299.0 4.0 copy-start
  439.1 3.6 copy-start.39
  442.7 13.1 %copy-start.36 = (f32[512,128]{1,0:T(8,128)S(1)}, f32[512,128]{1,0:T(8,128)}, u32[]{:S(2)}) copy-start(f32[512,128]{1,0:T(8,128)} %copy-done.35) | copy-start | bytes 786436
  442.7 14.0 %copy-start.34 = (f32[512,128]{1,0:T(8,128)S(1)}, f32[512,128]{1,0:T(8,128)}, u32[]{:S(2)}) copy-start(f32[512,128]{1,0:T(8,128)} %copy-done.33) | copy-start | bytes 786436
  715.1 56.6 %collective-permute-start.1 = (bf16[64,2048]{1,0:T(8,128)(2,1)S(1)}, bf16[64,2048]{1,0:T(8,128)(2,1)S(1)}, u32[]{:S(2)}, u32[]{:S(2)}) collective-permute-start(bf16[64,2048]{1,0:T(8,128)(2,1)S(1)} %copy-done.41), channel_id=1, source_target_pairs={{0,0},{16,1},{2,2},{18,3},{1,4},{17,5},{3,6},{19,7},{4,8},{20,9},{... | collective-permute-start | bytes 786440 | tf_op jit(solution)/shard_map/ppermute | solution.py:1349
  715.8 9.8 %copy-start.23 = (bf16[3,256,2048]{2,1,0:T(8,128)(2,1)S(1)}, bf16[3,256,2048]{2,1,0:T(8,128)(2,1)}, u32[]{:S(2)}) copy-start(bf16[3,256,2048]{2,1,0:T(8,128)(2,1)} %get-tuple-element.63) | copy-start | bytes 9437188
  715.8 9.8 %copy-start.25 = (f32[1,2,128,2048]{3,2,1,0:T(8,128)S(1)}, f32[1,2,128,2048]{3,2,1,0:T(8,128)}, u32[]{:S(2)}) copy-start(f32[1,2,128,2048]{3,2,1,0:T(8,128)} %get-tuple-element.92) | copy-start | bytes 6291460
  715.8 9.8 %copy-start.27 = (bf16[3,256,2048]{2,1,0:T(8,128)(2,1)S(1)}, bf16[3,256,2048]{2,1,0:T(8,128)(2,1)}, u32[]{:S(2)}) copy-start(bf16[3,256,2048]{2,1,0:T(8,128)(2,1)} %get-tuple-element.71) | copy-start | bytes 9437188
  715.8 9.8 %copy-start.30 = (bf16[1,2,128,2048]{3,2,1,0:T(8,128)(2,1)S(1)}, bf16[1,2,128,2048]{3,2,1,0:T(8,128)(2,1)}, u32[]{:S(2)}) copy-start(bf16[1,2,128,2048]{3,2,1,0:T(8,128)(2,1)} %param.23) | copy-start | bytes 3145732
  715.8 9.8 %copy-start.31 = (bf16[1,1,256,2048]{3,2,1,0:T(8,128)(2,1)S(1)}, bf16[1,1,256,2048]{3,2,1,0:T(8,128)(2,1)}, u32[]{:S(2)}) copy-start(bf16[1,1,256,2048]{3,2,1,0:T(8,128)(2,1)} %slice.100) | copy-start | bytes 3145732
  731.3 50.3 %copy-start.5 = (bf16[64,8192]{1,0:T(8,128)(2,1)S(1)}, bf16[64,8192]{1,0:T(8,128)(2,1)}, u32[]{:S(2)}) copy-start(bf16[64,8192]{1,0:T(8,128)(2,1)} %wg.1) | copy-start | bytes 3145732
  731.3 50.3 %copy-start.7 = (bf16[64,8192]{1,0:T(8,128)(2,1)S(1)}, bf16[64,8192]{1,0:T(8,128)(2,1)}, u32[]{:S(2)}) copy-start(bf16[64,8192]{1,0:T(8,128)(2,1)} %wu.1) | copy-start | bytes 3145732
  731.3 50.3 %copy-start.12 = (bf16[64,2048]{1,0:T(8,128)(2,1)S(1)}, bf16[64,2048]{1,0:T(8,128)(2,1)}, u32[]{:S(2)}) copy-start(bf16[64,2048]{1,0:T(8,128)(2,1)} %wq.1) | copy-start | bytes 786436
  731.3 50.3 %copy-start.18 = (bf16[64,1024]{1,0:T(8,128)(2,1)S(1)}, bf16[64,1024]{1,0:T(8,128)(2,1)}, u32[]{:S(2)}) copy-start(bf16[64,1024]{1,0:T(8,128)(2,1)} %wv.1) | copy-start | bytes 393220
  731.3 50.4 %copy-start.19 = (bf16[64,1024]{1,0:T(8,128)(2,1)S(1)}, bf16[64,1024]{1,0:T(8,128)(2,1)}, u32[]{:S(2)}) copy-start(bf16[64,1024]{1,0:T(8,128)(2,1)} %wk.1) | copy-start | bytes 393220
  781.6 4.4 copy-start.43
  (15 other events, 30.9 us)
Sparse Core Ops, SparseCore 0:
  9.9 125.2 all-gather.1

commit v5 on v4

--- a/solution.py
+++ b/solution.py
@@ -147,7 +147,9 @@
 
 
 CHUNKS = 4
-AHEAD = 2
+AHEAD = 10
+EARLY = 0
+FLOW = (2, 8, 6, 6)
 
 
 class TeamSum:
@@ -156,15 +158,6 @@
 
     def shape(self, sizes):
         return (2,) + self.x.shape[2:]
-
-
-class PeerSum:
-    def __init__(self, x, x_inside):
-        self.x, self.x_inside = x, x_inside
-
-    def shape(self, sizes):
-        rows, columns = self.x.shape
-        return (rows // (sizes["x"] * sizes["zh"]), columns)
 
 
 class Net:
@@ -263,17 +256,29 @@
 
 
 class Stream:
-    def __init__(self, net, shape, x_inside):
-        self.net, self.x_inside = net, x_inside
+    def __init__(self, net, shape, owners):
+        self.net, self.owners = net, owners
         self.nx, self.nz = net.sizes["x"], net.sizes["zh"]
         self.columns, self.dtype = shape[1], BF16
         self.rows = shape[0] // (self.nx * self.nz * CHUNKS)
         self.chunks = [(z, q) for z in [*range(1, self.nz), 0] for q in range(CHUNKS)]
         self.x_wires = [[net.wire({"x": d}) for d in range(1, self.nx)] for _ in self.chunks]
         self.z_wires = [net.wire({"zh": z}) if z else None for z, _ in self.chunks]
+        if owners:
+            self.members = offsets(net.sizes, TEAM)
+            self.own_rows = self.rows // net.sizes["c"]
+            self.cores = [
+                [({**o, "c": c}, net.wire({**o, "c": c}) if c or any(o.values()) else None)
+                 for c in range(net.sizes["c"])]
+                for o in self.members
+            ]
 
     def shape(self):
-        return jax.ShapeDtypeStruct((CHUNKS * self.rows, self.columns), self.dtype)
+        rows = CHUNKS * self.rows
+        if not self.owners:
+            return jax.ShapeDtypeStruct((rows, self.columns), self.dtype)
+        n = math.prod(self.net.sizes[a] for a in OWNERS)
+        return jax.ShapeDtypeStruct((n, rows // n, self.columns), self.dtype)
 
     def scratch(self):
         n, chunk = len(self.chunks), (self.rows, self.columns)
@@ -289,18 +294,16 @@
         self.term, self.out, self.mine = term, out, mine
         self.from_x, self.from_z = from_x, from_z
         self.load_sem, self.store_sem = load_sem, store_sem
-        self.loads, self.x_sent, self.z_sent, self.stores = {}, {}, {}, []
+        self.loads, self.x_sent, self.z_sent, self.stores, self.handed = {}, {}, {}, [], []
 
     def window(self, x, z, q):
         zh = self.net.moved({"zh": z})["zh"]
-        if self.x_inside:
+        if self.owners:
+            q = place(self.net.moved(self.members[q]), TEAM, self.net.sizes)
             block = (zh * CHUNKS + q) * self.nx + x
         else:
             block = (x * self.nz + zh) * CHUNKS + q
         return self.term.at[pl.ds(pl.multiple_of(block * self.rows, self.rows), self.rows)]
-
-    def run(self, step, k):
-        (self.issue, self.merge, self.last)[step](k)
 
     def issue(self, k):
         z, q = self.chunks[k]
@@ -337,6 +340,19 @@
             self.z_sent[z, q].wait_recv()
             total += self.from_z[z - 1, q].astype(F32)
         self.mine[k] = total.astype(self.dtype)
+        if self.owners:
+            mine = place(self.net.here, OWNERS, self.net.sizes)
+            for off, wire in self.cores[q]:
+                core = self.net.moved(off)["c"]
+                start = pl.multiple_of(core * self.own_rows, self.own_rows)
+                src = self.mine.at[k, pl.ds(start, self.own_rows)]
+                if wire:
+                    self.handed.append(self.net.send(src, self.out.at[mine], wire))
+                else:
+                    store = pltpu.make_async_copy(src, self.out.at[mine], self.store_sem.at[q])
+                    store.start()
+                    self.stores.append(store)
+            return
         store = pltpu.make_async_copy(
             self.mine.at[k], self.out.at[pl.ds(q * self.rows, self.rows)], self.store_sem.at[q]
         )
@@ -344,6 +360,8 @@
         self.stores.append(store)
 
     def close(self):
+        for cp in self.handed:
+            cp.wait_recv()
         for store in self.stores:
             store.wait()
 
@@ -415,14 +433,6 @@
             runner = Adder(job, number, net)
             steps += runner.steps
             stage = runner.scratch()
-        elif isinstance(job, PeerSum):
-            runner = Stream(net, job.x.shape, job.x_inside)
-            for k in range(len(runner.chunks)):
-                steps.append(((0, k, 0, number, k), runner, 0, k))
-                steps.append(((1, k + 2, 1, number, k), runner, 1, k))
-            for k in range(CHUNKS):
-                steps.append(((1, k + len(runner.chunks) + 2, 2, number, k), runner, 2, k))
-            stage = runner.scratch()
         else:
             runner = None
             n = math.prod(sizes[a] for a in SHARES) if isinstance(job, ColumnSwap) else 1
@@ -441,7 +451,7 @@
         loads, stores = [], []
         for number, job in enumerate(jobs):
             runner, lo, hi = runners[number]
-            if isinstance(job, (TeamSum, PeerSum)):
+            if isinstance(job, TeamSum):
                 runner.open(ins[number], outs[number], *rest[lo:hi])
                 continue
             (stage,) = rest[lo:hi]
@@ -495,9 +505,6 @@
             if isinstance(runner, Adder):
                 runner.finish()
         net.close()
-        for runner, _, _ in runners:
-            if isinstance(runner, Stream):
-                runner.close()
         for store in stores:
             store.wait()
 
@@ -558,18 +565,108 @@
     return lax.rsqrt(jnp.mean(values * values, axis=-1, keepdims=True) + EPS)
 
 
-def attention(q, kv, q_pos, k_pos, scaling):
+def attention_front(
+    norm, attn_part, out_part, gate_part, gd, q_pos, k_pos, cos, sin, scaling, collective_id
+):
+    net = Net({a: lax.axis_size(a) for a in AXES})
+    sizes = net.sizes
+    own, width = norm.shape
     n_slot, n_zh, _, n = k_pos.shape
-    heads = q.shape[1] // HEAD
-
-    def kernel(q_ref, kv_ref, q_pos_ref, k_pos_ref, o_ref, lse_ref):
-        for s in range(n_slot):
+    n_tok = n_slot * n
+    columns = attn_part.shape[2]
+    q_cols = columns - 2 * HEAD
+    heads = q_cols // HEAD
+    half = q_cols // 2
+    team = attn_part.shape[0]
+    norm_job = NearGather(norm, PAIRED_SLOTS, TO_TEAM)
+    attn_job = RowGather(attn_part, None, [OUTWARD] * team)
+    out_job = Gather(out_part, SHARES, [OUTWARD] * (out_part.shape[0] // 16), rank=2)
+    gd_job = NearGather(gd, PAIRED_SLOTS, TO_TEAM)
+    gate_job = RowGather(gate_part, None, [OUTWARD] * team)
+    norms, attns, outs = (Relay(job, i, net) for i, job in enumerate((norm_job, attn_job, out_job)))
+    gds, gates = (Relay(job, i, net) for i, job in enumerate((gd_job, gate_job)))
+    first = sorted(norms.steps + attns.steps + outs.steps, key=lambda step: step[0])
+    gd_steps = sorted(gds.steps, key=lambda step: step[0])
+    gate_steps = sorted(gates.steps, key=lambda step: step[0])
+    kv_wires = [[net.wire({"zh": z}) for z in range(1, n_zh)] for _ in range(n_slot)]
+    half_wires = [net.wire({"c": 1}) for _ in range(n_slot)]
+    y_rows, zl_rows = pl.ds(0, own // 2), pl.ds(own // 2, own // 2)
+    far_wires = net.wire({"y": 1}), net.wire({"zl": 1})
+    near_wires = net.wire({"y": 1}), net.wire({"zl": 1})
+    n_local = 64
+    out_shapes = [job.shape(sizes) for job in (norm_job, gd_job, attn_job, out_job, gate_job)]
+
+    def kernel(
+        norm_ref, attn_ref, outp_ref, gate_ref, gd_ref, q_pos_ref, k_pos_ref, cos_ref, sin_ref,
+        norms_ref, gds_ref, w_attn_ref, w_out_ref, w_gate_ref, q_ref, kv_ref, lse_ref, half_ref,
+        terms_ref,
+        nv, wa, wo, q, kv, o, terms, far, gd_stage, gate_stage, send_sem, recv_sem, local_sem,
+    ):
+        net.open(send_sem, recv_sem)
+        norms.open(norm_ref, norms_ref)
+        attns.open(attn_ref, wa)
+        outs.open(outp_ref, wo)
+        gds.open(gd_ref, gds_ref)
+        gates.open(gate_ref, w_gate_ref)
+        used = iter(range(n_local))
+
+        def local(src, dst):
+            cp = pltpu.make_async_copy(src, dst, local_sem.at[next(used)])
+            cp.start()
+            return cp
+
+        def start(steps):
+            for _, runner, hops, *what in steps:
+                if not hops:
+                    runner.run(hops, *what)
+
+        gate_first = [step for step in gate_steps if not step[2] and step[3] < EARLY]
+        gate_rest = [step for step in gate_steps if not step[2] and step[3] >= EARLY]
+        start(first)
+        got_norm = local(norm_ref, nv.at[0, 0])
+        got_attn = [local(attn_job.cut(attn_ref, p), attns.own(p)) for p in range(team)]
+        got_attn += [
+            local(out_job.cut(outp_ref, p), outs.own(p)) for p in range(len(out_job.orders))
+        ]
+        got_gd, got_gate = local(gd_ref, gd_stage), local(gate_ref, gate_stage)
+        got_norm.wait()
+        kept = [local(norm_job.cut(nv.at[0, 0], p), norms.own(p)) for p in range(CHUNKS)]
+        got_gd.wait()
+        kept += [local(gd_job.cut(gd_stage, p), gds.own(p)) for p in range(CHUNKS)]
+        got_gate.wait()
+        kept += [local(gate_job.cut(gate_stage, p), gates.own(p)) for p in range(team)]
+
+        def turn(t, rows):
+            h = HEAD // 2
+            c, sn = cos_ref[rows], sin_ref[rows]
+            front, back = t[:, :h], t[:, h:]
+            return jnp.concatenate([front * c - back * sn, back * c + front * sn], axis=1).astype(
+                BF16
+            )
+
+        def project(s):
+            for j in range(n // own):
+                rows = slice(s * n + j * own, s * n + (j + 1) * own)
+                for g in range(heads):
+                    cols = slice(g * HEAD, (g + 1) * HEAD)
+                    q[rows, cols] = turn(dot(nv[s, j], wa[:, cols]), rows)
+                kv[0, rows, :HEAD] = turn(dot(nv[s, j], wa[:, q_cols : q_cols + HEAD]), rows)
+                kv[0, rows, HEAD:] = dot(nv[s, j], wa[:, q_cols + HEAD :]).astype(BF16)
+            window = pl.ds(s * n, n)
+            return [
+                net.send(kv.at[0, window], kv.at[n_zh - z, window], kv_wires[s][z - 1])
+                for z in range(1, n_zh)
+            ]
+
+        def attend(s, sent):
+            for cp in sent:
+                cp.wait_recv()
             rows = slice(s * n, (s + 1) * n)
             for g in range(heads):
                 cols = slice(g * HEAD, (g + 1) * HEAD)
                 scores = []
                 for z in range(n_zh):
-                    score = dot(q_ref[rows, cols], kv_ref[z, rows, :HEAD], COLS_T) * scaling
+                    score = dot(q[rows, cols], kv[z, rows, :HEAD], COLS_T) * scaling
                     allowed = k_pos_ref[s, z] <= q_pos_ref[...]
                     scores.append(jnp.where(allowed, score, -jnp.inf))
                 peak = scores[0].max(axis=1, keepdims=True)
@@ -578,23 +675,128 @@
                 exps = [jnp.exp(score - peak) for score in scores]
                 total = sum(e.sum(axis=1, keepdims=True) for e in exps)
                 inverse = 1.0 / total
-                o_ref[rows, cols] = sum(
-                    dot((e * inverse).astype(BF16), kv_ref[z, rows, HEAD:])
-                    for z, e in enumerate(exps)
+                o[rows, cols] = sum(
+                    dot((e * inverse).astype(BF16), kv[z, rows, HEAD:]) for z, e in enumerate(exps)
                 ).astype(BF16)
                 lse_ref[s, g] = peak + jnp.log(total)
-
-    vmem = pl.BlockSpec(memory_space=pltpu.VMEM)
+            away = pl.ds(pl.multiple_of((1 - net.here["c"]) * half, half), half)
+            here = pl.ds(pl.multiple_of(net.here["c"] * half, half), half)
+            window = pl.ds(s * n, n)
+            halves.append(net.send(o.at[window, away], half_ref.at[1, window], half_wires[s]))
+            kept.append(local(o.at[window, here], half_ref.at[0, window]))
+
+        def term(r):
+            n_part = out_part.shape[0]
+
+            def tile(t, _):
+                at = pl.ds(pl.multiple_of(t * TILE, TILE), TILE)
+                weight = wo[:, :, at].reshape(q_cols, TILE)
+                terms[r, :, at] = dot(o[r * own : (r + 1) * own], weight).astype(BF16)
+                return 0
+
+            lax.fori_loop(0, width // TILE, tile, 0)
+
+        def add(r, window):
+            terms[r, window] = (terms[r, window].astype(F32) + far[window].astype(F32)).astype(BF16)
+
+        halves, late = [], []
+
+        def relay(steps, most=9):
+            for _, runner, hops, part, off, sends in steps:
+                if not hops:
+                    continue
+                if runner in (norms, gds) and off["c"]:
+                    late.append((runner, hops, part, off, sends))
+                    continue
+                runner.run(hops, part, off, sends)
+                if runner is attns and hops == 1 and off["zh"] and part == team - 1:
+                    start(gate_first)
+                    gate_first.clear()
+                if runner is norms and part == CHUNKS - 1:
+                    i, j = off["y"], off["zl"]
+                    got[i, j] = local(norms_ref.at[0, i, j], nv.at[i, j])
+
+        got = {}
+        relay(first)
+        for cp in got_attn:
+            cp.wait()
+        kept.append(local(wa, w_attn_ref))
+        kept.append(local(wo, w_out_ref))
+        start(gd_steps)
+        got[0, 1].wait()
+        sent = [project(0)]
+        got[1, 0].wait()
+        got[1, 1].wait()
+        sent.append(project(1))
+        start(gate_rest)
+        relay([step for step in gd_steps if step[2] == 1])
+        attend(0, sent[0])
+        term(1)
+        term(0)
+        relay([step for step in gd_steps if step[2] > 1])
+        attend(1, sent[1])
+        term(3)
+        to_far = (
+            net.send(terms.at[3, y_rows], far.at[y_rows], far_wires[0]),
+            net.send(terms.at[3, zl_rows], far.at[zl_rows], far_wires[1]),
+        )
+        term(2)
+        kept.append(local(terms.at[0], terms_ref.at[0]))
+        kept.append(local(q, q_ref))
+        kept.append(local(kv, kv_ref))
+        relay([step for step in gate_steps if step[2] == 1 and step[3] < 2])
+        to_far[1].wait_recv()
+        add(2, zl_rows)
+        to_y = net.send(terms.at[2], terms_ref.at[1], near_wires[0])
+        to_far[0].wait_recv()
+        add(1, y_rows)
+        to_zl = net.send(terms.at[1], terms_ref.at[2], near_wires[1])
+        relay([step for step in gate_steps if not (step[2] == 1 and step[3] < 2)])
+        for runner, *step in late:
+            runner.run(*step)
+        for cp in halves + [to_y, to_zl]:
+            cp.wait_recv()
+        net.close()
+        for cp in kept:
+            cp.wait()
+
+    shape = jax.ShapeDtypeStruct
+    vmem, hbm = pl.BlockSpec(memory_space=pltpu.VMEM), pl.BlockSpec(memory_space=pl.ANY)
+    q_shape, kv_shape = (n_tok, q_cols), (n_zh, n_tok, 2 * HEAD)
     return pl.pallas_call(
         kernel,
         out_shape=[
-            jax.ShapeDtypeStruct(q.shape, BF16),
-            jax.ShapeDtypeStruct((n_slot, heads, n, 1), F32),
+            *[shape(dims, BF16) for dims in out_shapes],
+            shape(q_shape, BF16),
+            shape(kv_shape, BF16),
+            shape((n_slot, heads, n, 1), F32),
+            shape((2, n_tok, half), BF16),
+            shape((3, own, width), BF16),
         ],
-        in_specs=[vmem] * 4,
-        out_specs=[vmem] * 2,
-        compiler_params=pltpu.CompilerParams(vmem_limit_bytes=VMEM_LIMIT),
-    )(q, kv, q_pos, k_pos)
+        in_specs=[hbm] * 5 + [vmem] * 4,
+        out_specs=[hbm] * 7 + [vmem] + [hbm] * 2,
+        scratch_shapes=[
+            pltpu.VMEM((2, 2, own, width), BF16),
+            pltpu.VMEM(out_shapes[2], BF16),
+            pltpu.VMEM(out_shapes[3], BF16),
+            pltpu.VMEM(q_shape, BF16),
+            pltpu.VMEM(kv_shape, BF16),
+            pltpu.VMEM(q_shape, BF16),
+            pltpu.VMEM((4, own, width), BF16),
+            pltpu.VMEM((own, width), BF16),
+            pltpu.VMEM(gd.shape, BF16),
+            pltpu.VMEM(gate_part.shape, BF16),
+            pltpu.SemaphoreType.DMA((net.count,)),
+            pltpu.SemaphoreType.DMA((net.count,)),
+            pltpu.SemaphoreType.DMA((n_local,)),
+        ],
+        cost_estimate=pl.CostEstimate(
+            flops=0, bytes_accessed=160 * 3_000_000, transcendentals=0
+        ),
+        compiler_params=pltpu.CompilerParams(
+            collective_id=collective_id, has_side_effects=True, vmem_limit_bytes=FFN_VMEM_LIMIT
+        ),
+    )(norm, attn_part, out_part, gate_part, gd, q_pos, k_pos, cos, sin)
 
 
 def attention_back(
@@ -613,10 +815,10 @@
     adder = Adder(TeamSum(out_parts, CHUNKS), 1, net)
     streams, made = [], []
     if sums:
-        down, _, gate_half, _, o_half = sums
-        made = [(width, gate_half.shape[2])] * 2 + [(o_half.shape[2], width)]
+        down, _, gate_half, _, o_half, _ = sums
+        made = [(width, gate_half.shape[2])] * 2 + [(o_half.shape[2], width), (width, half)]
         streams = [Stream(net, down.shape, False)]
-        streams += [Stream(net, made[i], i < 2) for i in range(3)]
+        streams += [Stream(net, dims, i != 2) for i, dims in enumerate(made)]
     n_chunks = n_zh * CHUNKS
     kv_wires = [[net.wire({"zh": z}) for z in range(1, n_zh)] for _ in range(n_slot)]
     half_wires = [net.wire({"c": 1}) for _ in range(n_slot)]
@@ -665,10 +867,11 @@
 
         def pump():
             for i, stream in enumerate(streams):
-                allowed = min(n_chunks, merged[i - 1] + AHEAD) if i else n_chunks
-                while ready[i] and issued[i] < allowed:
+                while ready[i] and issued[i] < n_chunks and sum(issued) < sum(merged) + AHEAD:
                     stream.issue(issued[i])
                     issued[i] += 1
+                if issued[i] < n_chunks:
+                    return
 
         def there(i):
             if sums:
@@ -692,8 +895,8 @@
         if sums:
             wr, lt, ot, o_v, wr_sem, lt_sem, ot_sem = take(7)
 
-        def product(rhs_ref, term_ref, steps):
-            lhs_ref, n_cols = sum_ins[1], wr.shape[2]
+        def product(lhs_ref, rhs_ref, term_ref, steps):
+            n_cols = wr.shape[2]
             n_tiles = width // own
 
             def lhs(t, slot, c):
@@ -758,7 +961,7 @@
         got_wo.wait()
         got_wa.wait()
         if sums:
-            product(sum_ins[2], made_refs[0], 1)
+            product(sum_ins[1], sum_ins[2], made_refs[0], 1)
             there(1)
 
         def turn_back(t, rows):
@@ -838,6 +1041,10 @@
                 if at == hops:
                     adder.run(at, *what)
 
+        def relay_late():
+            for hops, part, off, sends in late:
+                gas.run(hops, part, off, sends)
+
         halves, late, arrived, sent = [], [], set(), {}
         for _, _, hops, part, off, sends in ga_steps:
             if not hops:
@@ -859,13 +1066,43 @@
         add_out(0)
         flow(2)
         if sums:
-            product(sum_ins[3], made_refs[1], 2)
+            product(sum_ins[1], sum_ins[3], made_refs[1], 2)
             there(2)
+            relay_late()
+            got_o.wait()
+            others = [
+                local(gas_ref.at[1, i, j], gn1.at[2 * i + j]) for i in range(2) for j in range(2)
+            ]
+            for cp in others:
+                cp.wait()
+
+            def output(t, _):
+                at = pl.ds(pl.multiple_of(t * TILE, TILE), TILE)
+                value = dot(o_v[0], gav[:, :, :, at].reshape(n_tok, TILE), ROWS_T)
+                value += dot(o_v[1], gn1[:, :, at].reshape(n_tok, TILE), ROWS_T)
+                block = pl.ds(pl.multiple_of(t * o_v.shape[2], o_v.shape[2]), o_v.shape[2])
+                wr[0, block] = value.astype(BF16)
+                return 0
+
+            lax.fori_loop(0, width // TILE, output, 0)
+            n_rows = o_v.shape[2]
+            kept_out = [
+                local(
+                    wr.at[0, pl.ds(t * n_rows, n_rows)], made_refs[2].at[:, pl.ds(t * TILE, TILE)]
+                )
+                for t in range(width // TILE)
+            ]
+            for cp in kept_out:
+                cp.wait()
+            there(3)
+            flow(FLOW[0])
+        else:
+            relay_late()
         keys(0, sent[0])
         term(1)
         term(0)
         add_out(1)
-        flow(4)
+        flow(FLOW[1])
         keys(1, sent[1])
         term(3)
         to_far = (
@@ -873,50 +1110,30 @@
             net.send(gn1.at[3, zl_rows], far.at[zl_rows], far_wires[1]),
         )
         term(2)
-        kept_gn1 = local(gn1.at[0], gn1_ref.at[0])
-        flow(2)
+        kept.append(local(gn1.at[0], gn1_ref.at[0]))
+        flow(FLOW[2])
         to_far[1].wait_recv()
         add(2, zl_rows)
         to_y = net.send(gn1.at[2], gn1_ref.at[1], near_wires[0])
         to_far[0].wait_recv()
         add(1, y_rows)
         to_zl = net.send(gn1.at[1], gn1_ref.at[2], near_wires[1])
-        for hops, part, off, sends in late:
-            gas.run(hops, part, off, sends)
-        flow(2)
+        for cp in halves:
+            cp.wait_recv()
+        for cp in kept:
+            cp.wait()
         if sums:
-            for cp in (*to_far, to_y, to_zl):
-                net.settle(cp)
-            kept_gn1.wait()
-            got_o.wait()
-            others = [
-                local(gas_ref.at[1, i, j], gn1.at[2 * i + j]) for i in range(2) for j in range(2)
-            ]
-            for cp in others:
-                cp.wait()
-
-            def output(t, _):
-                at = pl.ds(pl.multiple_of(t * TILE, TILE), TILE)
-                value = dot(o_v[0], gav[:, :, :, at].reshape(n_tok, TILE), ROWS_T)
-                value += dot(o_v[1], gn1[:, :, at].reshape(n_tok, TILE), ROWS_T)
-                far[:, at] = value.astype(BF16)
-                return 0
-
-            lax.fori_loop(0, width // TILE, output, 0)
-            local(far, made_refs[2]).wait()
-            there(3)
-        else:
-            kept_gn1.wait()
+            flow(FLOW[3])
+            product(sum_ins[5], half_ref, made_refs[3], 1)
+            there(4)
         flow(100)
         assert not plan
-        for cp in halves + [to_y, to_zl]:
+        for cp in (to_y, to_zl):
             cp.wait_recv()
         adder.finish()
         net.close()
         for stream in streams:
             stream.close()
-        for cp in kept:
-            cp.wait()
 
     shape = jax.ShapeDtypeStruct
     vmem, hbm = pl.BlockSpec(memory_space=pltpu.VMEM), pl.BlockSpec(memory_space=pl.ANY)
@@ -1282,42 +1499,20 @@
     tokens = inputs.reshape(own, width).astype(F32)
     scale_one = rms_scale(tokens)
     norm_one = (tokens * scale_one * gain_one).astype(BF16)
-    norm_one_pair, w_attn, w_out = exchange(
-        [
-            NearGather(norm_one, PAIRED_SLOTS, TO_TEAM),
-            row_gather(attn_part),
-            Gather(out_part, SHARES, [OUTWARD] * (rows // 16)),
-        ],
-        2,
+    gy = valid * cotangent.reshape(own, width).astype(F32)
+    (
+        norm_one_pair, gd_pair, w_attn, w_out, w_gate, q, kv_all, lse, o_half, o_terms
+    ) = attention_front(
+        norm_one, attn_part, out_part, gate_part, gy.astype(BF16), q_pos, k_pos, cos, sin,
+        scaling, 2,
     )
     norm_one_pair = norm_one_pair.reshape(2, n_tok, width)
-    w_attn = w_attn.reshape(width, -1)
     w_out = w_out.reshape(q_cols, width)
-    qkv = dot(norm_one_pair[0], w_attn)
-    turned = [
-        rotate(qkv[:, h * HEAD : (h + 1) * HEAD], cos, sin).astype(BF16) for h in range(heads + 1)
-    ]
-    q = jnp.concatenate(turned[:heads], axis=1)
-    kv = jnp.concatenate([turned[heads], qkv[:, q_cols + kv_cols :].astype(BF16)], axis=1)
-    gy = valid * cotangent.reshape(own, width).astype(F32)
-    kv_all, gd_pair = exchange(
-        [
-            NearGather(kv, ("zh",), [("zh",)]),
-            NearGather(gy.astype(BF16), PAIRED_SLOTS, TO_TEAM_EVEN),
-        ],
-        3,
-    )
-    o, lse = attention(q, kv_all, q_pos, k_pos, scaling)
-
-    o_parts = dot(o, w_out).astype(BF16).reshape(2, 2, own, width)
-    o_added, w_gate, o_half = exchange(
-        [TeamSum(o_parts, 4), row_gather(gate_part), Halves(o)], 4, micros=70
-    )
 
     def added(term, others):
         return term.astype(F32) + others[0].astype(F32) + others[1].astype(F32)
 
-    h1 = tokens + added(o_parts[0, 0], o_added)
+    h1 = tokens + added(o_terms[0], o_terms[1:])
     scale_two = rms_scale(h1)
     norm_two = (h1 * scale_two * gain_two).astype(BF16)
     norm_two_pair, gate_half, up_half, mixed_half, gn2_terms, out_parts = feed_forward(
@@ -1330,14 +1525,13 @@
 
     down_term = dot(mixed_half, gd_pair, PAIR_ROWS_T).astype(BF16)
     pairs = size["x"] == size["zh"] == 2
-    sums = (down_term, norm_two_pair, gate_half, up_half, o_half) if pairs else None
+    sums = (down_term, norm_two_pair, gate_half, up_half, o_half, norm_one_pair) if pairs else None
     ga_pair, g_qkv_half, gn1_terms, out_added, *totals = attention_back(
         gh1.astype(BF16), q, kv_all, lse, q_pos, k_pos, cos, sin, w_out, w_attn, out_parts, sums,
         scaling, 8,
     )
     outputs = valid * (h1 + added(out_parts[0, 0], out_added))
     outputs = outputs.astype(BF16).reshape(inputs.shape)
-    attn_term = dot(norm_one_pair, g_qkv_half, PAIR_ROWS_T).astype(BF16)
     n_owners = math.prod(size[a] for a in OWNERS)
 
     def by_owner(total):
@@ -1345,19 +1539,15 @@
 
     homeward = [(b, a) for a, b in homes]
     if pairs:
-        down_grad, gate_sum, up_sum, out_sum = totals[:4]
+        down_grad, gate_sum, up_sum, out_sum, attn_sum = totals[:5]
         output_grad = lax.ppermute(out_sum, AXES, homeward)
-        attn_sum, gate_sum, up_sum = exchange(
-            [PeerSum(attn_term, True), by_owner(gate_sum), by_owner(up_sum)], 9
-        )
-        attn_sum, output_grad = lax.optimization_barrier((attn_sum, output_grad))
-        (attn_sum,) = exchange([by_owner(attn_sum)], 10, micros=10)
     else:
         outer = size["zh"] * team
 
         def sum_peers(term, outer=1):
             return sum_over(sum_over(term, "x", outer).astype(BF16), "zh").astype(BF16)
 
+        attn_term = dot(norm_one_pair, g_qkv_half, PAIR_ROWS_T).astype(BF16)
         gate_term = dot(norm_two_pair, gate_half, PAIR_ROWS_T).astype(BF16)
         up_term = dot(norm_two_pair, up_half, PAIR_ROWS_T).astype(BF16)
         out_term = dot(o_half, ga_pair.reshape(2, n_tok, width), PAIR_ROWS_T).astype(BF16)

time: 802 us -> 735 us (0.916)
  Pallas kernels: 697 us -> 643 us
  matrix products: 31.7 us -> 13.2 us
    pallas_call x6 -> x1, Pallas kernels: 309 us -> 60.7 us  [exchange(): pl.pallas_call(kernel, out_shape=[jax.ShapeDtypeStruct(job.shape(sizes),...]
    pallas_call x1, Pallas kernels: 4.36 us -> 180 us  [attention_front(): pl.pallas_call(kernel, out_shape=[*[shape(dims, BF16) for dims in out_sha...]
    pallas_call x1, Pallas kernels: 253 us -> 269 us  [attention_back(): pl.pallas_call(kernel, out_shape=[shape((2, 2, 2, own, width), BF16), sha...]
    dot_general x2 -> x1, matrix products: 22.9 us -> 13.2 us  [dot(): return lax.dot_general(a, b, dims, preferred_element_type=F32)]
    dot_general x2 -> x0, matrix products: 8.8 us -> none  [dot(): return jnp.dot(a, b, preferred_element_type=F32)]
  transfers between devices with their start and end apart: 3 -> 3, of which waited for: 0 -> 0; matrix products, arithmetic and copies ran while one was open for 5% -> 4% of each run, Pallas kernels for 38% -> 34%
where the time goes in v5:
time: 735 us; the launch traced here: 725 us
  Pallas kernels  643 us (87%)
  other arithmetic  31.5 us (4%)
  local copies, waits for them, and re-layouts  16.4 us (2%)
  between operations  15.3 us (2%)
  matrix products  13.2 us (2%)
    pallas_call x1, Pallas kernels, attention_back(): pl.pallas_call(kernel, out_shape=[shape((2, 2, 2, own, width), BF16), sha...  269 us
    pallas_call x1, Pallas kernels, attention_front(): pl.pallas_call(kernel, out_shape=[*[shape(dims, BF16) for dims in out_sha...  180 us
    pallas_call x1, Pallas kernels, feed_forward(): pl.pallas_call(kernel, out_shape=[shape((2, 2, 2, own, width), BF16), *[s...  130 us
    pallas_call x1, Pallas kernels, exchange(): pl.pallas_call(kernel, out_shape=[jax.ShapeDtypeStruct(job.shape(sizes),...  60.7 us
  transfers between devices with their start and end apart: 3, of which 0 were waited for; matrix products, arithmetic and copies ran while one was open for 4% of the time, Pallas kernels for 34%

profile of v5, /device:TPU:0, one launch (start us, length us, event | category | flops | bytes accessed | tf_op | source)
XLA Modules:
  0.0 725.2 jit_solution(18026954939375516168)
XLA Ops:
  7.9 3.6 collective-permute-start
  11.5 1.0 copy.37
  14.5 1.0 bitcast_bitcast_fusion.1
  15.6 60.7 %shard_map.203 = (f32[32,8,128]{2,1,0:T(8,128)S(1)}, bf16[4,64,1024]{2,1,0:T(8,128)(2,1)S(1)}, bf16[4,64,2048]{2,1,0:T(8,128)(2,1)S(1)}, bf16[4,64,2048]{2,1,0:T(8,128)(2,1)S(1)}) custom-call(f32[8,128]{1,0:T(8,128)S(1)} %concatenate.13.refs_0_, bf16[4,64,1024]{2,1,0:T(8,128)(2,1)S(1)} %pad_maximum_fusion.refs_1_, bf16[64,8192]{1,0:T(8,128)(2,1)S(1)} %copy-done, ...), custom_call_target="tpu_custom_call" | custom-call | bytes 150000000 | tf_op jit(solution)/shard_map/pallas_call | solution.py:511
  76.4 1.0 copy-done.3
  77.3 1.0 copy-done.7
  78.3 0.8 copy-done.8
  81.8 2.4 fusion.14.gd_ref
  84.2 1.3 fusion.13.norm_ref
  85.5 0.9 copy.27.q_pos_ref.refs_4_
  86.5 1.0 multiply_sine_fusion
  87.5 0.8 tile.8
  88.3 0.8 tile.20
  89.1 180.4 %shard_map.204 = (bf16[2,2,2,256,2048]{4,3,2,1,0:T(8,128)(2,1)}, bf16[2,2,2,256,2048]{4,3,2,1,0:T(8,128)(2,1)}, bf16[2048,1024]{1,0:T(8,128)(2,1)}, bf16[8,64,20...) custom-call(bf16[256,2048]{1,0:T(8,128)(2,1)} %fusion.13.norm_ref, ...), custom_call_target="tpu_custom_call" | custom-call | bytes 480000000 | tf_op jit(solution)/shard_map/pallas_call | solution.py:766
  269.5 2.5 convert_add_fusion.5
  272.0 1.3 copy-done.19
  273.8 0.9 copy-done.16
  274.7 1.8 multiply_convert_fusion.norm_ref
  276.5 129.6 %shard_map.205 = (bf16[2,2,2,256,2048]{4,3,2,1,0:T(8,128)(2,1)}, bf16[2,1024,1024]{2,1,0:T(8,128)(2,1)}, bf16[2,1024,1024]{2,1,0:T(8,128)(2,1)}, bf16[2,1024,102...) custom-call(bf16[256,2048]{1,0:T(8,128)(2,1)} %multiply_convert_fusion.norm_ref, ...), custom_call_target="tpu_custom_call" | custom-call | bytes 390000000 | tf_op jit(solution)/shard_map/pallas_call | solution.py:1370
  406.2 2.6 convert_add_fusion.4
  409.6 2.6 slice.60
  412.1 13.2 %bitcast_convert_fusion.refs_11_ = bf16[1024,2048]{1,0:T(8,128)(2,1)} fusion(bf16[2,1024,1024]{2,1,0:T(8,128)(2,1)S(1)} %copy-done.25, bf16[2,1024,2048]{2,1,0:T(8,128)(2,1)} %bitcast.102), kind=kOutput, calls=%fused_computation.1 | convolution fusion | flops 8592031744 | bytes 16777216 | tf_op jit(solution)/shard_map/dot_general | solution.py:555
  425.4 2.5 fusion.6.refs_0_
  427.8 269.2 %shard_map.206 = (bf16[2,2,2,256,2048]{4,3,2,1,0:T(8,128)(2,1)}, bf16[2,1024,512]{2,1,0:T(8,128)(2,1)}, bf16[3,256,2048]{2,1,0:T(8,128)(2,1)}, bf16[2,256,2048]{...) custom-call(bf16[256,2048]{1,0:T(8,128)(2,1)} %fusion.6.refs_0_, ...), custom_call_target="tpu_custom_call" | custom-call | tf_op jit(solution)/shard_map/pallas_call | solution.py:1169
  697.0 2.5 convert_add_fusion.3
  699.9 1.2 copy-done.23
  701.1 1.6 fusion.26
  702.7 1.7 collective-permute-start.1
  704.5 2.8 shard_map.207
  707.5 7.1 fusion.10
  715.2 1.6 convert_element_type.312
  717.3 0.8 convert_element_type.311
  (98 shorter events, 7.9 us)
Async XLA Ops:
  7.2 8.4 %copy-start = (bf16[64,8192]{1,0:T(8,128)(2,1)S(1)}, bf16[64,8192]{1,0:T(8,128)(2,1)}, u32[]{:S(2)}) copy-start(bf16[64,8192]{1,0:T(8,128)(2,1)} %wg.1) | copy-start | bytes 3145732
  7.2 8.4 %copy-start.1 = (bf16[64,8192]{1,0:T(8,128)(2,1)S(1)}, bf16[64,8192]{1,0:T(8,128)(2,1)}, u32[]{:S(2)}) copy-start(bf16[64,8192]{1,0:T(8,128)(2,1)} %wu.1) | copy-start | bytes 3145732
  7.2 269.3 %all-gather.2.cloned.1.call-start = ((), (), s32[]{:S(2)}) async-start(), calls=%async_computation | async-start | bytes 9437184 | tf_op jit(solution)/shard_map/all_gather | solution.py:1459
  7.9 79.5 %collective-permute-start = (bf16[64,2048]{1,0:T(8,128)(2,1)}, bf16[64,2048]{1,0:T(8,128)(2,1)}, u32[]{:S(2)}, u32[]{:S(2)}) collective-permute-start(bf16[64,2048]{1,0:T(8,128)(2,1)} %param.18), channel_id=1, source_target_pairs={{0,0},{1,16},{2,2},{3,18},{4,1},{5,17},{6,3},{7,19},{8,4},{9,20},{... | collective-permute-start | bytes 786440 | tf_op jit(solution)/shard_map/ppermute | solution.py:1477
  15.5 65.0 %copy-start.12 = (bf16[1,2,128,2048]{3,2,1,0:T(8,128)(2,1)S(1)}, bf16[1,2,128,2048]{3,2,1,0:T(8,128)(2,1)}, u32[]{:S(2)}) copy-start(bf16[1,2,128,2048]{3,2,1,0:T(8,128)(2,1)} %param.12) | copy-start | bytes 3145732
  76.3 1.0 copy-start.3
  77.3 1.0 copy-start.7
  78.3 0.8 copy-start.8
  269.5 3.8 copy-start.13
  272.0 1.3 copy-start.19
  272.0 2.6 copy-start.16
  406.2 2.6 copy-start.14
  406.2 2.9 copy-start.20
  409.0 3.1 copy-start.25
  412.1 13.2 %copy-start.17 = (bf16[3,256,2048]{2,1,0:T(8,128)(2,1)S(1)}, bf16[3,256,2048]{2,1,0:T(8,128)(2,1)}, u32[]{:S(2)}) copy-start(bf16[3,256,2048]{2,1,0:T(8,128)(2,1)} %get-tuple-element.48) | copy-start | bytes 9437188
  412.1 13.2 %copy-start.18 = (bf16[3,256,2048]{2,1,0:T(8,128)(2,1)S(1)}, bf16[3,256,2048]{2,1,0:T(8,128)(2,1)}, u32[]{:S(2)}) copy-start(bf16[3,256,2048]{2,1,0:T(8,128)(2,1)} %get-tuple-element.53) | copy-start | bytes 9437188
  412.1 13.2 %copy-start.21 = (bf16[1,2,128,2048]{3,2,1,0:T(8,128)(2,1)S(1)}, bf16[1,2,128,2048]{3,2,1,0:T(8,128)(2,1)}, u32[]{:S(2)}) copy-start(bf16[1,2,128,2048]{3,2,1,0:T(8,128)(2,1)} %param.23) | copy-start | bytes 3145732
  697.0 2.5 copy-start.15
  699.5 1.6 copy-start.23
  701.1 3.3 copy-start.2
  701.1 3.3 copy-start.4
  701.1 3.3 copy-start.5
  701.1 3.3 copy-start.6
  701.1 3.3 copy-start.9
  701.1 3.3 copy-start.10
  701.1 3.3 copy-start.11
  702.7 14.6 %collective-permute-start.1 = (bf16[64,2048]{1,0:T(8,128)(2,1)}, bf16[64,2048]{1,0:T(8,128)(2,1)S(1)}, u32[]{:S(2)}, u32[]{:S(2)}) collective-permute-start(bf16[64,2048]{1,0:T(8,128)(2,1)} %get-tuple-element.74), channel_id=1, source_target_pairs={{0,0},{16,1},{2,2},{18,3},{1,4},{17,5},{3,6},{19,7},{4,8},{20,9},{... | collective-permute-start | bytes 786440 | tf_op jit(solution)/shard_map/ppermute | solution.py:1543
  704.5 3.0 copy-start.22
  707.4 7.1 copy-start.26
  707.5 7.7 %copy-start.24 = (bf16[256,2048]{1,0:T(8,128)(2,1)S(1)}, bf16[256,2048]{1,0:T(8,128)(2,1)}, u32[]{:S(2)}) copy-start(bf16[256,2048]{1,0:T(8,128)(2,1)} %get-tuple-element.78) | copy-start | bytes 3145732
  714.5 2.2 copy-start.27
Sparse Core Ops, SparseCore 0:
  9.9 108.5 all-gather.1

commit v6 on v5

--- a/solution.py
+++ b/solution.py
@@ -77,6 +77,12 @@
         return out.at[pl.ds(start, rows)]
 
 
+class RowGatherOf(RowGather):
+    def __init__(self, source, x, orders):
+        super().__init__(jax.ShapeDtypeStruct(x.shape, x.dtype), None, orders)
+        self.source = source
+
+
 class Swap:
     def __init__(self, x, layout):
         self.x, self.layout = x, layout
@@ -148,7 +154,7 @@
 
 CHUNKS = 4
 AHEAD = 10
-EARLY = 0
+ROOM = 5
 FLOW = (2, 8, 6, 6)
 
 
@@ -423,11 +429,13 @@
     net = Net({a: lax.axis_size(a) for a in AXES})
     sizes = net.sizes
     count = len(jobs)
+    n_in = sum(not isinstance(job, RowGatherOf) for job in jobs)
     steps, swaps, runners, scratch = [], [], [], []
     for number, job in enumerate(jobs):
         if isinstance(job, Gather):
             runner = Relay(job, number, net)
-            steps += runner.steps
+            if not isinstance(job, RowGatherOf):
+                steps += runner.steps
             stage = [pltpu.VMEM(job.x.shape, job.x.dtype)]
         elif isinstance(job, TeamSum):
             runner = Adder(job, number, net)
@@ -445,7 +453,7 @@
     steps.sort(key=lambda s: s[0])
 
     def kernel(*refs):
-        ins, outs, rest = refs[:count], refs[count : 2 * count], refs[2 * count :]
+        ins, outs, rest = refs[:n_in], refs[n_in : n_in + count], refs[n_in + count :]
         send_sem, recv_sem, local_sem, piece_sem = rest[-4:]
         net.open(send_sem, recv_sem)
         loads, stores = [], []
@@ -453,6 +461,8 @@
             runner, lo, hi = runners[number]
             if isinstance(job, TeamSum):
                 runner.open(ins[number], outs[number], *rest[lo:hi])
+                continue
+            if isinstance(job, RowGatherOf):
                 continue
             (stage,) = rest[lo:hi]
             if runner:
@@ -489,29 +499,57 @@
             else:
                 pairs = [job.pair(ins[number], outs[number], net.here, to, off, sizes)]
             for (src, dst), wire in zip(pairs, wires, strict=True):
-                received.append(net.send(src, dst, wire))
+                received.append((number, net.send(src, dst, wire)))
         for load, number, puts in loads:
             load.wait()
             for i, (src, dst) in enumerate(puts):
                 store = pltpu.make_async_copy(src, dst, local_sem.at[number, 1 + i])
                 store.start()
-                stores.append(store)
+                stores.append((number, store))
         for _, runner, hops, *what in steps:
             if hops:
                 runner.run(hops, *what)
-        for cp in received:
+        for number, job in enumerate(jobs):
+            if not isinstance(job, RowGatherOf):
+                continue
+            for cps in (received, stores):
+                for other, cp in [one for one in cps if one[0] == job.source]:
+                    cp.wait_recv() if cps is received else cp.wait()
+            received = [one for one in received if one[0] != job.source]
+            stores = [one for one in stores if one[0] != job.source]
+            runner, lo, hi = runners[number]
+            (stage,) = rest[lo:hi]
+            source = outs[job.source]
+            runner.open(source, outs[number])
+            load = pltpu.make_async_copy(source, stage, local_sem.at[number, 0])
+            load.start()
+            waiting = sorted(runner.steps, key=lambda step: step[0])
+            for _, _, hops, *what in waiting:
+                if not hops:
+                    runner.run(hops, *what)
+            load.wait()
+            for part in range(len(job.orders)):
+                store = pltpu.make_async_copy(
+                    job.cut(stage, part), runner.own(part), local_sem.at[number, 1 + part]
+                )
+                store.start()
+                stores.append((number, store))
+            for _, _, hops, *what in waiting:
+                if hops:
+                    runner.run(hops, *what)
+        for _, cp in received:
             cp.wait_recv()
         for runner, _, _ in runners:
             if isinstance(runner, Adder):
                 runner.finish()
         net.close()
-        for store in stores:
+        for _, store in stores:
             store.wait()
 
     return pl.pallas_call(
         kernel,
         out_shape=[jax.ShapeDtypeStruct(job.shape(sizes), job.x.dtype) for job in jobs],
-        in_specs=[pl.BlockSpec(memory_space=pl.ANY)] * count,
+        in_specs=[pl.BlockSpec(memory_space=pl.ANY)] * n_in,
         out_specs=[pl.BlockSpec(memory_space=pl.ANY)] * count,
         scratch_shapes=scratch
         + [
@@ -526,7 +564,7 @@
         compiler_params=pltpu.CompilerParams(
             collective_id=collective_id, has_side_effects=True, vmem_limit_bytes=VMEM_LIMIT
         ),
-    )(*[job.x for job in jobs])
+    )(*[job.x for job in jobs[:n_in]])
 
 
 def sum_over(term, axis, outer=1):
@@ -566,45 +604,47 @@
 
 
 def attention_front(
-    norm, attn_part, out_part, gate_part, gd, q_pos, k_pos, cos, sin, scaling, collective_id
+    norm, w_attn, out_part, gate_part, down_part, gd, q_pos, k_pos, cos, sin, scaling, collective_id
 ):
     net = Net({a: lax.axis_size(a) for a in AXES})
     sizes = net.sizes
     own, width = norm.shape
     n_slot, n_zh, _, n = k_pos.shape
     n_tok = n_slot * n
-    columns = attn_part.shape[2]
+    columns = w_attn.shape[1]
     q_cols = columns - 2 * HEAD
     heads = q_cols // HEAD
     half = q_cols // 2
-    team = attn_part.shape[0]
+    team = gate_part.shape[0]
     norm_job = NearGather(norm, PAIRED_SLOTS, TO_TEAM)
-    attn_job = RowGather(attn_part, None, [OUTWARD] * team)
+    down_job = Gather(down_part, SHARES, [OUTWARD] * CHUNKS)
     out_job = Gather(out_part, SHARES, [OUTWARD] * (out_part.shape[0] // 16), rank=2)
     gd_job = NearGather(gd, PAIRED_SLOTS, TO_TEAM)
     gate_job = RowGather(gate_part, None, [OUTWARD] * team)
-    norms, attns, outs = (Relay(job, i, net) for i, job in enumerate((norm_job, attn_job, out_job)))
+    norms, downs, outs = (Relay(job, i, net) for i, job in enumerate((norm_job, down_job, out_job)))
     gds, gates = (Relay(job, i, net) for i, job in enumerate((gd_job, gate_job)))
-    first = sorted(norms.steps + attns.steps + outs.steps, key=lambda step: step[0])
+    first = sorted(norms.steps + downs.steps, key=lambda step: step[0])
+    out_steps = sorted(outs.steps, key=lambda step: step[0])
     gd_steps = sorted(gds.steps, key=lambda step: step[0])
     gate_steps = sorted(gates.steps, key=lambda step: step[0])
     kv_wires = [[net.wire({"zh": z}) for z in range(1, n_zh)] for _ in range(n_slot)]
     half_wires = [net.wire({"c": 1}) for _ in range(n_slot)]
-    y_rows, zl_rows = pl.ds(0, own // 2), pl.ds(own // 2, own // 2)
+    y_rows, zl_rows = pl.ds(0, own * 6 // 8), pl.ds(own * 6 // 8, own - own * 6 // 8)
     far_wires = net.wire({"y": 1}), net.wire({"zl": 1})
     near_wires = net.wire({"y": 1}), net.wire({"zl": 1})
     n_local = 64
-    out_shapes = [job.shape(sizes) for job in (norm_job, gd_job, attn_job, out_job, gate_job)]
+    out_shapes = [job.shape(sizes) for job in (norm_job, gd_job, out_job, gate_job, down_job)]
 
     def kernel(
-        norm_ref, attn_ref, outp_ref, gate_ref, gd_ref, q_pos_ref, k_pos_ref, cos_ref, sin_ref,
-        norms_ref, gds_ref, w_attn_ref, w_out_ref, w_gate_ref, q_ref, kv_ref, lse_ref, half_ref,
-        terms_ref,
-        nv, wa, wo, q, kv, o, terms, far, gd_stage, gate_stage, send_sem, recv_sem, local_sem,
+        norm_ref, w_attn_ref, outp_ref, gate_ref, down_ref, gd_ref, q_pos_ref, k_pos_ref, cos_ref,
+        sin_ref, norms_ref, gds_ref, w_out_ref, w_gate_ref, w_down_ref, q_ref, kv_ref, lse_ref,
+        half_ref, terms_ref,
+        nv, wa, wo, q, kv, o, terms, far, gd_stage, gate_stage, down_stage,
+        send_sem, recv_sem, local_sem,
     ):
         net.open(send_sem, recv_sem)
         norms.open(norm_ref, norms_ref)
-        attns.open(attn_ref, wa)
+        downs.open(down_ref, w_down_ref)
         outs.open(outp_ref, wo)
         gds.open(gd_ref, gds_ref)
         gates.open(gate_ref, w_gate_ref)
@@ -620,21 +660,23 @@
                 if not hops:
                     runner.run(hops, *what)
 
-        gate_first = [step for step in gate_steps if not step[2] and step[3] < EARLY]
-        gate_rest = [step for step in gate_steps if not step[2] and step[3] >= EARLY]
         start(first)
         got_norm = local(norm_ref, nv.at[0, 0])
-        got_attn = [local(attn_job.cut(attn_ref, p), attns.own(p)) for p in range(team)]
+        start(out_steps)
+        got_attn = [local(w_attn_ref, wa)]
         got_attn += [
             local(out_job.cut(outp_ref, p), outs.own(p)) for p in range(len(out_job.orders))
         ]
         got_gd, got_gate = local(gd_ref, gd_stage), local(gate_ref, gate_stage)
+        got_down = local(down_ref, down_stage)
         got_norm.wait()
         kept = [local(norm_job.cut(nv.at[0, 0], p), norms.own(p)) for p in range(CHUNKS)]
         got_gd.wait()
         kept += [local(gd_job.cut(gd_stage, p), gds.own(p)) for p in range(CHUNKS)]
         got_gate.wait()
         kept += [local(gate_job.cut(gate_stage, p), gates.own(p)) for p in range(team)]
+        got_down.wait()
+        kept += [local(down_job.cut(down_stage, p), downs.own(p)) for p in range(CHUNKS)]
 
         def turn(t, rows):
             h = HEAD // 2
@@ -686,8 +728,6 @@
             kept.append(local(o.at[window, here], half_ref.at[0, window]))
 
         def term(r):
-            n_part = out_part.shape[0]
-
             def tile(t, _):
                 at = pl.ds(pl.multiple_of(t * TILE, TILE), TILE)
                 weight = wo[:, :, at].reshape(q_cols, TILE)
@@ -701,7 +741,7 @@
 
         halves, late = [], []
 
-        def relay(steps, most=9):
+        def relay(steps):
             for _, runner, hops, part, off, sends in steps:
                 if not hops:
                     continue
@@ -709,28 +749,26 @@
                     late.append((runner, hops, part, off, sends))
                     continue
                 runner.run(hops, part, off, sends)
-                if runner is attns and hops == 1 and off["zh"] and part == team - 1:
-                    start(gate_first)
-                    gate_first.clear()
                 if runner is norms and part == CHUNKS - 1:
                     i, j = off["y"], off["zl"]
                     got[i, j] = local(norms_ref.at[0, i, j], nv.at[i, j])
 
         got = {}
-        relay(first)
+        relay([step for step in first if step[1] is norms or step[0][1] <= ROOM])
         for cp in got_attn:
             cp.wait()
-        kept.append(local(wa, w_attn_ref))
-        kept.append(local(wo, w_out_ref))
         start(gd_steps)
         got[0, 1].wait()
         sent = [project(0)]
         got[1, 0].wait()
         got[1, 1].wait()
         sent.append(project(1))
-        start(gate_rest)
+        relay([step for step in first if not (step[1] is norms or step[0][1] <= ROOM)])
+        relay(out_steps)
+        kept.append(local(wo, w_out_ref))
         relay([step for step in gd_steps if step[2] == 1])
         attend(0, sent[0])
+        start(gate_steps)
         term(1)
         term(0)
         relay([step for step in gd_steps if step[2] > 1])
@@ -773,12 +811,12 @@
             shape((2, n_tok, half), BF16),
             shape((3, own, width), BF16),
         ],
-        in_specs=[hbm] * 5 + [vmem] * 4,
+        in_specs=[hbm] * 6 + [vmem] * 4,
         out_specs=[hbm] * 7 + [vmem] + [hbm] * 2,
         scratch_shapes=[
             pltpu.VMEM((2, 2, own, width), BF16),
+            pltpu.VMEM(w_attn.shape, BF16),
             pltpu.VMEM(out_shapes[2], BF16),
-            pltpu.VMEM(out_shapes[3], BF16),
             pltpu.VMEM(q_shape, BF16),
             pltpu.VMEM(kv_shape, BF16),
             pltpu.VMEM(q_shape, BF16),
@@ -786,6 +824,7 @@
             pltpu.VMEM((own, width), BF16),
             pltpu.VMEM(gd.shape, BF16),
             pltpu.VMEM(gate_part.shape, BF16),
+            pltpu.VMEM(down_part.shape, BF16),
             pltpu.SemaphoreType.DMA((net.count,)),
             pltpu.SemaphoreType.DMA((net.count,)),
             pltpu.SemaphoreType.DMA((n_local,)),
@@ -796,7 +835,7 @@
         compiler_params=pltpu.CompilerParams(
             collective_id=collective_id, has_side_effects=True, vmem_limit_bytes=FFN_VMEM_LIMIT
         ),
-    )(norm, attn_part, out_part, gate_part, gd, q_pos, k_pos, cos, sin)
+    )(norm, w_attn, out_part, gate_part, down_part, gd, q_pos, k_pos, cos, sin)
 
 
 def attention_back(
@@ -812,7 +851,7 @@
     ga_job = NearGather(ga, PAIRED_SLOTS, TO_TEAM_EVEN)
     gas = Relay(ga_job, 0, net)
     ga_steps = sorted(gas.steps, key=lambda step: step[0])
-    adder = Adder(TeamSum(out_parts, CHUNKS), 1, net)
+    adder = Adder(TeamSum(out_parts, CHUNKS // 2), 1, net)
     streams, made = [], []
     if sums:
         down, _, gate_half, _, o_half, _ = sums
@@ -1447,16 +1486,16 @@
     tile = jnp.concatenate(
         [jnp.concatenate(row)[None], jnp.full((7, 128), lengths[0].astype(F32))]
     )
-    tiles, attn_part, gate_part, up_part = exchange(
+    tiles, _, gate_part, up_part, w_attn = exchange(
         [
             Gather(tile, AXES, [(("c", "x", "y"), ("zl", "zh"))], rank=0),
             Swap(attn_cut, TEAM),
             ff_cut(gate_weight),
             ff_cut(up_weight),
+            RowGatherOf(1, attn_cut, [OUTWARD] * team),
         ],
         1,
     )
-    w_down = lax.all_gather(down_weight, SHARES, axis=0, tiled=True)
     gain_one = tiles[:, 0, :rows].reshape(1, width)
     gain_two = tiles[:, 0, 64 : 64 + rows].reshape(1, width)
     slots = tiles[: n_dev // (size["zh"] * size["zl"]), 1, 0].reshape(
@@ -1501,11 +1540,12 @@
     norm_one = (tokens * scale_one * gain_one).astype(BF16)
     gy = valid * cotangent.reshape(own, width).astype(F32)
     (
-        norm_one_pair, gd_pair, w_attn, w_out, w_gate, q, kv_all, lse, o_half, o_terms
+        norm_one_pair, gd_pair, w_out, w_gate, w_down, q, kv_all, lse, o_half, o_terms
     ) = attention_front(
-        norm_one, attn_part, out_part, gate_part, gy.astype(BF16), q_pos, k_pos, cos, sin,
-        scaling, 2,
+        norm_one, w_attn, out_part, gate_part, down_weight, gy.astype(BF16), q_pos, k_pos, cos,
+        sin, scaling, 2,
     )
+    w_down = w_down.reshape(ff, width)
     norm_one_pair = norm_one_pair.reshape(2, n_tok, width)
     w_out = w_out.reshape(q_cols, width)
 

time: 735 us -> 725 us (0.986)
  between operations: 15.3 us -> 1.88 us
    pallas_call x1, Pallas kernels: 60.7 us -> 73.7 us  [exchange(): pl.pallas_call(kernel, out_shape=[jax.ShapeDtypeStruct(job.shape(sizes),...]
  transfers between devices with their start and end apart: 3 -> 2, of which waited for: 0 -> 0; matrix products, arithmetic and copies ran while one was open for 4% -> 3% of each run, Pallas kernels for 34% -> 11%
where the time goes in v6:
time: 725 us; the launch traced here: 714 us
  Pallas kernels  647 us (89%)
  other arithmetic  33.3 us (5%)
  local copies, waits for them, and re-layouts  16.1 us (2%)
  matrix products  13.3 us (2%)
    pallas_call x1, Pallas kernels, attention_back(): pl.pallas_call(kernel, out_shape=[shape((2, 2, 2, own, width), BF16), sha...  264 us
    pallas_call x1, Pallas kernels, attention_front(): pl.pallas_call(kernel, out_shape=[*[shape(dims, BF16) for dims in out_sha...  179 us
    pallas_call x1, Pallas kernels, feed_forward(): pl.pallas_call(kernel, out_shape=[shape((2, 2, 2, own, width), BF16), *[s...  128 us
    pallas_call x1, Pallas kernels, exchange(): pl.pallas_call(kernel, out_shape=[jax.ShapeDtypeStruct(job.shape(sizes),...  73.7 us
  transfers between devices with their start and end apart: 2, of which 0 were waited for; matrix products, arithmetic and copies ran while one was open for 3% of the time, Pallas kernels for 11%

profile of v6, /device:TPU:0, one launch (start us, length us, event | category | flops | bytes accessed | tf_op | source)
XLA Modules:
  0.0 714.2 jit_solution(13064261324922338693)
XLA Ops:
  0.7 1.7 collective-permute-start
  2.4 1.0 copy.37
  5.4 1.0 bitcast_bitcast_fusion.1
  6.5 73.7 %shard_map.203 = (f32[32,8,128]{2,1,0:T(8,128)S(1)}, bf16[4,64,1024]{2,1,0:T(8,128)(2,1)}, bf16[4,64,2048]{2,1,0:T(8,128)(2,1)S(1)}, bf16[4,64,2048]{2,1,0:T(8,128)(2,1)S(1)}, bf16[2048,1024]{1,0:T(8,128)(2,1)}) custom-call(f32[8,128]{1,0:T(8,128)S(1)} %concatenate.13.refs_0_, bf16[4,64,1024]{2,1,0:T(8,128)(2,1)S(1)} %pad_maximum_fusion.refs_1_, ...), custom_call_target="tpu_custom_call" | custom-call | bytes 150000000 | tf_op jit(solution)/shard_map/pallas_call | solution.py:549
  80.2 1.0 copy-done.6
  81.2 1.0 copy-done.7
  83.8 1.5 fusion.7
  86.1 2.4 fusion.14.gd_ref
  88.5 1.3 fusion.13.norm_ref
  89.8 0.9 copy.27.q_pos_ref.refs_4_
  90.8 1.0 multiply_sine_fusion
  91.8 0.9 tile.8
  92.6 0.8 tile.20
  93.5 178.9 %shard_map.204 = (bf16[2,2,2,256,2048]{4,3,2,1,0:T(8,128)(2,1)}, bf16[2,2,2,256,2048]{4,3,2,1,0:T(8,128)(2,1)}, bf16[8,64,2048]{2,1,0:T(8,128)(2,1)}, bf16[2048,...) custom-call(bf16[256,2048]{1,0:T(8,128)(2,1)} %fusion.13.norm_ref, ...), custom_call_target="tpu_custom_call" | custom-call | bytes 480000000 | tf_op jit(solution)/shard_map/pallas_call | solution.py:804
  272.4 2.5 convert_add_fusion.5
  274.9 1.3 copy-done.18
  276.7 0.9 copy-done.15
  277.6 1.8 multiply_convert_fusion.norm_ref
  279.4 128.1 %shard_map.205 = (bf16[2,2,2,256,2048]{4,3,2,1,0:T(8,128)(2,1)}, bf16[2,1024,1024]{2,1,0:T(8,128)(2,1)}, bf16[2,1024,1024]{2,1,0:T(8,128)(2,1)}, bf16[2,1024,102...) custom-call(bf16[256,2048]{1,0:T(8,128)(2,1)} %multiply_convert_fusion.norm_ref, ...), custom_call_target="tpu_custom_call" | custom-call | bytes 390000000 | tf_op jit(solution)/shard_map/pallas_call | solution.py:1409
  407.6 2.6 convert_add_fusion.4
  410.9 2.6 slice.60
  413.5 13.3 %bitcast_convert_fusion.refs_11_ = bf16[1024,2048]{1,0:T(8,128)(2,1)} fusion(bf16[2,1024,1024]{2,1,0:T(8,128)(2,1)S(1)} %copy-done.24, bf16[2,1024,2048]{2,1,0:T(8,128)(2,1)} %bitcast.103), kind=kOutput, calls=%fused_computation.1 | convolution fusion | flops 8592031744 | bytes 16777216 | tf_op jit(solution)/shard_map/dot_general | solution.py:593
  426.8 2.5 fusion.6.refs_0_
  429.2 263.6 %shard_map.206 = (bf16[2,2,2,256,2048]{4,3,2,1,0:T(8,128)(2,1)}, bf16[2,1024,512]{2,1,0:T(8,128)(2,1)}, bf16[3,256,2048]{2,1,0:T(8,128)(2,1)}, bf16[2,256,2048]{...) custom-call(bf16[256,2048]{1,0:T(8,128)(2,1)} %fusion.6.refs_0_, ...), custom_call_target="tpu_custom_call" | custom-call | tf_op jit(solution)/shard_map/pallas_call | solution.py:1208
  692.8 2.5 convert_add_fusion.3
  695.7 1.2 copy-done.21
  696.9 1.6 fusion.26
  698.5 0.8 collective-permute-start.1
  699.8 2.8 shard_map.207
  702.7 7.7 %fusion.10 = (bf16[1,2,128,2048]{3,2,1,0:T(8,128)(2,1)}, bf16[1,2,128,2048]{3,2,1,0:T(8,128)(2,1)}) fusion(bf16[1,2,128,2048]{3,2,1,0:T(8,128)(2,1)} %param.12, bf16[1,2,128,2048]{3,2,1,0:T(8,128)(2,1)} %param.23, f32[2,128]{1,0:T(2,128)S(1)} %broadcast_multiply_fusion, f32[2,128]{1,0:T(2,128)S(1)} %get-tuple-element.96, f32[2048]{0:T(1024)S(1)} %mul.253, ...), kind=kLoop, calls=%fused_computation.22 | loop fusion | flops 20971520 | bytes 16800768 | tf_op jit(solution)/shard_map/convert_element_type | solution.py:1606
  711.1 1.6 convert_element_type.312
  713.2 0.8 convert_element_type.311
  (95 shorter events, 7.3 us)
Async XLA Ops:
  0.6 5.9 copy-start
  0.7 5.9 copy-start.1
  0.7 91.1 %collective-permute-start = (bf16[64,2048]{1,0:T(8,128)(2,1)}, bf16[64,2048]{1,0:T(8,128)(2,1)S(1)}, u32[]{:S(2)}, u32[]{:S(2)}) collective-permute-start(bf16[64,2048]{1,0:T(8,128)(2,1)} %param.18), channel_id=1, source_target_pairs={{0,0},{1,16},{2,2},{3,18},{4,1},{5,17},{6,3},{7,19},{8,4},{9,20},{... | collective-permute-start | bytes 786440 | tf_op jit(solution)/shard_map/ppermute | solution.py:1516
  80.2 1.0 copy-start.6
  81.2 1.0 copy-start.7
  82.2 6.4 copy-start.11
  91.8 1.7 copy-start.23
  272.4 3.8 copy-start.12
  274.9 1.3 copy-start.18
  274.9 2.6 copy-start.15
  407.6 2.6 copy-start.13
  407.6 2.9 copy-start.19
  410.4 3.1 copy-start.24
  413.5 13.3 %copy-start.16 = (bf16[3,256,2048]{2,1,0:T(8,128)(2,1)S(1)}, bf16[3,256,2048]{2,1,0:T(8,128)(2,1)}, u32[]{:S(2)}) copy-start(bf16[3,256,2048]{2,1,0:T(8,128)(2,1)} %get-tuple-element.48) | copy-start | bytes 9437188
  413.5 13.3 %copy-start.17 = (bf16[3,256,2048]{2,1,0:T(8,128)(2,1)S(1)}, bf16[3,256,2048]{2,1,0:T(8,128)(2,1)}, u32[]{:S(2)}) copy-start(bf16[3,256,2048]{2,1,0:T(8,128)(2,1)} %get-tuple-element.54) | copy-start | bytes 9437188
  413.5 13.3 %copy-start.20 = (bf16[1,2,128,2048]{3,2,1,0:T(8,128)(2,1)S(1)}, bf16[1,2,128,2048]{3,2,1,0:T(8,128)(2,1)}, u32[]{:S(2)}) copy-start(bf16[1,2,128,2048]{3,2,1,0:T(8,128)(2,1)} %param.23) | copy-start | bytes 3145732
  692.8 2.5 copy-start.14
  695.3 1.6 copy-start.21
  695.3 3.2 copy-start.25
  696.9 2.4 copy-start.2
  696.9 2.4 copy-start.3
  696.9 2.6 copy-start.4
  696.9 2.6 copy-start.5
  696.9 2.8 copy-start.8
  696.9 2.8 copy-start.9
  696.9 2.8 copy-start.10
  698.5 14.7 %collective-permute-start.1 = (bf16[64,2048]{1,0:T(8,128)(2,1)S(1)}, bf16[64,2048]{1,0:T(8,128)(2,1)S(1)}, u32[]{:S(2)}, u32[]{:S(2)}) collective-permute-start(bf16[64,2048]{1,0:T(8,128)(2,1)S(1)} %copy-done.25), channel_id=1, source_target_pairs={{0,0},{16,1},{2,2},{18,3},{1,4},{17,5},{3,6},{19,7},{4,8},{20,9},{... | collective-permute-start | bytes 786440 | tf_op jit(solution)/shard_map/ppermute | solution.py:1583
  702.7 7.7 %copy-start.26 = (bf16[64]{0:T(256)(128)(2,1)S(1)}, bf16[64]{0:T(256)(128)(2,1)}, u32[]{:S(2)}) copy-start(bf16[64]{0:T(256)(128)(2,1)} %param.19) | copy-start | bytes 388
  702.7 8.3 %copy-start.22 = (bf16[256,2048]{1,0:T(8,128)(2,1)S(1)}, bf16[256,2048]{1,0:T(8,128)(2,1)}, u32[]{:S(2)}) copy-start(bf16[256,2048]{1,0:T(8,128)(2,1)} %get-tuple-element.78) | copy-start | bytes 3145732
  710.4 2.2 copy-start.27

commit v7 on v6

--- a/solution.py
+++ b/solution.py
@@ -854,10 +854,11 @@
     adder = Adder(TeamSum(out_parts, CHUNKS // 2), 1, net)
     streams, made = [], []
     if sums:
-        down, _, gate_half, _, o_half, _ = sums
+        mixed_half, _, gate_half, _, o_half, _, gd = sums
         made = [(width, gate_half.shape[2])] * 2 + [(o_half.shape[2], width), (width, half)]
-        streams = [Stream(net, down.shape, False)]
-        streams += [Stream(net, dims, i != 2) for i, dims in enumerate(made)]
+        made.append((mixed_half.shape[2], gd.shape[2]))
+        streams = [Stream(net, made[4], False)]
+        streams += [Stream(net, dims, i != 2) for i, dims in enumerate(made[:4])]
     n_chunks = n_zh * CHUNKS
     kv_wires = [[net.wire({"zh": z}) for z in range(1, n_zh)] for _ in range(n_slot)]
     half_wires = [net.wire({"c": 1}) for _ in range(n_slot)]
@@ -885,7 +886,7 @@
         gas.open(ga_ref, gas_ref)
         adder.open(parts_ref, added_ref, *adder_scratch)
         for i, stream in enumerate(streams):
-            stream.open([*sum_ins[:1], *made_refs][i], sum_outs[i], *take(5))
+            stream.open([*made_refs[4:], *made_refs[:4]][i], sum_outs[i], *take(5))
         used = iter(range(n_local))
 
         def local(src, dst):
@@ -902,7 +903,7 @@
                     plan.append((i - 1, q_chunk, True))
         plan += [(i, q_chunk, True) for i in range(len(streams))[-1:] for q_chunk in range(CHUNKS)]
         issued, merged = [0] * len(streams), [0] * len(streams)
-        ready = [i == 0 for i in range(len(streams))]
+        ready = [False] * len(streams)
 
         def pump():
             for i, stream in enumerate(streams):
@@ -936,7 +937,7 @@
 
         def product(lhs_ref, rhs_ref, term_ref, steps):
             n_cols = wr.shape[2]
-            n_tiles = width // own
+            n_tiles = lhs_ref.shape[2] // own
 
             def lhs(t, slot, c):
                 at = pl.ds(pl.multiple_of(t * own, own), own)
@@ -991,7 +992,6 @@
             if not hops:
                 gas.run(hops, *what)
         if sums:
-            pump()
             got_o = local(sum_ins[4], o_v)
         got_wo, got_wa = local(wo_ref, wo), local(wa_ref, wa)
         got_ga = local(ga_ref, gav.at[0, 0])
@@ -1000,6 +1000,8 @@
         got_wo.wait()
         got_wa.wait()
         if sums:
+            product(sum_ins[0], sum_ins[6], made_refs[4], 0)
+            there(0)
             product(sum_ins[1], sum_ins[2], made_refs[0], 1)
             there(1)
 
@@ -1563,9 +1565,9 @@
     gn2 = added(gn2_terms[0], gn2_terms[1:]) * gain_two
     gh1 = gy + scale_two * gn2 - h1 * scale_two**3 * jnp.mean(h1 * gn2, axis=-1, keepdims=True)
 
-    down_term = dot(mixed_half, gd_pair, PAIR_ROWS_T).astype(BF16)
     pairs = size["x"] == size["zh"] == 2
-    sums = (down_term, norm_two_pair, gate_half, up_half, o_half, norm_one_pair) if pairs else None
+    sums = (mixed_half, norm_two_pair, gate_half, up_half, o_half, norm_one_pair, gd_pair)
+    sums = sums if pairs else None
     ga_pair, g_qkv_half, gn1_terms, out_added, *totals = attention_back(
         gh1.astype(BF16), q, kv_all, lse, q_pos, k_pos, cos, sin, w_out, w_attn, out_parts, sums,
         scaling, 8,
@@ -1591,6 +1593,7 @@
         gate_term = dot(norm_two_pair, gate_half, PAIR_ROWS_T).astype(BF16)
         up_term = dot(norm_two_pair, up_half, PAIR_ROWS_T).astype(BF16)
         out_term = dot(o_half, ga_pair.reshape(2, n_tok, width), PAIR_ROWS_T).astype(BF16)
+        down_term = dot(mixed_half, gd_pair, PAIR_ROWS_T).astype(BF16)
         down_grad = sum_peers(down_term)
         output_grad = lax.ppermute(sum_peers(out_term), AXES, homeward)
         terms = (attn_term, gate_term, up_term)

time: 725 us -> 734 us (1.012)
  Pallas kernels: 647 us -> 670 us
  matrix products: 13.3 us -> 0 us
    pallas_call x1, Pallas kernels: 264 us -> 288 us  [attention_back(): pl.pallas_call(kernel, out_shape=[shape((2, 2, 2, own, width), BF16), sha...]
    dot_general x1 -> x0, matrix products: 13.3 us -> none  [dot(): return lax.dot_general(a, b, dims, preferred_element_type=F32)]
  transfers between devices with their start and end apart: 2 -> 2, of which waited for: 0 -> 0; matrix products, arithmetic and copies ran while one was open for 3% -> 3% of each run, Pallas kernels for 11% -> 10%
where the time goes in v7:
time: 734 us; the launch traced here: 724 us
  Pallas kernels  670 us (91%)
  other arithmetic  30.2 us (4%)
  local copies, waits for them, and re-layouts  16.5 us (2%)
    pallas_call x1, Pallas kernels, attention_back(): pl.pallas_call(kernel, out_shape=[shape((2, 2, 2, own, width), BF16), sha...  288 us
    pallas_call x1, Pallas kernels, attention_front(): pl.pallas_call(kernel, out_shape=[*[shape(dims, BF16) for dims in out_sha...  179 us
    pallas_call x1, Pallas kernels, feed_forward(): pl.pallas_call(kernel, out_shape=[shape((2, 2, 2, own, width), BF16), *[s...  128 us
    pallas_call x1, Pallas kernels, exchange(): pl.pallas_call(kernel, out_shape=[jax.ShapeDtypeStruct(job.shape(sizes),...  71.7 us
  transfers between devices with their start and end apart: 2, of which 0 were waited for; matrix products, arithmetic and copies ran while one was open for 3% of the time, Pallas kernels for 10%

profile of v7, /device:TPU:0, one launch (start us, length us, event | category | flops | bytes accessed | tf_op | source)
XLA Modules:
  0.0 723.9 jit_solution(17852416061404287085)
XLA Ops:
  0.7 3.7 collective-permute-start
  4.4 1.0 copy.34
  6.1 0.7 convert_element_type.275
  7.4 1.0 bitcast_bitcast_fusion.1
  8.5 71.7 %shard_map.203 = (f32[32,8,128]{2,1,0:T(8,128)S(1)}, bf16[4,64,1024]{2,1,0:T(8,128)(2,1)}, bf16[4,64,2048]{2,1,0:T(8,128)(2,1)S(1)}, bf16[4,64,2048]{2,1,0:T(8,128)(2,1)S(1)}, bf16[2048,1024]{1,0:T(8,128)(2,1)}) custom-call(f32[8,128]{1,0:T(8,128)S(1)} %concatenate.13.refs_0_, bf16[4,64,1024]{2,1,0:T(8,128)(2,1)S(1)} %pad_maximum_fusion.refs_1_, ...), custom_call_target="tpu_custom_call" | custom-call | bytes 150000000 | tf_op jit(solution)/shard_map/pallas_call | solution.py:549
  80.2 1.0 copy-done.6
  81.2 1.0 copy-done.7
  84.1 0.7 compare_select_fusion.k_pos_ref.refs_5_
  84.9 1.2 fusion.14.gd_ref
  86.1 1.3 fusion.13.norm_ref
  87.4 0.9 copy.26.q_pos_ref.refs_4_
  88.3 1.0 multiply_sine_fusion
  89.3 0.8 tile.8
  90.2 0.8 tile.20
  91.0 178.9 %shard_map.204 = (bf16[2,2,2,256,2048]{4,3,2,1,0:T(8,128)(2,1)}, bf16[2,2,2,256,2048]{4,3,2,1,0:T(8,128)(2,1)}, bf16[8,64,2048]{2,1,0:T(8,128)(2,1)}, bf16[2048,...) custom-call(bf16[256,2048]{1,0:T(8,128)(2,1)} %fusion.13.norm_ref, ...), custom_call_target="tpu_custom_call" | custom-call | bytes 480000000 | tf_op jit(solution)/shard_map/pallas_call | solution.py:804
  269.9 2.5 convert_add_fusion.5
  272.5 1.3 copy-done.18
  274.2 0.9 copy-done.15
  275.1 1.8 multiply_convert_fusion.norm_ref
  276.9 128.3 %shard_map.205 = (bf16[2,2,2,256,2048]{4,3,2,1,0:T(8,128)(2,1)}, bf16[2,1024,1024]{2,1,0:T(8,128)(2,1)}, bf16[2,1024,1024]{2,1,0:T(8,128)(2,1)}, bf16[2,1024,102...) custom-call(bf16[256,2048]{1,0:T(8,128)(2,1)} %multiply_convert_fusion.norm_ref, ...), custom_call_target="tpu_custom_call" | custom-call | bytes 390000000 | tf_op jit(solution)/shard_map/pallas_call | solution.py:1411
  405.3 2.6 convert_add_fusion.4
  408.6 2.5 slice.60
  412.0 2.4 fusion.6.refs_0_
  414.4 287.9 %shard_map.206 = (bf16[2,2,2,256,2048]{4,3,2,1,0:T(8,128)(2,1)}, bf16[2,1024,512]{2,1,0:T(8,128)(2,1)}, bf16[3,256,2048]{2,1,0:T(8,128)(2,1)}, bf16[2,256,2048]{...) custom-call(bf16[256,2048]{1,0:T(8,128)(2,1)} %fusion.6.refs_0_, ...), custom_call_target="tpu_custom_call" | custom-call | tf_op jit(solution)/shard_map/pallas_call | solution.py:1210
  702.3 2.5 convert_add_fusion.3
  705.2 1.2 copy-done.23
  706.4 1.6 fusion.26
  708.0 1.7 collective-permute-start.1
  709.8 2.8 shard_map.207
  712.8 7.1 fusion.10
  720.5 1.6 convert_element_type.308
  722.6 0.8 convert_element_type.307
  (92 shorter events, 6.7 us)
Async XLA Ops:
  0.6 7.9 %copy-start = (bf16[64,8192]{1,0:T(8,128)(2,1)S(1)}, bf16[64,8192]{1,0:T(8,128)(2,1)}, u32[]{:S(2)}) copy-start(bf16[64,8192]{1,0:T(8,128)(2,1)} %wg.1) | copy-start | bytes 3145732
  0.7 7.9 %copy-start.1 = (bf16[64,8192]{1,0:T(8,128)(2,1)S(1)}, bf16[64,8192]{1,0:T(8,128)(2,1)}, u32[]{:S(2)}) copy-start(bf16[64,8192]{1,0:T(8,128)(2,1)} %wu.1) | copy-start | bytes 3145732
  0.7 88.7 %collective-permute-start = (bf16[64,2048]{1,0:T(8,128)(2,1)}, bf16[64,2048]{1,0:T(8,128)(2,1)}, u32[]{:S(2)}, u32[]{:S(2)}) collective-permute-start(bf16[64,2048]{1,0:T(8,128)(2,1)} %param.18), channel_id=1, source_target_pairs={{0,0},{1,16},{2,2},{3,18},{4,1},{5,17},{6,3},{7,19},{8,4},{9,20},{... | collective-permute-start | bytes 786440 | tf_op jit(solution)/shard_map/ppermute | solution.py:1518
  8.4 75.3 %copy-start.11 = (bf16[1,2,128,2048]{3,2,1,0:T(8,128)(2,1)S(1)}, bf16[1,2,128,2048]{3,2,1,0:T(8,128)(2,1)}, u32[]{:S(2)}) copy-start(bf16[1,2,128,2048]{3,2,1,0:T(8,128)(2,1)} %param.12) | copy-start | bytes 3145732
  80.2 1.0 copy-start.6
  81.2 1.0 copy-start.7
  82.2 2.7 copy-start.20
  269.9 3.8 copy-start.12
  272.4 1.3 copy-start.18
  272.5 2.6 copy-start.15
  405.2 2.6 copy-start.13
  405.3 2.9 copy-start.19
  408.1 3.0 copy-start.16
  408.1 3.5 copy-start.17
  408.6 3.4 copy-start.21
  702.3 2.5 copy-start.14
  704.8 1.6 copy-start.23
  706.4 3.3 copy-start.2
  706.4 3.3 copy-start.3
  706.4 3.3 copy-start.4
  706.4 3.3 copy-start.5
  706.4 3.3 copy-start.8
  706.4 3.3 copy-start.9
  706.4 3.3 copy-start.10
  708.0 14.6 %collective-permute-start.1 = (bf16[64,2048]{1,0:T(8,128)(2,1)}, bf16[64,2048]{1,0:T(8,128)(2,1)S(1)}, u32[]{:S(2)}, u32[]{:S(2)}) collective-permute-start(bf16[64,2048]{1,0:T(8,128)(2,1)} %get-tuple-element.74), channel_id=1, source_target_pairs={{0,0},{16,1},{2,2},{18,3},{1,4},{17,5},{3,6},{19,7},{4,8},{20,9},{... | collective-permute-start | bytes 786440 | tf_op jit(solution)/shard_map/ppermute | solution.py:1585
  709.8 3.0 copy-start.22
  712.7 7.1 copy-start.25
  712.8 7.7 %copy-start.24 = (bf16[256,2048]{1,0:T(8,128)(2,1)S(1)}, bf16[256,2048]{1,0:T(8,128)(2,1)}, u32[]{:S(2)}) copy-start(bf16[256,2048]{1,0:T(8,128)(2,1)} %get-tuple-element.78) | copy-start | bytes 3145732
  719.9 2.2 copy-start.26
